TPU v7x, 512 devices: a whole 4x8x8 slice. The times are simulated.
512 devices in a mesh: side: 2 (over z_hi), seq: 32 (over z_lo, x, core), tp: 8 (over y).
Axes of the slice: x: 4, y: 8, z: 8 (z_hi: 2, z_lo: 4; z = z_hi * 4 + z_lo), core: 2. Of those that a mesh axis runs over, the one named last changes fastest.
Arguments:
- self_query: bfloat16 [2, 32, 1024, 2048], P('side', 'seq', None, 'tp'), may hold values from -64 to 64
- self_key: bfloat16 [2, 32, 1024, 2048], P('side', 'seq', None, 'tp'), may hold values from -64 to 64
- self_value: bfloat16 [2, 32, 1024, 2048], P('side', 'seq', None, 'tp'), may hold values from -6 to 6
- cross_query: bfloat16 [2, 32, 1024, 2048], P('side', 'seq', None, 'tp'), may hold values from -72 to 72
- passages: bfloat16 [2, 32, 16, 128, 1024], P('side', 'seq', None, None, 'tp'), may hold values from -6 to 6
- w_key: bfloat16 [1024, 2048], P(None, 'tp'), may hold values from -0.1875 to 0.1875
- w_value: bfloat16 [1024, 2048], P(None, 'tp'), may hold values from -0.1875 to 0.1875
- block_map: int32 [2, 32, 32], replicated, may hold values from 0 to 31, each once within a row
- passage_ids: int32 [2, 32, 32], replicated, may hold values from 0 to 15
Outputs:
- mixed: bfloat16 [2, 32, 1024, 2048], P('side', 'seq', None, 'tp')
Inputs may be any that keep to these rules, and one draw needn't show every extreme that they name: Each row block_map[h, d, :] names every block 0 to 31 exactly once.
All inputs are finite; a program needn't handle non-finite values.
Results may differ from a plain program's by a relative error of at most 0.0069.
Values may be sent and summed in bfloat16 or wider, within the bound.
No kernel may reach another device: no remote copies, remote signals or barrier semaphores. Data moves between devices by JAX's collectives and lax.ppermute only.
A program may use at most 64 MiB of HBM per device.

v0:
```python
import math

import jax
import jax.numpy as jnp
from jax import lax
from jax.sharding import PartitionSpec as P

HD = 128
GROUP = 64
NEIGH = 2


def from_partner(block, axis, apart):
    count = lax.axis_size(axis)
    route = []
    for low in range(count):
        high = low | 1 << apart
        if high != low and high < count:
            route += [(low, high), (high, low)]
    return lax.ppermute(block, axis, route)


def self_attention(queries, key_rows, value_rows, head_count):
    length = queries.shape[0]
    query_heads = queries.reshape(length, head_count, HD)
    key_heads = key_rows.reshape(length, head_count, HD)
    value_heads = value_rows.reshape(length, head_count, HD)
    scores = jnp.einsum(
        "qhd,khd->hqk", query_heads, key_heads, preferred_element_type=jnp.float32
    ) * (1.0 / math.sqrt(HD))
    row_ids = lax.broadcasted_iota(jnp.int32, (length, length), 0)
    col_ids = lax.broadcasted_iota(jnp.int32, (length, length), 1)
    scores = jnp.where((col_ids <= row_ids)[None], scores, -jnp.inf)
    row_max = jnp.max(scores, axis=-1, keepdims=True)
    raised = jnp.exp(scores - row_max)
    weights = (raised / jnp.sum(raised, axis=-1, keepdims=True)).astype(jnp.bfloat16)
    attended = jnp.einsum("hqk,khd->qhd", weights, value_heads, preferred_element_type=jnp.float32)
    return attended.reshape(length, head_count * HD)


def cross_attention(queries, slot_keys, slot_values, head_count):
    length, feats = queries.shape
    groups = length // GROUP
    lead_rows = GROUP - 1
    shifted = jnp.concatenate(
        [queries[lead_rows:], jnp.zeros((lead_rows, feats), queries.dtype)], 0
    )
    shifted = shifted.reshape(groups, GROUP, head_count, HD)
    group_keys = slot_keys.reshape(groups, NEIGH * slot_keys.shape[1], head_count, HD)
    group_values = slot_values.reshape(groups, NEIGH * slot_values.shape[1], head_count, HD)
    scores = jnp.einsum(
        "cqhd,ckhd->chqk", shifted, group_keys, preferred_element_type=jnp.float32
    ) * (1.0 / math.sqrt(HD))
    row_max = jnp.max(scores, axis=-1, keepdims=True)
    raised = jnp.exp(scores - row_max)
    weights = (raised / jnp.sum(raised, axis=-1, keepdims=True)).astype(jnp.bfloat16)
    attended = jnp.einsum(
        "chqk,ckhd->cqhd", weights, group_values, preferred_element_type=jnp.float32
    )
    attended = attended.reshape(length, feats)
    return jnp.concatenate(
        [jnp.zeros((lead_rows, feats), jnp.float32), attended[: length - lead_rows]], 0
    )


def deliver(outgoing):
    swapped = from_partner(outgoing, "side", 0)
    arrived = lax.all_to_all(swapped, "seq", split_axis=1, concat_axis=1, tiled=True)
    return arrived


def served_rows(block_map, passage_ids, which_side, block_now):
    served_map = lax.dynamic_index_in_dim(block_map, which_side, 0, keepdims=False)
    served_ids = lax.dynamic_index_in_dim(passage_ids, which_side, 0, keepdims=False)
    return jnp.sum(jnp.where(served_map == block_now, served_ids, 0), axis=1)


def on_device(
    self_query, self_key, self_value, cross_query, passages, w_key, w_value, block_map, passage_ids
):
    side_now = lax.axis_index("side")
    block_now = lax.axis_index("seq")
    far_side = 1 - side_now
    own_rows = lax.dynamic_index_in_dim(block_map, side_now, 0, keepdims=False)
    own_map = lax.dynamic_index_in_dim(own_rows, block_now, 0, keepdims=False)
    pool_block = passages[0, 0]
    head_feats = w_key.shape[1]
    wanted = served_rows(block_map, passage_ids, far_side, block_now)
    column_part = lax.all_gather(pool_block, "tp", axis=2, tiled=True)
    key_sum = jnp.einsum("prc,cf->prf", column_part, w_key, preferred_element_type=jnp.float32)
    value_sum = jnp.einsum("prc,cf->prf", column_part, w_value, preferred_element_type=jnp.float32)
    key_sum, value_sum = (key_sum, value_sum)
    panels = jnp.stack([key_sum, value_sum]).astype(jnp.bfloat16)
    outgoing = jnp.take(panels, wanted, axis=1)
    arrived = deliver(outgoing)
    slot_panels = jnp.take(arrived, own_map, axis=1)
    head_count = head_feats // HD
    self_out = self_attention(self_query[0, 0], self_key[0, 0], self_value[0, 0], head_count)
    cross_out = cross_attention(cross_query[0, 0], slot_panels[0], slot_panels[1], head_count)
    return (self_out + cross_out).astype(jnp.bfloat16)[None, None]


def solution(mesh):
    return jax.shard_map(
        on_device,
        mesh=mesh,
        in_specs=(
            P("side", "seq", None, "tp"),
            P("side", "seq", None, "tp"),
            P("side", "seq", None, "tp"),
            P("side", "seq", None, "tp"),
            P("side", "seq", None, None, "tp"),
            P(None, "tp"),
            P(None, "tp"),
            P(),
            P(),
        ),
        out_specs=P("side", "seq", None, "tp"),
        check_vma=False,
    )
```

profile of v0, /device:TPU:1, one launch (start us, length us, event | category | flops | bytes accessed | tf_op | source)
XLA Modules:
  0.0 410.2 jit_solution(1269943070539979746)
XLA Ops:
  6.5 0.7 all-gather.3.cloned.1.call-update
  7.3 0.8 select_reduce_fusion
  8.2 68.3 %all-gather.3.cloned.1.call-done = bf16[1,1,16,128,1024]{4,3,2,1,0:T(8,128)(2,1)} async-done(((bf16[1,1,16,128,128]{4,3,2,1,0:T(8,128)(2,1)}), bf16[1,1,16,128,1024]{4,3,2,1,0:T(8,128)(2,1)}) %all-gather.3.cloned.1.call-update) | async-done | bytes 4194320 | tf_op jit(solution)/shard_map/all_gather | solution.py:89
  76.5 3.6 fusion.22
  80.1 1.3 fusion.25
  81.4 0.2 pad_maximum_fusion
  81.6 2.8 gather_fusion
  84.3 2.6 select_bitcast_fusion.1
  87.0 7.9 %collective-permute-start = (bf16[2,32,128,256]{3,2,0,1:T(8,128)(2,1)S(1)}, bf16[2,32,128,256]{3,2,0,1:T(8,128)(2,1)}, u32[]{:S(2)}, u32[]{:S(2)}) collective-permute-start(bf16[2,32,128,256]{3,2,0,1:T(8,128)(2,1)S(1)} %select_bitcast_fusion.1), channel_id=1, source_target_pairs={{0,256},{256,0},{1,257},{257,1},{2,258},{258,2},{3,259},{259,3},{4... | collective-permute-start | bytes 12582920 | tf_op jit(solution)/shard_map/ppermute | solution.py:20
  95.0 178.2 %collective-permute-done = bf16[2,32,128,256]{3,2,0,1:T(8,128)(2,1)} collective-permute-done((bf16[2,32,128,256]{3,2,0,1:T(8,128)(2,1)S(1)}, bf16[2,32,128,256]{3,2,0,1:T(8,128)(2,1)}, u32[]{:S(2)}, u32[]{:S(2)}) %collective-permute-start) | collective-permute-done | bytes 4194336 | tf_op jit(solution)/shard_map/ppermute | solution.py:20
  273.2 12.0 %all-to-all-start = ((bf16[2,32,128,256]{3,2,0,1:T(8,128)(2,1)}), bf16[2,32,128,256]{3,2,0,1:T(8,128)(2,1)}, u32[]{:S(2)}, u32[]{:S(2)}) async-start(bf16[2,32,128,256]{3,2,0,1:T(8,128)(2,1)} %collective-permute-done), calls=%async_computation | async-start | bytes 8388608 | tf_op jit(solution)/shard_map/all_to_all | solution.py:68
  285.2 0.2 copy.27
  285.5 0.1 reshape_squeeze.16
  285.7 0.3 iota_compare_fusion
  286.0 5.2 %fusion.63 = (f32[2,1024]{1,0:T(2,128)S(1)}, f32[2,1024,1024]{1,2,0:T(8,128)}) fusion(pred[1024,1024]{0,1:T(8,128)(4,1)S(1)} %iota_compare_fusion, bf16[1024,2,128]{2,1,0:T(2,128)(2,1)S(1)} %reshape_squeeze.16, bf16[1024,2,128]{2,1,0:T(2,128)(2,1)S(1)} %reshape_squeeze.15), kind=kOutput, calls=%fused_computation.67 | convolution fusion | flops 545260544 | bytes 10493952 | tf_op jit(solution)/shard_map/sub | solution.py:35
  291.2 4.2 %fusion.10 = f32[2,1024,128]{1,2,0:T(8,128)S(1)} fusion(bf16[1024,2,128]{0,2,1:T(8,128)(2,1)S(1)} %bitcast.68, f32[2,1024,1024]{1,2,0:T(8,128)} %get-tuple-element.8, f32[2,1024]{1,0:T(2,128)S(1)} %get-tuple-element.7), kind=kOutput, calls=%fused_computation.18 | convolution fusion | flops 541065216 | bytes 9969664 | tf_op jit(solution)/shard_map/hqk,khd->qhd/dot_general | solution.py:37
  295.4 1.3 copy.25
  297.0 0.7 fusion.55
  297.7 0.7 compare_and_fusion.1
  298.4 80.2 %all-to-all-done = bf16[2,32,128,256]{3,2,0,1:T(8,128)(2,1)} async-done(((bf16[2,32,128,256]{3,2,0,1:T(8,128)(2,1)}), bf16[2,32,128,256]{3,2,0,1:T(8,128)(2,1)}, u32[]{:S(2)}, u32[]{:S(2)}) %all-to-all-start) | async-done | bytes 4194336 | tf_op jit(solution)/shard_map/all_to_all | solution.py:68
  378.5 4.9 %gather_fusion.1 = bf16[32,2,128,256]{3,2,1,0:T(8,128)(2,1)} fusion(bf16[2,32,128,256]{3,2,0,1:T(8,128)(2,1)} %all-to-all-done, s32[1024]{0:T(1024)S(1)} %pad_clamp_fusion), kind=kCustom, calls=%fused_computation.1 | custom fusion | bytes 8388736 | tf_op jit(solution)/shard_map/jit(_take)/gather | solution.py:96
  383.5 2.6 select_bitcast_fusion
  386.1 1.6 fusion.62
  387.7 2.1 reshape_squeeze.18
  389.8 2.5 reshape_squeeze.19
  392.3 0.8 fusion.13
  393.2 1.3 copy-done.3
  394.5 0.8 fusion.72
  395.3 5.9 %fusion.28 = f32[16,64,2,128]{3,1,2,0:T(8,128)S(1)} fusion(bf16[16,256,2,128]{3,2,1,0:T(2,128)(2,1)} %reshape_squeeze.18, f32[16,2,64]{2,1,0:T(2,128)S(1)} %fusion.72, f32[16,2,64,256]{3,2,1,0:T(8,128)} %copy-done.3), kind=kOutput, calls=%fused_computation.32 | convolution fusion | flops 136317184 | bytes 5251072 | tf_op jit(solution)/shard_map/chqk,ckhd->cqhd/dot_general | solution.py:57
  401.2 0.8 copy.24
  402.2 0.2 copy-done.2
  402.4 0.9 fusion.35
  (29 shorter events, 0.6 us)
Async XLA Ops:
  6.5 69.9 %copy-start = (bf16[1024,256]{1,0:T(8,128)(2,1)S(1)}, bf16[1024,256]{1,0:T(8,128)(2,1)}, u32[]{:S(2)}) copy-start(bf16[1024,256]{1,0:T(8,128)(2,1)} %param.15) | copy-start | bytes 1572868
  6.5 73.5 %copy-start.9 = (bf16[1024,256]{1,0:T(8,128)(2,1)S(1)}, bf16[1024,256]{1,0:T(8,128)(2,1)}, u32[]{:S(2)}) copy-start(bf16[1024,256]{1,0:T(8,128)(2,1)} %param.14) | copy-start | bytes 1572868
  6.5 69.9 %all-gather.3.cloned.1.call-start = ((), (), s32[]{:S(2)}) async-start(), calls=%async_computation.1 | async-start | bytes 4718592 | tf_op jit(solution)/shard_map/all_gather | solution.py:89
  76.5 3.6 copy-start.8
  87.0 198.2 %copy-start.4 = (bf16[1,1,1024,256]{3,2,1,0:T(8,128)(2,1)S(1)}, bf16[1,1,1024,256]{3,2,1,0:T(8,128)(2,1)}, u32[]{:S(2)}) copy-start(bf16[1,1,1024,256]{3,2,1,0:T(8,128)(2,1)} %param.11) | copy-start | bytes 1572868
  87.0 198.5 %copy-start.5 = (bf16[1,1,1024,256]{3,2,1,0:T(8,128)(2,1)S(1)}, bf16[1,1,1024,256]{3,2,1,0:T(8,128)(2,1)}, u32[]{:S(2)}) copy-start(bf16[1,1,1024,256]{3,2,1,0:T(8,128)(2,1)} %param.10) | copy-start | bytes 1572868
  87.0 198.6 %copy-start.6 = (bf16[1,1,1024,256]{3,2,1,0:T(8,128)(2,1)S(1)}, bf16[1,1,1024,256]{3,2,1,0:T(8,128)(2,1)}, u32[]{:S(2)}) copy-start(bf16[1,1,1024,256]{3,2,1,0:T(8,128)(2,1)} %param.9) | copy-start | bytes 1572868
  87.0 186.2 %collective-permute-start = (bf16[2,32,128,256]{3,2,0,1:T(8,128)(2,1)S(1)}, bf16[2,32,128,256]{3,2,0,1:T(8,128)(2,1)}, u32[]{:S(2)}, u32[]{:S(2)}) collective-permute-start(bf16[2,32,128,256]{3,2,0,1:T(8,128)(2,1)S(1)} %select_bitcast_fusion.1), channel_id=1, source_target_pairs={{0,256},{256,0},{1,257},{257,1},{2,258},{258,2},{3,259},{259,3},{4... | collective-permute-start | bytes 12582920 | tf_op jit(solution)/shard_map/ppermute | solution.py:20
  273.2 105.3 %all-to-all-start = ((bf16[2,32,128,256]{3,2,0,1:T(8,128)(2,1)}), bf16[2,32,128,256]{3,2,0,1:T(8,128)(2,1)}, u32[]{:S(2)}, u32[]{:S(2)}) async-start(bf16[2,32,128,256]{3,2,0,1:T(8,128)(2,1)} %collective-permute-done), calls=%async_computation | async-start | bytes 8388608 | tf_op jit(solution)/shard_map/all_to_all | solution.py:68
  291.2 5.5 %copy-start.7 = (bf16[1,1,1024,256]{3,2,1,0:T(8,128)(2,1)S(1)}, bf16[1,1,1024,256]{3,2,1,0:T(8,128)(2,1)}, u32[]{:S(2)}) copy-start(bf16[1,1,1024,256]{3,2,1,0:T(8,128)(2,1)} %param.12) | copy-start | bytes 1572868
  393.2 1.3 copy-start.3
  395.2 8.1 %copy-start.1 = (bf16[1024,256]{1,0:T(8,128)(2,1)S(1)}, bf16[1024,256]{1,0:T(8,128)(2,1)}, u32[]{:S(2)}) copy-start(bf16[1024,256]{1,0:T(8,128)(2,1)} %param.15) | copy-start | bytes 1572868
  401.2 1.2 copy-start.2
Sparse Core Ops, SparseCore 0:
  9.4 67.0 all-gather.2
where the time goes:
time: 411 us; the launch traced here: 410 us
  waiting for transfers between devices  327 us (80%)
  matrix products  21 us (5%)
  starting transfers between devices  19.9 us (5%)
  local copies, waits for them, and re-layouts  18.5 us (5%)
  between operations  13.7 us (3%)
  other arithmetic  9.78 us (2%)
    ppermute x1, waiting for transfers between devices, from_partner(): return lax.ppermute(block, axis, route)  178 us
    all_to_all x1, waiting for transfers between devices, deliver(): lax.all_to_all(swapped, 'seq', split_axis=1, concat_axis=1, tiled=True)  80.2 us
    all_gather x1, waiting for transfers between devices, on_device(): column_part = lax.all_gather(pool_block, 'tp', axis=2, tiled=True)  68.3 us
    all_to_all x1, starting transfers between devices, deliver(): lax.all_to_all(swapped, 'seq', split_axis=1, concat_axis=1, tiled=True)  12 us
  transfers between devices with their start and end apart: 3, of which 3 were waited for; matrix products, arithmetic and copies ran while one was open for 3% of the time, Pallas kernels for 0%

commit v1 on v0

v1 whole, which is shorter than its diff:
```python
import math

import jax
import jax.numpy as jnp
from jax import lax
from jax.experimental import pallas as pl
from jax.experimental.pallas import tpu as pltpu
from jax.sharding import PartitionSpec as P

HD = 128
GROUP = 64
NEIGH = 2
EXTRA = 8
VMEM_BYTES = 40 * 1024 * 1024
EXP2_SCALE = math.log2(math.e) / math.sqrt(HD)

NT = (((1,), (1,)), ((), ()))
TN = (((0,), (0,)), ((), ()))


def params(**kwargs):
    return pltpu.CompilerParams(vmem_limit_bytes=VMEM_BYTES, **kwargs)


def last_row_mask(rows, cols):
    return lax.broadcasted_iota(jnp.int32, (rows, cols), 0) < rows - 1


def pack_kernel(place, block_map, query_ref, out_ref):
    groups, rows, cols = query_ref.shape
    own_side, own_seq = place[0], place[1]
    head = last_row_mask(rows, cols)
    for u in range(groups):
        chunk = jnp.where(head, query_ref[min(u + 1, groups - 1)], query_ref[u])
        for n in range(NEIGH):
            out_ref[block_map[own_side, own_seq, NEIGH * u + n]] = chunk


def pack_queries(place, block_map, queries, blocks):
    groups, rows, cols = queries.shape
    return pl.pallas_call(
        pack_kernel,
        out_shape=jax.ShapeDtypeStruct((blocks, rows, cols), queries.dtype),
        grid_spec=pltpu.PrefetchScalarGridSpec(
            num_scalar_prefetch=2,
            grid=(1,),
            in_specs=[pl.BlockSpec((groups, rows, cols), lambda i, *_: (0, 0, 0))],
            out_specs=pl.BlockSpec((blocks, rows, cols), lambda i, *_: (0, 0, 0)),
        ),
        compiler_params=params(),
        cost_estimate=pl.CostEstimate(
            flops=0, bytes_accessed=2 * (groups + blocks) * rows * cols, transcendentals=0
        ),
        name="pack_queries",
    )(place, block_map, queries)


def self_kernel(query_ref, key_ref, value_ref, out_ref, *, block):
    length, feats = query_ref.shape
    row = lax.broadcasted_iota(jnp.int32, (block, block), 0)
    col = lax.broadcasted_iota(jnp.int32, (block, block), 1)
    for g in range(feats // HD):
        cols = slice(g * HD, (g + 1) * HD)
        for i in range(length // block):
            rows = slice(i * block, (i + 1) * block)
            stop = (i + 1) * block
            query = query_ref[rows, cols]
            scores = lax.dot_general(
                query, key_ref[:stop, cols], NT, preferred_element_type=jnp.float32
            )
            tail = jnp.where(col <= row, scores[:, i * block :], -jnp.inf)
            scores = tail if i == 0 else jnp.concatenate([scores[:, : i * block], tail], 1)
            top = jnp.max(scores, axis=1, keepdims=True)
            raised = jnp.exp2((scores - top) * EXP2_SCALE)
            total = jnp.sum(raised, axis=1, keepdims=True)
            weights = (raised * (1.0 / total)).astype(jnp.bfloat16)
            out_ref[rows, cols] = jnp.dot(
                weights, value_ref[:stop, cols], preferred_element_type=jnp.float32
            )


def self_attention(queries, key_rows, value_rows):
    length, feats = queries.shape
    block = min(256, length)
    return pl.pallas_call(
        lambda *refs: self_kernel(*refs, block=block),
        out_shape=jax.ShapeDtypeStruct((length, feats), jnp.float32),
        in_specs=[pl.BlockSpec(memory_space=pltpu.VMEM)] * 3,
        out_specs=pl.BlockSpec(memory_space=pltpu.VMEM),
        compiler_params=params(),
        cost_estimate=pl.CostEstimate(
            flops=3 * length * length * feats,
            bytes_accessed=10 * length * feats,
            transcendentals=length * length * feats // HD // 2,
        ),
        name="self_attention",
    )(queries, key_rows, value_rows)


def cross_kernel(wanted, passage_ref, wkey_ref, wvalue_ref, query_ref, out_ref, kv_ref, *, project_steps):
    step = pl.program_id(0)
    shards, per_step, rlen, part = passage_ref.shape
    feats = wkey_ref.shape[1]

    @pl.when(step < project_steps)
    def _():
        lhs = jnp.concatenate(
            [passage_ref[t].reshape(per_step * rlen, part) for t in range(shards)], axis=1
        )
        keys = jnp.dot(lhs, wkey_ref[...], preferred_element_type=jnp.float32)
        values = jnp.dot(lhs, wvalue_ref[...], preferred_element_type=jnp.float32)
        where = pl.ds(step * per_step, per_step)
        kv_ref[where, :, :feats] = keys.astype(jnp.bfloat16).reshape(per_step, rlen, feats)
        kv_ref[where, :, feats:] = values.astype(jnp.bfloat16).reshape(per_step, rlen, feats)

    @pl.when(step >= project_steps)
    def _():
        per_chunk, rows, _ = query_ref.shape
        heads = feats // HD
        first = (step - project_steps) * per_chunk
        zeros = jnp.zeros((rows, HD), jnp.bfloat16)
        for i in range(per_chunk):
            passage = wanted[first + i]
            query = query_ref[i]
            spread = jnp.concatenate(
                [
                    jnp.concatenate(
                        [query[:, g * HD : (g + 1) * HD] if g == k else zeros for k in range(heads)], 1
                    )
                    for g in range(heads)
                ],
                0,
            )
            scores = lax.dot_general(
                kv_ref[passage, :, :feats], spread, NT, preferred_element_type=jnp.float32
            )
            top = jnp.max(scores, axis=0, keepdims=True)
            raised = jnp.exp2((scores - top) * EXP2_SCALE)
            total = jnp.sum(raised, axis=0, keepdims=True)
            weights = (raised * (1.0 / total)).astype(jnp.bfloat16)
            attended = lax.dot_general(
                weights, kv_ref[passage, :, feats:], TN, preferred_element_type=jnp.float32
            )
            for g in range(heads):
                out_ref[i, :rows, g * HD : (g + 1) * HD] = attended[
                    g * rows : (g + 1) * rows, g * HD : (g + 1) * HD
                ].astype(jnp.bfloat16)
            level = top * EXP2_SCALE + jnp.log2(total)
            high = level.astype(jnp.bfloat16)
            rest = level - high.astype(jnp.float32)
            middle = rest.astype(jnp.bfloat16)
            low = (rest - middle.astype(jnp.float32)).astype(jnp.bfloat16)
            lead = jnp.concatenate([high, middle], 1).astype(jnp.float32)
            follow = jnp.concatenate([low, low], 1).astype(jnp.float32)
            picked = lax.broadcasted_iota(jnp.int32, (EXTRA, feats), 0) == 0
            out_ref[i, rows:, :] = jnp.where(picked, lead, follow).astype(jnp.bfloat16)


def cross_attention(wanted, gathered, w_key, w_value, queries):
    shards, pool, rlen, part = gathered.shape
    chunks, rows, feats = queries.shape
    project_steps, attend_steps = 4, 2
    per_step, per_chunk = pool // project_steps, chunks // attend_steps
    depth = shards * part
    late = lambda i: jnp.maximum(i - project_steps, 0)
    return pl.pallas_call(
        lambda *refs: cross_kernel(*refs, project_steps=project_steps),
        out_shape=jax.ShapeDtypeStruct((chunks, rows + EXTRA, feats), jnp.bfloat16),
        grid_spec=pltpu.PrefetchScalarGridSpec(
            num_scalar_prefetch=1,
            grid=(project_steps + attend_steps,),
            in_specs=[
                pl.BlockSpec(
                    (shards, per_step, rlen, part),
                    lambda i, *_: (0, jnp.minimum(i, project_steps - 1), 0, 0),
                ),
                pl.BlockSpec((depth, feats), lambda i, *_: (0, 0)),
                pl.BlockSpec((depth, feats), lambda i, *_: (0, 0)),
                pl.BlockSpec((per_chunk, rows, feats), lambda i, *_: (late(i), 0, 0)),
            ],
            out_specs=pl.BlockSpec((per_chunk, rows + EXTRA, feats), lambda i, *_: (late(i), 0, 0)),
            scratch_shapes=[pltpu.VMEM((pool, rlen, 2 * feats), jnp.bfloat16)],
        ),
        compiler_params=params(),
        cost_estimate=pl.CostEstimate(
            flops=4 * pool * rlen * depth * feats + 8 * chunks * rows * rlen * feats,
            bytes_accessed=2 * (pool * rlen * depth + 2 * depth * feats + 2 * chunks * rows * feats),
            transcendentals=chunks * rows * rlen * feats // HD,
        ),
        name="cross_attention",
    )(wanted, gathered, w_key, w_value, queries)


def mix_kernel(place, block_map, arrived_ref, self_ref, out_ref):
    groups, rows, feats = self_ref.shape
    heads = feats // HD
    own_side, own_seq = place[0], place[1]

    def level_of(block):
        packed = arrived_ref[block, rows:, :].astype(jnp.float32)
        half = feats // 2
        return packed[0:1, :half] + packed[0:1, half:] + packed[1:2, :half]

    slots = [
        [block_map[own_side, own_seq, NEIGH * u + n] for n in range(NEIGH)] for u in range(groups)
    ]
    firsts = jnp.concatenate([level_of(pair[0]) for pair in slots], 0)
    seconds = jnp.concatenate([level_of(pair[1]) for pair in slots], 0)
    top = jnp.maximum(firsts, seconds)
    raised = jnp.exp2(firsts - top)
    share = raised / (raised + jnp.exp2(seconds - top))
    columns = share.T
    head = last_row_mask(rows, HD)
    for g in range(heads):
        cols = slice(g * HD, (g + 1) * HD)
        before = jnp.zeros((rows, HD), jnp.float32)
        for u in range(groups):
            one = arrived_ref[slots[u][0], :rows, cols].astype(jnp.float32)
            two = arrived_ref[slots[u][1], :rows, cols].astype(jnp.float32)
            part = columns[g * rows : (g + 1) * rows, u : u + 1]
            now = two + part * (one - two)
            cross = jnp.where(head, before, now)
            out_ref[u, :, cols] = (self_ref[u, :, cols] + cross).astype(jnp.bfloat16)
            before = now


def mix(place, block_map, arrived, self_out):
    groups, rows, feats = self_out.shape
    chunks = arrived.shape[0]
    whole = lambda i, *_: (0, 0, 0)
    return pl.pallas_call(
        mix_kernel,
        out_shape=jax.ShapeDtypeStruct(self_out.shape, jnp.bfloat16),
        grid_spec=pltpu.PrefetchScalarGridSpec(
            num_scalar_prefetch=2,
            grid=(1,),
            in_specs=[
                pl.BlockSpec((chunks, rows + EXTRA, feats), whole),
                pl.BlockSpec((groups, rows, feats), whole),
            ],
            out_specs=pl.BlockSpec((groups, rows, feats), whole),
        ),
        compiler_params=params(),
        cost_estimate=pl.CostEstimate(
            flops=8 * groups * rows * feats,
            bytes_accessed=10 * groups * rows * feats,
            transcendentals=0,
        ),
        name="mix",
    )(place, block_map, arrived, self_out)


def on_device(
    self_query, self_key, self_value, cross_query, passages, w_key, w_value, block_map, passage_ids
):
    side_now = lax.axis_index("side")
    seq_now = lax.axis_index("seq")
    blocks = lax.axis_size("seq")
    place = jnp.stack([side_now, seq_now]).astype(jnp.int32)
    length, feats = cross_query.shape[2:]
    groups = length // GROUP

    near = lax.ppermute(passages[0, 0], "side", [(0, 1), (1, 0)])
    gathered = lax.all_gather(near, "tp")

    served_map = lax.dynamic_index_in_dim(block_map, side_now, 0, keepdims=False)
    served_ids = lax.dynamic_index_in_dim(passage_ids, side_now, 0, keepdims=False)
    wanted = jnp.sum(jnp.where(served_map == seq_now, served_ids, 0), axis=1)

    chunks = pack_queries(place, block_map, cross_query[0, 0].reshape(groups, GROUP, feats), blocks)
    chunks, _ = lax.optimization_barrier((chunks, near[0, 0, 0]))
    asked = lax.all_to_all(chunks, "seq", split_axis=0, concat_axis=0, tiled=True)
    self_out = self_attention(self_query[0, 0], self_key[0, 0], self_value[0, 0])

    answers = cross_attention(wanted, gathered, w_key, w_value, asked)
    arrived = lax.all_to_all(answers, "seq", split_axis=0, concat_axis=0, tiled=True)
    mixed = mix(place, block_map, arrived, self_out.reshape(groups, GROUP, feats))
    return mixed.reshape(1, 1, length, feats)


def solution(mesh):
    return jax.shard_map(
        on_device,
        mesh=mesh,
        in_specs=(
            P("side", "seq", None, "tp"),
            P("side", "seq", None, "tp"),
            P("side", "seq", None, "tp"),
            P("side", "seq", None, "tp"),
            P("side", "seq", None, None, "tp"),
            P(None, "tp"),
            P(None, "tp"),
            P(),
            P(),
        ),
        out_specs=P("side", "seq", None, "tp"),
        check_vma=False,
    )
```

time: 411 us -> 158 us (0.38)
  waiting for transfers between devices: 327 us -> 82.1 us
  matrix products: 21 us -> 0 us
  starting transfers between devices: 19.9 us -> 39.7 us
  Pallas kernels: 0 us -> 15.8 us
  local copies, waits for them, and re-layouts: 18.5 us -> 5.84 us
  other arithmetic: 9.78 us -> 0.19 us
    ppermute x1, waiting for transfers between devices: 178 us -> 11 us  [on_device(): near = lax.ppermute(passages[0, 0], 'side', [(0, 1), (1, 0)])]
    all_gather x1, waiting for transfers between devices: 68.3 us -> 20.8 us  [on_device(): gathered = lax.all_gather(near, 'tp')]
    all_to_all x1 -> x2, waiting for transfers between devices: 80.2 us -> 50.3 us  [the longest x1 26.4 us: on_device(): lax.all_to_all(chunks, 'seq', split_axis=0, concat_axis=0, tiled=True)]
    all_to_all x1 -> x2, starting transfers between devices: 12 us -> 28.2 us  [the longest x1 19.8 us: on_device(): lax.all_to_all(chunks, 'seq', split_axis=0, concat_axis=0, tiled=True)]
    dot_general x5 -> x0, matrix products: 15.8 us -> none  [the longest x1 5.94 us: cross_attention(): jnp.einsum('chqk,ckhd->cqhd', weights, group_values, preferred_element_ty...]
    pallas_call x0 -> x4, Pallas kernels: none -> 15.8 us  [the longest x1 7.07 us: cross_attention(): pl.pallas_call(lambda *refs: cross_kernel(*refs, project_steps=project_st...]
    gather x2 -> x0, local copies, waits for them, and re-layouts: 7.69 us -> none  [the longest x1 4.94 us: on_device(): slot_panels = jnp.take(arrived, own_map, axis=1)]
    select_n x4 -> x0, other arithmetic: 6.01 us -> none  [the longest x2 3.35 us: on_device(): slot_panels = jnp.take(arrived, own_map, axis=1)]
  transfers between devices with their start and end apart: 3 -> 4, of which waited for: 3 -> 4; matrix products, arithmetic and copies ran while one was open for 3% -> 0% of each run, Pallas kernels for 0% -> 4%
where the time goes in v1:
time: 158 us; the launch traced here: 157 us
  waiting for transfers between devices  82.1 us (52%)
  starting transfers between devices  39.7 us (25%)
  Pallas kernels  15.8 us (10%)
  between operations  13.5 us (9%)
  local copies, waits for them, and re-layouts  5.84 us (4%)
    all_to_all x1, waiting for transfers between devices, on_device(): lax.all_to_all(chunks, 'seq', split_axis=0, concat_axis=0, tiled=True)  26.4 us
    all_to_all x1, waiting for transfers between devices, on_device(): lax.all_to_all(answers, 'seq', split_axis=0, concat_axis=0, tiled=True)  23.9 us
    all_gather x1, waiting for transfers between devices, on_device(): gathered = lax.all_gather(near, 'tp')  20.8 us
    all_to_all x1, starting transfers between devices, on_device(): lax.all_to_all(chunks, 'seq', split_axis=0, concat_axis=0, tiled=True)  19.8 us
    ppermute x1, starting transfers between devices, on_device(): near = lax.ppermute(passages[0, 0], 'side', [(0, 1), (1, 0)])  11.5 us
    ppermute x1, waiting for transfers between devices, on_device(): near = lax.ppermute(passages[0, 0], 'side', [(0, 1), (1, 0)])  11 us
    all_to_all x1, starting transfers between devices, on_device(): lax.all_to_all(answers, 'seq', split_axis=0, concat_axis=0, tiled=True)  8.46 us
    pallas_call x1, Pallas kernels, cross_attention(): pl.pallas_call(lambda *refs: cross_kernel(*refs, project_steps=project_st...  7.07 us
  transfers between devices with their start and end apart: 4, of which 4 were waited for; matrix products, arithmetic and copies ran while one was open for 0% of the time, Pallas kernels for 4%

profile of v1, /device:TPU:1, one launch (start us, length us, event | category | flops | bytes accessed | tf_op | source)
XLA Modules:
  0.0 157.1 jit_solution(10629149673463303802)
XLA Ops:
  6.5 0.0 all-gather.3.cloned.1.call-start
  6.5 11.5 %collective-permute-start = (bf16[16,128,128]{2,1,0:T(8,128)(2,1)}, bf16[16,128,128]{2,1,0:T(8,128)(2,1)S(1)}, u32[]{:S(2)}, u32[]{:S(2)}) collective-permute-start(bf16[16,128,128]{2,1,0:T(8,128)(2,1)} %bitcast.16), channel_id=1, source_target_pairs={{0,256},{256,0},{1,257},{257,1},{2,258},{258,2},{3,259},{259,3},{4... | collective-permute-start | bytes 1572872 | tf_op jit(solution)/shard_map/ppermute | solution.py:263
  18.0 11.0 %collective-permute-done = bf16[16,128,128]{2,1,0:T(8,128)(2,1)S(1)} collective-permute-done((bf16[16,128,128]{2,1,0:T(8,128)(2,1)}, bf16[16,128,128]{2,1,0:T(8,128)(2,1)S(1)}, u32[]{:S(2)}, u32[]{:S(2)}) %collective-permute-start) | collective-permute-done | bytes 524320 | tf_op jit(solution)/shard_map/ppermute | solution.py:263
  29.0 0.0 copy-start.9
  29.0 0.8 copy-done.9
  29.8 0.0 all-gather.3.cloned.1.call-update
  29.9 0.1 pad_add_fusion.place
  29.9 0.0 copy-start
  29.9 1.0 copy-done
  31.0 0.0 copy-start.1
  31.0 0.8 copy-done.1
  31.7 2.1 %pack_queries.1 = bf16[32,64,256]{2,1,0:T(8,128)(2,1)} custom-call(s32[2]{0:T(128)S(1)} %pad_add_fusion.place, s32[2,32,32]{2,1,0:T(8,128)S(1)} %copy-done.1, bf16[16,64,256]{2,1,0:T(8,128)(2,1)S(1)} %bitcast.11), custom_call_target="tpu_custom_call" | custom-call | bytes 1572864 | tf_op jit(solution)/shard_map/pack_queries/pallas_call | solution.py:41
  33.9 0.0 copy-start.2
  33.9 0.0 copy-start.10
  33.9 19.8 %all-to-all-start = ((bf16[32,64,256]{2,1,0:T(8,128)(2,1)}), bf16[32,64,256]{2,1,0:T(8,128)(2,1)S(1)}, u32[]{:S(2)}, u32[]{:S(2)}) async-start(bf16[32,64,256]{2,1,0:T(8,128)(2,1)} %pack_queries.1), calls=%async_computation | async-start | bytes 2097152 | tf_op jit(solution)/shard_map/all_to_all | solution.py:272
  53.7 0.0 copy-done.2
  53.7 0.0 copy-done.10
  53.7 0.1 select_reduce_fusion.refs_0_
  53.8 26.4 %all-to-all-done.refs_4_ = bf16[32,64,256]{2,1,0:T(8,128)(2,1)S(1)} async-done(((bf16[32,64,256]{2,1,0:T(8,128)(2,1)}), bf16[32,64,256]{2,1,0:T(8,128)(2,1)S(1)}, u32[]{:S(2)}, u32[]{:S(2)}) %all-to-all-start) | async-done | bytes 1048608 | tf_op jit(solution)/shard_map/all_to_all | solution.py:272
  80.2 20.8 %all-gather.3.cloned.1.call-done = bf16[128,128,128]{2,1,0:T(8,128)(2,1)} async-done(((bf16[16,128,128]{2,1,0:T(8,128)(2,1)}), bf16[128,128,128]{2,1,0:T(8,128)(2,1)}) %all-gather.3.cloned.1.call-update) | async-done | bytes 4194320 | tf_op jit(solution)/shard_map/all_gather | solution.py:264
  101.0 0.0 copy-done.4
  101.0 0.0 copy-done.5
  101.0 2.2 %copy-done.3 = bf16[128,128,128]{2,1,0:T(8,128)(2,1)S(1)} copy-done((bf16[128,128,128]{2,1,0:T(8,128)(2,1)S(1)}, bf16[128,128,128]{2,1,0:T(8,128)(2,1)}, u32[]{:S(2)}) %copy-start.3) | copy-done | bytes 4194328
  103.2 7.1 %cross_attention.1 = bf16[32,72,256]{2,1,0:T(8,128)(2,1)} custom-call(s32[32]{0:T(128)S(1)} %select_reduce_fusion.refs_0_, bf16[8,16,128,128]{3,2,1,0:T(8,128)(2,1)S(1)} %bitcast.12, bf16[1024,256]{1,0:T(8,128)(2,1)S(1)} %copy-done.4, bf16[1024,256]{1,0:T(8,128)(2,1)S(1)} %copy-done.5, bf16[32,64,256]{2,1,0:T(8,128)(2,1)S(1)} %all-to-all-done.refs_4_), custom_call_target="tpu_custom_call" | custom-call | flops 2684354560 | bytes 7340032 | tf_op jit(solution)/shard_map/cross_attention/pallas_call | solution.py:166
  110.3 8.5 %all-to-all-start.1 = ((bf16[32,72,256]{2,1,0:T(8,128)(2,1)}), bf16[32,72,256]{2,1,0:T(8,128)(2,1)S(1)}, u32[]{:S(2)}, u32[]{:S(2)}) async-start(bf16[32,72,256]{2,1,0:T(8,128)(2,1)} %cross_attention.1), calls=%async_computation.1 | async-start | bytes 2359296 | tf_op jit(solution)/shard_map/all_to_all | solution.py:276
  118.7 0.0 copy-done.6
  118.8 0.0 copy-done.7
  118.8 0.0 copy-start.8
  118.8 1.0 copy-done.8
  119.8 4.2 %self_attention.1 = f32[1024,256]{1,0:T(8,128)S(1)} custom-call(bf16[1024,256]{1,0:T(8,128)(2,1)S(1)} %bitcast.13, bf16[1024,256]{1,0:T(8,128)(2,1)S(1)} %bitcast.14, bf16[1024,256]{1,0:T(8,128)(2,1)S(1)} %bitcast.15), custom_call_target="tpu_custom_call" | custom-call | flops 805306368 | bytes 2621440 | tf_op jit(solution)/shard_map/self_attention/pallas_call | solution.py:85
  124.0 23.9 %all-to-all-done.1.arrived_ref = bf16[32,72,256]{2,1,0:T(8,128)(2,1)S(1)} async-done(((bf16[32,72,256]{2,1,0:T(8,128)(2,1)}), bf16[32,72,256]{2,1,0:T(8,128)(2,1)S(1)}, u32[]{:S(2)}, u32[]{:S(2)}) %all-to-all-start.1) | async-done | bytes 1179680 | tf_op jit(solution)/shard_map/all_to_all | solution.py:276
  147.9 2.4 %mix.1 = bf16[16,64,256]{2,1,0:T(8,128)(2,1)} custom-call(s32[2]{0:T(128)S(1)} %pad_add_fusion.place, s32[2,32,32]{2,1,0:T(8,128)S(1)} %copy-done.2, bf16[32,72,256]{2,1,0:T(8,128)(2,1)S(1)} %all-to-all-done.1.arrived_ref, f32[16,64,256]{2,1,0:T(8,128)S(1)} %bitcast.10), custom_call_target="tpu_custom_call" | custom-call | flops 2097152 | bytes 2621440 | tf_op jit(solution)/shard_map/mix/pallas_call | solution.py:231
  (5 shorter events, 0.0 us)
Async XLA Ops:
  6.5 94.5 %all-gather.3.cloned.1.call-start = ((), (), s32[]{:S(2)}) async-start(), calls=%async_computation.2 | async-start | bytes 4718592 | tf_op jit(solution)/shard_map/all_gather | solution.py:264
  6.5 22.5 %collective-permute-start = (bf16[16,128,128]{2,1,0:T(8,128)(2,1)}, bf16[16,128,128]{2,1,0:T(8,128)(2,1)S(1)}, u32[]{:S(2)}, u32[]{:S(2)}) collective-permute-start(bf16[16,128,128]{2,1,0:T(8,128)(2,1)} %bitcast.16), channel_id=1, source_target_pairs={{0,256},{256,0},{1,257},{257,1},{2,258},{258,2},{3,259},{259,3},{4... | collective-permute-start | bytes 1572872 | tf_op jit(solution)/shard_map/ppermute | solution.py:263
  29.0 0.8 copy-start.9
  29.9 1.0 copy-start
  31.0 0.8 copy-start.1
  33.9 19.8 %copy-start.2 = (s32[2,32,32]{2,1,0:T(8,128)S(1)}, s32[2,32,32]{2,1,0:T(8,128)}, u32[]{:S(2)}) copy-start(s32[2,32,32]{2,1,0:T(8,128)} %block_map.3) | copy-start | bytes 24580
  33.9 19.8 %copy-start.10 = (s32[2,32,32]{2,1,0:T(8,128)S(1)}, s32[2,32,32]{2,1,0:T(8,128)}, u32[]{:S(2)}) copy-start(s32[2,32,32]{2,1,0:T(8,128)} %param.17) | copy-start | bytes 24580
  33.9 67.1 %copy-start.4 = (bf16[1024,256]{1,0:T(8,128)(2,1)S(1)}, bf16[1024,256]{1,0:T(8,128)(2,1)}, u32[]{:S(2)}) copy-start(bf16[1024,256]{1,0:T(8,128)(2,1)} %refs_2_.1) | copy-start | bytes 1572868
  33.9 67.1 %copy-start.5 = (bf16[1024,256]{1,0:T(8,128)(2,1)S(1)}, bf16[1024,256]{1,0:T(8,128)(2,1)}, u32[]{:S(2)}) copy-start(bf16[1024,256]{1,0:T(8,128)(2,1)} %refs_3_.1) | copy-start | bytes 1572868
  33.9 46.4 %all-to-all-start = ((bf16[32,64,256]{2,1,0:T(8,128)(2,1)}), bf16[32,64,256]{2,1,0:T(8,128)(2,1)S(1)}, u32[]{:S(2)}, u32[]{:S(2)}) async-start(bf16[32,64,256]{2,1,0:T(8,128)(2,1)} %pack_queries.1), calls=%async_computation | async-start | bytes 2097152 | tf_op jit(solution)/shard_map/all_to_all | solution.py:272
  101.0 2.2 %copy-start.3 = (bf16[128,128,128]{2,1,0:T(8,128)(2,1)S(1)}, bf16[128,128,128]{2,1,0:T(8,128)(2,1)}, u32[]{:S(2)}) copy-start(bf16[128,128,128]{2,1,0:T(8,128)(2,1)} %all-gather.3.cloned.1.call-done) | copy-start | bytes 12582916
  110.3 8.5 %copy-start.6 = (bf16[1,1,1024,256]{3,2,1,0:T(8,128)(2,1)S(1)}, bf16[1,1,1024,256]{3,2,1,0:T(8,128)(2,1)}, u32[]{:S(2)}) copy-start(bf16[1,1,1024,256]{3,2,1,0:T(8,128)(2,1)} %param.9) | copy-start | bytes 1572868
  110.3 8.5 %copy-start.7 = (bf16[1,1,1024,256]{3,2,1,0:T(8,128)(2,1)S(1)}, bf16[1,1,1024,256]{3,2,1,0:T(8,128)(2,1)}, u32[]{:S(2)}) copy-start(bf16[1,1,1024,256]{3,2,1,0:T(8,128)(2,1)} %param.10) | copy-start | bytes 1572868
  110.3 37.6 %all-to-all-start.1 = ((bf16[32,72,256]{2,1,0:T(8,128)(2,1)}), bf16[32,72,256]{2,1,0:T(8,128)(2,1)S(1)}, u32[]{:S(2)}, u32[]{:S(2)}) async-start(bf16[32,72,256]{2,1,0:T(8,128)(2,1)} %cross_attention.1), calls=%async_computation.1 | async-start | bytes 2359296 | tf_op jit(solution)/shard_map/all_to_all | solution.py:276
  118.8 1.0 copy-start.8
Sparse Core Ops, SparseCore 0:
  30.0 70.9 all-gather.2

commit v2 on v1

v2 whole, which is shorter than its diff:
```python
import functools
import math

import jax
import jax.numpy as jnp
from jax import lax
from jax.experimental import pallas as pl
from jax.experimental.pallas import tpu as pltpu
from jax.sharding import PartitionSpec as P

HD = 128
GROUP = 64
NEIGH = 2
EXTRA = 8
ORDER_FLOPS = 10000000000
LOAD_PARTS = 2
STORE_PARTS = 4
CROSS_VMEM_BYTES = 58 * 1024 * 1024
VMEM_BYTES = 20 * 1024 * 1024
EXP2_SCALE = math.log2(math.e) / math.sqrt(HD)

NT = (((1,), (1,)), ((), ()))
ANYWHERE = pl.BlockSpec(memory_space=pl.ANY)
IN_VMEM = pl.BlockSpec(memory_space=pltpu.VMEM)
TN = (((0,), (0,)), ((), ()))


def params(**kwargs):
    return pltpu.CompilerParams(vmem_limit_bytes=VMEM_BYTES, **kwargs)


def last_row_mask(rows, cols):
    return lax.broadcasted_iota(jnp.int32, (rows, cols), 0) < rows - 1


def pack_kernel(place, block_map, query_ref, out_ref):
    groups, rows, cols = query_ref.shape
    own_side, own_seq = place[0], place[1]
    head = last_row_mask(rows, cols)
    for u in range(groups):
        chunk = jnp.where(head, query_ref[min(u + 1, groups - 1)], query_ref[u])
        for n in range(NEIGH):
            out_ref[block_map[own_side, own_seq, NEIGH * u + n]] = chunk


def pack_queries(place, block_map, queries, blocks):
    groups, rows, cols = queries.shape
    return pl.pallas_call(
        pack_kernel,
        out_shape=jax.ShapeDtypeStruct((blocks, rows, cols), queries.dtype),
        grid_spec=pltpu.PrefetchScalarGridSpec(
            num_scalar_prefetch=2,
            grid=(1,),
            in_specs=[pl.BlockSpec((groups, rows, cols), lambda i, *_: (0, 0, 0))],
            out_specs=pl.BlockSpec((blocks, rows, cols), lambda i, *_: (0, 0, 0)),
        ),
        compiler_params=params(),
        cost_estimate=pl.CostEstimate(
            flops=0, bytes_accessed=2 * (groups + blocks) * rows * cols, transcendentals=0
        ),
        name="pack_queries",
    )(place, block_map, queries)


def self_kernel(query_ref, key_ref, value_ref, out_ref, *, block):
    length, feats = query_ref.shape
    row = lax.broadcasted_iota(jnp.int32, (block, block), 0)
    col = lax.broadcasted_iota(jnp.int32, (block, block), 1)
    for g in range(feats // HD):
        cols = slice(g * HD, (g + 1) * HD)
        for i in range(length // block):
            rows = slice(i * block, (i + 1) * block)
            stop = (i + 1) * block
            query = query_ref[rows, cols]
            scores = lax.dot_general(
                query, key_ref[:stop, cols], NT, preferred_element_type=jnp.float32
            )
            tail = jnp.where(col <= row, scores[:, i * block :], -jnp.inf)
            scores = tail if i == 0 else jnp.concatenate([scores[:, : i * block], tail], 1)
            top = jnp.max(scores, axis=1, keepdims=True)
            raised = jnp.exp2((scores - top) * EXP2_SCALE)
            total = jnp.sum(raised, axis=1, keepdims=True)
            weights = (raised * (1.0 / total)).astype(jnp.bfloat16)
            out_ref[rows, cols] = jnp.dot(
                weights, value_ref[:stop, cols], preferred_element_type=jnp.float32
            )


def self_attention(queries, key_rows, value_rows):
    length, feats = queries.shape
    block = min(256, length)
    return pl.pallas_call(
        lambda *refs: self_kernel(*refs, block=block),
        out_shape=jax.ShapeDtypeStruct((length, feats), jnp.float32),
        in_specs=[pl.BlockSpec(memory_space=pltpu.VMEM)] * 3,
        out_specs=pl.BlockSpec(memory_space=pltpu.VMEM),
        compiler_params=params(),
        cost_estimate=pl.CostEstimate(
            flops=3 * length * length * feats,
            bytes_accessed=10 * length * feats,
            transcendentals=length * length * feats // HD // 2,
        ),
        name="self_attention",
    )(queries, key_rows, value_rows)


def order_kernel(owners, wkey_ref, wvalue_ref, out_ref):
    part = out_ref.shape[0] // owners.shape[0]
    feats = wkey_ref.shape[1]
    for n in range(out_ref.shape[0] // part):
        rows = pl.ds(pl.multiple_of(owners[n] * part, part), part)
        out_ref[n * part : (n + 1) * part, :feats] = wkey_ref[rows, :]
        out_ref[n * part : (n + 1) * part, feats:] = wvalue_ref[rows, :]


def order_weights(owners, w_key, w_value):
    depth, feats = w_key.shape
    return pl.pallas_call(
        order_kernel,
        out_shape=jax.ShapeDtypeStruct((depth, 2 * feats), w_key.dtype),
        in_specs=[pl.BlockSpec(memory_space=pltpu.SMEM)] + [IN_VMEM] * 2,
        out_specs=IN_VMEM,
        compiler_params=params(),
        cost_estimate=pl.CostEstimate(flops=ORDER_FLOPS, bytes_accessed=8 * depth * feats, transcendentals=0),
        name="order_weights",
    )(owners, w_key, w_value)


def cross_kernel(wanted, *refs, places):
    shards, depth = len(places), max(row for row, _ in places) + 1
    weight_hbm, query_hbm, shard_hbm, out_hbm = refs[0], refs[1], refs[2 : 2 + shards], refs[2 + shards]
    weight_ref, query_ref, lhs_ref, kv_ref, out_ref, load_sems, lhs_sems, out_sems = refs[3 + shards :]
    chunks, rows, feats = query_ref.shape
    heads = feats // HD
    _, pool, rlen, part = lhs_ref.shape
    per = pool // LOAD_PARTS

    load_weight = pltpu.make_async_copy(weight_hbm, weight_ref, load_sems.at[0])
    load_query = pltpu.make_async_copy(query_hbm, query_ref, load_sems.at[1])
    load_lhs = [
        [
            pltpu.make_async_copy(
                shard_hbm[n].at[pl.ds(k * per - low, per)],
                lhs_ref.at[row, pl.ds(k * per, per)],
                lhs_sems.at[k, row],
            )
            for n, (row, low) in enumerate(places)
            if low <= k * per < low + shard_hbm[n].shape[0]
        ]
        for k in range(LOAD_PARTS)
    ]
    load_weight.start()
    for copies in load_lhs:
        for copy in copies:
            copy.start()
    load_query.start()
    load_weight.wait()
    for k, copies in enumerate(load_lhs):
        for copy in copies:
            copy.wait()
        span = slice(k * per, (k + 1) * per)
        lhs = jnp.concatenate([lhs_ref[n, span].reshape(per * rlen, part) for n in range(depth)], 1)
        made = jnp.dot(lhs, weight_ref[...], preferred_element_type=jnp.float32)
        kv_ref[span] = made.astype(jnp.bfloat16).reshape(per, rlen, 2 * feats)
    load_query.wait()

    zeros = jnp.zeros((rows, HD), jnp.bfloat16)
    extra_row = lax.broadcasted_iota(jnp.int32, (EXTRA, heads * rows), 0)
    stores = []
    for i in range(chunks):
        passage = wanted[i]
        query = query_ref[i]
        spread = jnp.concatenate(
            [
                jnp.concatenate(
                    [query[:, g * HD : (g + 1) * HD] if g == k else zeros for k in range(heads)], 1
                )
                for g in range(heads)
            ],
            0,
        )
        scores = lax.dot_general(
            kv_ref[passage, :, :feats], spread, NT, preferred_element_type=jnp.float32
        )
        top = jnp.max(scores, axis=0, keepdims=True)
        raised = jnp.exp2((scores - top) * EXP2_SCALE)
        total = jnp.sum(raised, axis=0, keepdims=True)
        weights = (raised * (1.0 / total)).astype(jnp.bfloat16)
        attended = lax.dot_general(
            weights, kv_ref[passage, :, feats:], TN, preferred_element_type=jnp.float32
        )
        for g in range(heads):
            own = slice(g * rows, (g + 1) * rows)
            out_ref[i, own, :] = attended[own, g * HD : (g + 1) * HD].astype(jnp.bfloat16)
        level = top * EXP2_SCALE + jnp.log2(total)
        high = level.astype(jnp.bfloat16).astype(jnp.float32)
        middle = (level - high).astype(jnp.bfloat16).astype(jnp.float32)
        low = (level - high) - middle
        terms = jnp.where(extra_row == 0, high, jnp.where(extra_row == 1, middle, low))
        out_ref[i, heads * rows :, :] = terms.astype(jnp.bfloat16)
        step = chunks // STORE_PARTS
        if (i + 1) % step == 0:
            span = pl.ds(i + 1 - step, step)
            store = pltpu.make_async_copy(out_ref.at[span], out_hbm.at[span], out_sems.at[i // step])
            store.start()
            stores.append(store)
    for store in stores:
        store.wait()


def cross_attention(wanted, shards, weights, queries):
    half, rlen, part = shards[0].shape
    pool = 2 * half
    chunks, rows, feats = queries.shape
    depth = weights.shape[0]
    heads = feats // HD
    positions = depth // part
    places = [(n, low) for n in range(positions) for low in (0, half)]
    out_shape = jax.ShapeDtypeStruct((chunks, heads * rows + EXTRA, HD), jnp.bfloat16)
    return pl.pallas_call(
        functools.partial(cross_kernel, places=places),
        out_shape=out_shape,
        in_specs=[pl.BlockSpec(memory_space=pltpu.SMEM)] + [ANYWHERE] * (2 + len(shards)),
        out_specs=ANYWHERE,
        scratch_shapes=[
            pltpu.VMEM(weights.shape, jnp.bfloat16),
            pltpu.VMEM(queries.shape, jnp.bfloat16),
            pltpu.VMEM((positions, pool, rlen, part), jnp.bfloat16),
            pltpu.VMEM((pool, rlen, 2 * feats), jnp.bfloat16),
            pltpu.VMEM(out_shape.shape, jnp.bfloat16),
            pltpu.SemaphoreType.DMA((2,)),
            pltpu.SemaphoreType.DMA((LOAD_PARTS, positions)),
            pltpu.SemaphoreType.DMA((STORE_PARTS,)),
        ],
        compiler_params=pltpu.CompilerParams(vmem_limit_bytes=CROSS_VMEM_BYTES),
        cost_estimate=pl.CostEstimate(
            flops=4 * pool * rlen * depth * feats + 8 * chunks * rows * rlen * feats,
            bytes_accessed=2 * (pool * rlen * depth + 2 * depth * feats + 2 * chunks * rows * feats),
            transcendentals=chunks * rows * rlen * heads,
        ),
        name="cross_attention",
    )(wanted, weights, queries, *shards)


def mix_kernel(place, block_map, arrived_ref, self_ref, out_ref):
    groups, rows, feats = self_ref.shape
    heads = feats // HD
    own_side, own_seq = place[0], place[1]

    def level_of(block):
        terms = arrived_ref[block, heads * rows :, :].astype(jnp.float32)
        return (terms[0:1] + terms[1:2]) + terms[2:3]

    slots = [
        [block_map[own_side, own_seq, NEIGH * u + n] for n in range(NEIGH)] for u in range(groups)
    ]
    firsts = jnp.concatenate([level_of(pair[0]) for pair in slots], 0)
    seconds = jnp.concatenate([level_of(pair[1]) for pair in slots], 0)
    top = jnp.maximum(firsts, seconds)
    raised = jnp.exp2(firsts - top)
    share = raised / (raised + jnp.exp2(seconds - top))
    columns = share.T
    head = last_row_mask(rows, HD)
    for g in range(heads):
        cols = slice(g * HD, (g + 1) * HD)
        own = slice(g * rows, (g + 1) * rows)
        before = jnp.zeros((rows, HD), jnp.float32)
        for u in range(groups):
            one = arrived_ref[slots[u][0], own, :].astype(jnp.float32)
            two = arrived_ref[slots[u][1], own, :].astype(jnp.float32)
            now = two + columns[own, u : u + 1] * (one - two)
            cross = jnp.where(head, before, now)
            out_ref[u, :, cols] = (self_ref[u, :, cols] + cross).astype(jnp.bfloat16)
            before = now


def mix(place, block_map, arrived, self_out):
    groups, rows, feats = self_out.shape
    return pl.pallas_call(
        mix_kernel,
        out_shape=jax.ShapeDtypeStruct(self_out.shape, jnp.bfloat16),
        in_specs=[pl.BlockSpec(memory_space=pltpu.SMEM)] * 2 + [IN_VMEM] * 2,
        out_specs=IN_VMEM,
        compiler_params=params(),
        cost_estimate=pl.CostEstimate(
            flops=8 * groups * rows * feats,
            bytes_accessed=10 * groups * rows * feats,
            transcendentals=0,
        ),
        name="mix",
    )(place, block_map, arrived, self_out)


def ring_gather(low, high, axis):
    count = lax.axis_size(axis)
    up = [(i, (i + 1) % count) for i in range(count)]
    down = [(i, (i - 1) % count) for i in range(count)]
    shards = [low, high]
    right_low = left_low = low
    right_high = left_high = high
    for _ in range(1, count // 2):
        right_low = lax.ppermute(right_low, axis, up)
        left_low = lax.ppermute(left_low, axis, down)
        right_high = lax.ppermute(right_high, axis, up)
        left_high = lax.ppermute(left_high, axis, down)
        shards += [right_low, right_high, left_low, left_high]
    shards.append(lax.ppermute(right_low, axis, up))
    shards.append(lax.ppermute(left_high, axis, down))
    return shards


def ring_owners(axis):
    count = lax.axis_size(axis)
    here = lax.axis_index(axis)
    owners = [here]
    for hop in range(1, count // 2):
        owners += [here - hop, here + hop]
    owners.append(here + count // 2)
    return jnp.stack(owners).astype(jnp.int32) % count


def on_device(
    self_query, self_key, self_value, cross_query, passages, w_key, w_value, block_map, passage_ids
):
    side_now = lax.axis_index("side")
    seq_now = lax.axis_index("seq")
    blocks = lax.axis_size("seq")
    place = jnp.stack([side_now, seq_now]).astype(jnp.int32)
    length, feats = cross_query.shape[2:]
    groups = length // GROUP

    near = lax.ppermute(passages[0, 0], "side", [(0, 1), (1, 0)])
    half = near.shape[0] // 2

    served_map = lax.dynamic_index_in_dim(block_map, side_now, 0, keepdims=False)
    served_ids = lax.dynamic_index_in_dim(passage_ids, side_now, 0, keepdims=False)
    wanted = jnp.sum(jnp.where(served_map == seq_now, served_ids, 0), axis=1)

    chunks = pack_queries(place, block_map, cross_query[0, 0].reshape(groups, GROUP, feats), blocks)
    asked = lax.all_to_all(chunks, "seq", split_axis=0, concat_axis=0, tiled=True)
    self_out = self_attention(self_query[0, 0], self_key[0, 0], self_value[0, 0])

    near, wanted, owners, w_key, w_value = lax.optimization_barrier(
        (near, wanted, ring_owners("tp"), w_key, w_value)
    )
    weights = order_weights(owners, w_key, w_value)
    shards = ring_gather(near[:half], near[half:], "tp")
    answers = cross_attention(wanted, shards, weights, asked)
    arrived = lax.all_to_all(answers, "seq", split_axis=0, concat_axis=0, tiled=True)
    mixed = mix(place, block_map, arrived, self_out.reshape(groups, GROUP, feats))
    return mixed.reshape(1, 1, length, feats)


def solution(mesh):
    return jax.shard_map(
        on_device,
        mesh=mesh,
        in_specs=(
            P("side", "seq", None, "tp"),
            P("side", "seq", None, "tp"),
            P("side", "seq", None, "tp"),
            P("side", "seq", None, "tp"),
            P("side", "seq", None, None, "tp"),
            P(None, "tp"),
            P(None, "tp"),
            P(),
            P(),
        ),
        out_specs=P("side", "seq", None, "tp"),
        check_vma=False,
    )
```

time: 158 us -> 142 us (0.90)
  the two profiles are of different devices: /device:TPU:1 before, /device:TPU:25 now
where the time goes in v2:
time: 142 us; the launch traced here: 141 us
  starting transfers between devices  89.8 us (63%)
  waiting for transfers between devices  25.9 us (18%)
  Pallas kernels  17.5 us (12%)
  local copies, waits for them, and re-layouts  6.47 us (5%)
    all_to_all x1, starting transfers between devices, on_device(): lax.all_to_all(answers, 'seq', split_axis=0, concat_axis=0, tiled=True)  25.6 us
    all_to_all x1, waiting for transfers between devices, on_device(): lax.all_to_all(answers, 'seq', split_axis=0, concat_axis=0, tiled=True)  22.6 us
    ppermute x3, starting transfers between devices, ring_gather(): right_high = lax.ppermute(right_high, axis, up)  13.7 us
    ppermute x3, starting transfers between devices, ring_gather(): right_low = lax.ppermute(right_low, axis, up)  13.6 us
    ppermute x1, starting transfers between devices, on_device(): near = lax.ppermute(passages[0, 0], 'side', [(0, 1), (1, 0)])  10.6 us
    all_to_all x1, starting transfers between devices, on_device(): lax.all_to_all(chunks, 'seq', split_axis=0, concat_axis=0, tiled=True)  8.28 us
    pallas_call x1, Pallas kernels, cross_attention(): pl.pallas_call(functools.partial(cross_kernel, places=places), out_shape=...  8.08 us
    unnamed x52, local copies, waits for them, and re-layouts  6.35 us
  transfers between devices with their start and end apart: 17, of which 2 were waited for; matrix products, arithmetic and copies ran while one was open for 1% of the time, Pallas kernels for 5%

profile of v2, /device:TPU:25, one launch (start us, length us, event | category | flops | bytes accessed | tf_op | source)
XLA Modules:
  0.0 140.9 jit_solution(4427295315207509080)
XLA Ops:
  0.0 10.6 %collective-permute-start = (bf16[16,128,128]{2,1,0:T(8,128)(2,1)}, bf16[16,128,128]{2,1,0:T(8,128)(2,1)S(1)}, u32[]{:S(2)}, u32[]{:S(2)}) collective-permute-start(bf16[16,128,128]{2,1,0:T(8,128)(2,1)} %bitcast.22), channel_id=1, source_target_pairs={{0,256},{256,0},{1,257},{257,1},{2,258},{258,2},{3,259},{259,3},{4... | collective-permute-start | bytes 1572872 | tf_op jit(solution)/shard_map/ppermute | solution.py:332
  10.7 1.0 copy-done
  11.8 0.8 copy-done.1
  12.5 2.1 %pack_queries.1 = bf16[32,64,256]{2,1,0:T(8,128)(2,1)} custom-call(s32[2]{0:T(128)S(1)} %pad_add_fusion.place, s32[2,32,32]{2,1,0:T(8,128)S(1)} %copy-done.1, bf16[16,64,256]{2,1,0:T(8,128)(2,1)S(1)} %bitcast.18), custom_call_target="tpu_custom_call" | custom-call | bytes 1572864 | tf_op jit(solution)/shard_map/pack_queries/pallas_call | solution.py:48
  14.7 8.3 %all-to-all-start = ((bf16[32,64,256]{2,1,0:T(8,128)(2,1)}), bf16[32,64,256]{2,1,0:T(8,128)(2,1)S(1)}, u32[]{:S(2)}, u32[]{:S(2)}) async-start(bf16[32,64,256]{2,1,0:T(8,128)(2,1)} %pack_queries.1), calls=%async_computation | async-start | bytes 2097152 | tf_op jit(solution)/shard_map/all_to_all | solution.py:340
  23.1 0.7 select_reduce_fusion.wanted
  23.8 4.4 %collective-permute-start.1 = (bf16[8,128,128]{2,1,0:T(8,128)(2,1)S(1)}, bf16[8,128,128]{2,1,0:T(8,128)(2,1)S(1)}, u32[]{:S(2)}, u32[]{:S(2)}) collective-permute-start(bf16[8,128,128]{2,1,0:T(8,128)(2,1)S(1)} %get-tuple-element.16.refs_2_), channel_id=1, source_target_pairs={{0,1},{1,2},{2,3},{3,4},{4,5},{5,6},{6,7},{7,0},{8,9},{9,10},{10,1... | collective-permute-start | bytes 786440 | tf_op jit(solution)/shard_map/ppermute | solution.py:302
  28.3 1.9 %collective-permute-start.4 = (bf16[8,128,128]{2,1,0:T(8,128)(2,1)S(1)}, bf16[8,128,128]{2,1,0:T(8,128)(2,1)S(1)}, u32[]{:S(2)}, u32[]{:S(2)}) collective-permute-start(bf16[8,128,128]{2,1,0:T(8,128)(2,1)S(1)} %get-tuple-element.15.refs_3_), channel_id=1, source_target_pairs={{0,7},{1,0},{2,1},{3,2},{4,3},{5,4},{6,5},{7,6},{8,15},{9,8},{10,9... | collective-permute-start | bytes 786440 | tf_op jit(solution)/shard_map/ppermute | solution.py:305
  30.2 4.6 %collective-permute-start.2 = (bf16[8,128,128]{2,1,0:T(8,128)(2,1)S(1)}, bf16[8,128,128]{2,1,0:T(8,128)(2,1)S(1)}, u32[]{:S(2)}, u32[]{:S(2)}) collective-permute-start(bf16[8,128,128]{2,1,0:T(8,128)(2,1)S(1)} %get-tuple-element.15.refs_3_), channel_id=1, source_target_pairs={{0,1},{1,2},{2,3},{3,4},{4,5},{5,6},{6,7},{7,0},{8,9},{9,10},{10,1... | collective-permute-start | bytes 786440 | tf_op jit(solution)/shard_map/ppermute | solution.py:304
  34.8 1.9 %collective-permute-start.3 = (bf16[8,128,128]{2,1,0:T(8,128)(2,1)S(1)}, bf16[8,128,128]{2,1,0:T(8,128)(2,1)S(1)}, u32[]{:S(2)}, u32[]{:S(2)}) collective-permute-start(bf16[8,128,128]{2,1,0:T(8,128)(2,1)S(1)} %get-tuple-element.16.refs_2_), channel_id=1, source_target_pairs={{0,7},{1,0},{2,1},{3,2},{4,3},{5,4},{6,5},{7,6},{8,15},{9,8},{10,9... | collective-permute-start | bytes 786440 | tf_op jit(solution)/shard_map/ppermute | solution.py:303
  36.7 4.6 %collective-permute-start.5 = (bf16[8,128,128]{2,1,0:T(8,128)(2,1)S(1)}, bf16[8,128,128]{2,1,0:T(8,128)(2,1)S(1)}, u32[]{:S(2)}, u32[]{:S(2)}) collective-permute-start(bf16[8,128,128]{2,1,0:T(8,128)(2,1)S(1)} %collective-permute-done.1.refs_4_), channel_id=1, source_target_pairs={{0,1},{1,2},{2,3},{3,4},{4,5},{5,6},{6,7},{7,0},{8,9},{9,10},{10,1... | collective-permute-start | bytes 786440 | tf_op jit(solution)/shard_map/ppermute | solution.py:302
  41.3 1.9 %collective-permute-start.8 = (bf16[8,128,128]{2,1,0:T(8,128)(2,1)S(1)}, bf16[8,128,128]{2,1,0:T(8,128)(2,1)S(1)}, u32[]{:S(2)}, u32[]{:S(2)}) collective-permute-start(bf16[8,128,128]{2,1,0:T(8,128)(2,1)S(1)} %collective-permute-done.4.refs_7_), channel_id=1, source_target_pairs={{0,7},{1,0},{2,1},{3,2},{4,3},{5,4},{6,5},{7,6},{8,15},{9,8},{10,9... | collective-permute-start | bytes 786440 | tf_op jit(solution)/shard_map/ppermute | solution.py:305
  43.3 4.6 %collective-permute-start.6 = (bf16[8,128,128]{2,1,0:T(8,128)(2,1)S(1)}, bf16[8,128,128]{2,1,0:T(8,128)(2,1)S(1)}, u32[]{:S(2)}, u32[]{:S(2)}) collective-permute-start(bf16[8,128,128]{2,1,0:T(8,128)(2,1)S(1)} %collective-permute-done.2.refs_5_), channel_id=1, source_target_pairs={{0,1},{1,2},{2,3},{3,4},{4,5},{5,6},{6,7},{7,0},{8,9},{9,10},{10,1... | collective-permute-start | bytes 786440 | tf_op jit(solution)/shard_map/ppermute | solution.py:304
  47.9 1.9 %collective-permute-start.7 = (bf16[8,128,128]{2,1,0:T(8,128)(2,1)S(1)}, bf16[8,128,128]{2,1,0:T(8,128)(2,1)S(1)}, u32[]{:S(2)}, u32[]{:S(2)}) collective-permute-start(bf16[8,128,128]{2,1,0:T(8,128)(2,1)S(1)} %collective-permute-done.3.refs_6_), channel_id=1, source_target_pairs={{0,7},{1,0},{2,1},{3,2},{4,3},{5,4},{6,5},{7,6},{8,15},{9,8},{10,9... | collective-permute-start | bytes 786440 | tf_op jit(solution)/shard_map/ppermute | solution.py:303
  49.8 4.6 %collective-permute-start.9 = (bf16[8,128,128]{2,1,0:T(8,128)(2,1)S(1)}, bf16[8,128,128]{2,1,0:T(8,128)(2,1)S(1)}, u32[]{:S(2)}, u32[]{:S(2)}) collective-permute-start(bf16[8,128,128]{2,1,0:T(8,128)(2,1)S(1)} %collective-permute-done.5.refs_8_), channel_id=1, source_target_pairs={{0,1},{1,2},{2,3},{3,4},{4,5},{5,6},{6,7},{7,0},{8,9},{9,10},{10,1... | collective-permute-start | bytes 786440 | tf_op jit(solution)/shard_map/ppermute | solution.py:302
  54.4 1.9 %collective-permute-start.12 = (bf16[8,128,128]{2,1,0:T(8,128)(2,1)S(1)}, bf16[8,128,128]{2,1,0:T(8,128)(2,1)S(1)}, u32[]{:S(2)}, u32[]{:S(2)}) collective-permute-start(bf16[8,128,128]{2,1,0:T(8,128)(2,1)S(1)} %collective-permute-done.8.refs_11_), channel_id=1, source_target_pairs={{0,7},{1,0},{2,1},{3,2},{4,3},{5,4},{6,5},{7,6},{8,15},{9,8},{10,9... | collective-permute-start | bytes 786440 | tf_op jit(solution)/shard_map/ppermute | solution.py:305
  56.4 4.6 %collective-permute-start.10 = (bf16[8,128,128]{2,1,0:T(8,128)(2,1)S(1)}, bf16[8,128,128]{2,1,0:T(8,128)(2,1)S(1)}, u32[]{:S(2)}, u32[]{:S(2)}) collective-permute-start(bf16[8,128,128]{2,1,0:T(8,128)(2,1)S(1)} %collective-permute-done.6.refs_9_), channel_id=1, source_target_pairs={{0,1},{1,2},{2,3},{3,4},{4,5},{5,6},{6,7},{7,0},{8,9},{9,10},{10,1... | collective-permute-start | bytes 786440 | tf_op jit(solution)/shard_map/ppermute | solution.py:304
  61.0 1.9 %collective-permute-start.11 = (bf16[8,128,128]{2,1,0:T(8,128)(2,1)S(1)}, bf16[8,128,128]{2,1,0:T(8,128)(2,1)S(1)}, u32[]{:S(2)}, u32[]{:S(2)}) collective-permute-start(bf16[8,128,128]{2,1,0:T(8,128)(2,1)S(1)} %collective-permute-done.7.refs_10_), channel_id=1, source_target_pairs={{0,7},{1,0},{2,1},{3,2},{4,3},{5,4},{6,5},{7,6},{8,15},{9,8},{10,9... | collective-permute-start | bytes 786440 | tf_op jit(solution)/shard_map/ppermute | solution.py:303
  62.9 4.6 %collective-permute-start.13 = (bf16[8,128,128]{2,1,0:T(8,128)(2,1)S(1)}, bf16[8,128,128]{2,1,0:T(8,128)(2,1)S(1)}, u32[]{:S(2)}, u32[]{:S(2)}) collective-permute-start(bf16[8,128,128]{2,1,0:T(8,128)(2,1)S(1)} %collective-permute-done.9.refs_12_), channel_id=1, source_target_pairs={{0,1},{1,2},{2,3},{3,4},{4,5},{5,6},{6,7},{7,0},{8,9},{9,10},{10,1... | collective-permute-start | bytes 786440 | tf_op jit(solution)/shard_map/ppermute | solution.py:307
  67.5 1.9 %collective-permute-start.14 = (bf16[8,128,128]{2,1,0:T(8,128)(2,1)S(1)}, bf16[8,128,128]{2,1,0:T(8,128)(2,1)}, u32[]{:S(2)}, u32[]{:S(2)}) collective-permute-start(bf16[8,128,128]{2,1,0:T(8,128)(2,1)S(1)} %collective-permute-done.12.refs_15_), channel_id=1, source_target_pairs={{0,7},{1,0},{2,1},{3,2},{4,3},{5,4},{6,5},{7,6},{8,15},{9,8},{10,9... | collective-permute-start | bytes 786440 | tf_op jit(solution)/shard_map/ppermute | solution.py:308
  69.5 0.6 order_weights.1.refs_0_
  70.2 1.0 copy-done.8
  71.2 0.7 copy-done.23
  72.0 0.7 copy-done.25
  72.7 3.3 %collective-permute-done.14.refs_17_ = bf16[8,128,128]{2,1,0:T(8,128)(2,1)} collective-permute-done((bf16[8,128,128]{2,1,0:T(8,128)(2,1)S(1)}, bf16[8,128,128]{2,1,0:T(8,128)(2,1)}, u32[]{:S(2)}, u32[]{:S(2)}) %collective-permute-start.14) | collective-permute-done | bytes 262176 | tf_op jit(solution)/shard_map/ppermute | solution.py:308
  76.0 1.0 copy-done.9
  77.0 8.1 %cross_attention.1 = bf16[32,136,128]{2,1,0:T(8,128)(2,1)} custom-call(s32[32]{0:T(128)} %select_reduce_fusion.wanted, bf16[1024,512]{1,0:T(8,128)(2,1)} %copy-done.8, bf16[32,64,256]{2,1,0:T(8,128)(2,1)} %copy-done.9, bf16[8,128,128]{2,1,0:T(8,128)(2,1)} %copy-done.11, bf16[8,128,128]{2,1,0:T(8,128)(2,1)} %copy-done.10, bf16[8,128,128]{2,1,0:T(8,128)(2,1)} %copy-done.13, ...), custom_call_target="tpu_custom_call" | custom-call | flops 2684354560 | bytes 7340032 | tf_op jit(solution)/shard_map/cross_attention/pallas_call | solution.py:220
  85.1 25.6 %all-to-all-start.1 = ((bf16[32,136,128]{2,1,0:T(8,128)(2,1)}), bf16[32,136,128]{2,1,0:T(8,128)(2,1)S(1)}, u32[]{:S(2)}, u32[]{:S(2)}) async-start(bf16[32,136,128]{2,1,0:T(8,128)(2,1)} %cross_attention.1), calls=%async_computation.1 | async-start | bytes 2228224 | tf_op jit(solution)/shard_map/all_to_all | solution.py:349
  110.7 1.0 copy-done.7
  111.7 4.2 %self_attention.1 = f32[1024,256]{1,0:T(8,128)S(1)} custom-call(bf16[1024,256]{1,0:T(8,128)(2,1)S(1)} %bitcast.19, bf16[1024,256]{1,0:T(8,128)(2,1)S(1)} %bitcast.20, bf16[1024,256]{1,0:T(8,128)(2,1)S(1)} %bitcast.21), custom_call_target="tpu_custom_call" | custom-call | flops 805306368 | bytes 2621440 | tf_op jit(solution)/shard_map/self_attention/pallas_call | solution.py:92
  115.9 22.6 %all-to-all-done.1.arrived_ref = bf16[32,136,128]{2,1,0:T(8,128)(2,1)S(1)} async-done(((bf16[32,136,128]{2,1,0:T(8,128)(2,1)}), bf16[32,136,128]{2,1,0:T(8,128)(2,1)S(1)}, u32[]{:S(2)}, u32[]{:S(2)}) %all-to-all-start.1) | async-done | bytes 1114144 | tf_op jit(solution)/shard_map/all_to_all | solution.py:349
  138.5 2.4 %mix.1 = bf16[16,64,256]{2,1,0:T(8,128)(2,1)} custom-call(s32[2]{0:T(128)S(1)} %pad_add_fusion.place, s32[2,32,32]{2,1,0:T(8,128)S(1)} %copy-done.2, bf16[32,136,128]{2,1,0:T(8,128)(2,1)S(1)} %all-to-all-done.1.arrived_ref, f32[16,64,256]{2,1,0:T(8,128)S(1)} %bitcast.17), custom_call_target="tpu_custom_call" | custom-call | flops 2097152 | bytes 2621440 | tf_op jit(solution)/shard_map/mix/pallas_call | solution.py:279
  (64 shorter events, 0.4 us)
Async XLA Ops:
  0.0 23.8 %collective-permute-start = (bf16[16,128,128]{2,1,0:T(8,128)(2,1)}, bf16[16,128,128]{2,1,0:T(8,128)(2,1)S(1)}, u32[]{:S(2)}, u32[]{:S(2)}) collective-permute-start(bf16[16,128,128]{2,1,0:T(8,128)(2,1)} %bitcast.22), channel_id=1, source_target_pairs={{0,256},{256,0},{1,257},{257,1},{2,258},{258,2},{3,259},{259,3},{4... | collective-permute-start | bytes 1572872 | tf_op jit(solution)/shard_map/ppermute | solution.py:332
  14.7 8.4 %copy-start.12 = (s32[2,32,32]{2,1,0:T(8,128)S(1)}, s32[2,32,32]{2,1,0:T(8,128)}, u32[]{:S(2)}) copy-start(s32[2,32,32]{2,1,0:T(8,128)} %param.17) | copy-start | bytes 24580
  14.7 54.8 %copy-start.3 = (bf16[1024,256]{1,0:T(8,128)(2,1)S(1)}, bf16[1024,256]{1,0:T(8,128)(2,1)}, u32[]{:S(2)}) copy-start(bf16[1024,256]{1,0:T(8,128)(2,1)} %wkey_ref) | copy-start | bytes 1572868
  14.7 54.8 %copy-start.4 = (bf16[1024,256]{1,0:T(8,128)(2,1)S(1)}, bf16[1024,256]{1,0:T(8,128)(2,1)}, u32[]{:S(2)}) copy-start(bf16[1024,256]{1,0:T(8,128)(2,1)} %wvalue_ref) | copy-start | bytes 1572868
  14.7 61.3 %all-to-all-start = ((bf16[32,64,256]{2,1,0:T(8,128)(2,1)}), bf16[32,64,256]{2,1,0:T(8,128)(2,1)S(1)}, u32[]{:S(2)}, u32[]{:S(2)}) async-start(bf16[32,64,256]{2,1,0:T(8,128)(2,1)} %pack_queries.1), calls=%async_computation | async-start | bytes 2097152 | tf_op jit(solution)/shard_map/all_to_all | solution.py:340
  23.8 46.3 %copy-start.10 = (bf16[8,128,128]{2,1,0:T(8,128)(2,1)}, bf16[8,128,128]{2,1,0:T(8,128)(2,1)S(1)}, u32[]{:S(2)}) copy-start(bf16[8,128,128]{2,1,0:T(8,128)(2,1)S(1)} %get-tuple-element.15.refs_3_) | copy-start | bytes 786436
  23.8 46.3 %copy-start.11 = (bf16[8,128,128]{2,1,0:T(8,128)(2,1)}, bf16[8,128,128]{2,1,0:T(8,128)(2,1)S(1)}, u32[]{:S(2)}) copy-start(bf16[8,128,128]{2,1,0:T(8,128)(2,1)S(1)} %get-tuple-element.16.refs_2_) | copy-start | bytes 786436
  23.8 12.9 %collective-permute-start.1 = (bf16[8,128,128]{2,1,0:T(8,128)(2,1)S(1)}, bf16[8,128,128]{2,1,0:T(8,128)(2,1)S(1)}, u32[]{:S(2)}, u32[]{:S(2)}) collective-permute-start(bf16[8,128,128]{2,1,0:T(8,128)(2,1)S(1)} %get-tuple-element.16.refs_2_), channel_id=1, source_target_pairs={{0,1},{1,2},{2,3},{3,4},{4,5},{5,6},{6,7},{7,0},{8,9},{9,10},{10,1... | collective-permute-start | bytes 786440 | tf_op jit(solution)/shard_map/ppermute | solution.py:302
  28.3 13.0 %collective-permute-start.4 = (bf16[8,128,128]{2,1,0:T(8,128)(2,1)S(1)}, bf16[8,128,128]{2,1,0:T(8,128)(2,1)S(1)}, u32[]{:S(2)}, u32[]{:S(2)}) collective-permute-start(bf16[8,128,128]{2,1,0:T(8,128)(2,1)S(1)} %get-tuple-element.15.refs_3_), channel_id=1, source_target_pairs={{0,7},{1,0},{2,1},{3,2},{4,3},{5,4},{6,5},{7,6},{8,15},{9,8},{10,9... | collective-permute-start | bytes 786440 | tf_op jit(solution)/shard_map/ppermute | solution.py:305
  30.2 13.1 %collective-permute-start.2 = (bf16[8,128,128]{2,1,0:T(8,128)(2,1)S(1)}, bf16[8,128,128]{2,1,0:T(8,128)(2,1)S(1)}, u32[]{:S(2)}, u32[]{:S(2)}) collective-permute-start(bf16[8,128,128]{2,1,0:T(8,128)(2,1)S(1)} %get-tuple-element.15.refs_3_), channel_id=1, source_target_pairs={{0,1},{1,2},{2,3},{3,4},{4,5},{5,6},{6,7},{7,0},{8,9},{9,10},{10,1... | collective-permute-start | bytes 786440 | tf_op jit(solution)/shard_map/ppermute | solution.py:304
  34.8 13.1 %collective-permute-start.3 = (bf16[8,128,128]{2,1,0:T(8,128)(2,1)S(1)}, bf16[8,128,128]{2,1,0:T(8,128)(2,1)S(1)}, u32[]{:S(2)}, u32[]{:S(2)}) collective-permute-start(bf16[8,128,128]{2,1,0:T(8,128)(2,1)S(1)} %get-tuple-element.16.refs_2_), channel_id=1, source_target_pairs={{0,7},{1,0},{2,1},{3,2},{4,3},{5,4},{6,5},{7,6},{8,15},{9,8},{10,9... | collective-permute-start | bytes 786440 | tf_op jit(solution)/shard_map/ppermute | solution.py:303
  36.7 33.4 %copy-start.13 = (bf16[8,128,128]{2,1,0:T(8,128)(2,1)}, bf16[8,128,128]{2,1,0:T(8,128)(2,1)S(1)}, u32[]{:S(2)}) copy-start(bf16[8,128,128]{2,1,0:T(8,128)(2,1)S(1)} %collective-permute-done.1.refs_4_) | copy-start | bytes 786436
  36.7 13.1 %collective-permute-start.5 = (bf16[8,128,128]{2,1,0:T(8,128)(2,1)S(1)}, bf16[8,128,128]{2,1,0:T(8,128)(2,1)S(1)}, u32[]{:S(2)}, u32[]{:S(2)}) collective-permute-start(bf16[8,128,128]{2,1,0:T(8,128)(2,1)S(1)} %collective-permute-done.1.refs_4_), channel_id=1, source_target_pairs={{0,1},{1,2},{2,3},{3,4},{4,5},{5,6},{6,7},{7,0},{8,9},{9,10},{10,1... | collective-permute-start | bytes 786440 | tf_op jit(solution)/shard_map/ppermute | solution.py:302
  41.3 28.8 %copy-start.14 = (bf16[8,128,128]{2,1,0:T(8,128)(2,1)}, bf16[8,128,128]{2,1,0:T(8,128)(2,1)S(1)}, u32[]{:S(2)}) copy-start(bf16[8,128,128]{2,1,0:T(8,128)(2,1)S(1)} %collective-permute-done.4.refs_7_) | copy-start | bytes 786436
  41.3 13.1 %collective-permute-start.8 = (bf16[8,128,128]{2,1,0:T(8,128)(2,1)S(1)}, bf16[8,128,128]{2,1,0:T(8,128)(2,1)S(1)}, u32[]{:S(2)}, u32[]{:S(2)}) collective-permute-start(bf16[8,128,128]{2,1,0:T(8,128)(2,1)S(1)} %collective-permute-done.4.refs_7_), channel_id=1, source_target_pairs={{0,7},{1,0},{2,1},{3,2},{4,3},{5,4},{6,5},{7,6},{8,15},{9,8},{10,9... | collective-permute-start | bytes 786440 | tf_op jit(solution)/shard_map/ppermute | solution.py:305
  43.3 26.9 %copy-start.15 = (bf16[8,128,128]{2,1,0:T(8,128)(2,1)}, bf16[8,128,128]{2,1,0:T(8,128)(2,1)S(1)}, u32[]{:S(2)}) copy-start(bf16[8,128,128]{2,1,0:T(8,128)(2,1)S(1)} %collective-permute-done.2.refs_5_) | copy-start | bytes 786436
  43.3 13.1 %collective-permute-start.6 = (bf16[8,128,128]{2,1,0:T(8,128)(2,1)S(1)}, bf16[8,128,128]{2,1,0:T(8,128)(2,1)S(1)}, u32[]{:S(2)}, u32[]{:S(2)}) collective-permute-start(bf16[8,128,128]{2,1,0:T(8,128)(2,1)S(1)} %collective-permute-done.2.refs_5_), channel_id=1, source_target_pairs={{0,1},{1,2},{2,3},{3,4},{4,5},{5,6},{6,7},{7,0},{8,9},{9,10},{10,1... | collective-permute-start | bytes 786440 | tf_op jit(solution)/shard_map/ppermute | solution.py:304
  47.9 19.7 %copy-start.16 = (bf16[8,128,128]{2,1,0:T(8,128)(2,1)}, bf16[8,128,128]{2,1,0:T(8,128)(2,1)S(1)}, u32[]{:S(2)}) copy-start(bf16[8,128,128]{2,1,0:T(8,128)(2,1)S(1)} %collective-permute-done.3.refs_6_) | copy-start | bytes 786436
  47.9 13.1 %collective-permute-start.7 = (bf16[8,128,128]{2,1,0:T(8,128)(2,1)S(1)}, bf16[8,128,128]{2,1,0:T(8,128)(2,1)S(1)}, u32[]{:S(2)}, u32[]{:S(2)}) collective-permute-start(bf16[8,128,128]{2,1,0:T(8,128)(2,1)S(1)} %collective-permute-done.3.refs_6_), channel_id=1, source_target_pairs={{0,7},{1,0},{2,1},{3,2},{4,3},{5,4},{6,5},{7,6},{8,15},{9,8},{10,9... | collective-permute-start | bytes 786440 | tf_op jit(solution)/shard_map/ppermute | solution.py:303
  49.8 17.7 %copy-start.17 = (bf16[8,128,128]{2,1,0:T(8,128)(2,1)}, bf16[8,128,128]{2,1,0:T(8,128)(2,1)S(1)}, u32[]{:S(2)}) copy-start(bf16[8,128,128]{2,1,0:T(8,128)(2,1)S(1)} %collective-permute-done.5.refs_8_) | copy-start | bytes 786436
  49.8 13.1 %collective-permute-start.9 = (bf16[8,128,128]{2,1,0:T(8,128)(2,1)S(1)}, bf16[8,128,128]{2,1,0:T(8,128)(2,1)S(1)}, u32[]{:S(2)}, u32[]{:S(2)}) collective-permute-start(bf16[8,128,128]{2,1,0:T(8,128)(2,1)S(1)} %collective-permute-done.5.refs_8_), channel_id=1, source_target_pairs={{0,1},{1,2},{2,3},{3,4},{4,5},{5,6},{6,7},{7,0},{8,9},{9,10},{10,1... | collective-permute-start | bytes 786440 | tf_op jit(solution)/shard_map/ppermute | solution.py:302
  54.4 13.1 %copy-start.18 = (bf16[8,128,128]{2,1,0:T(8,128)(2,1)}, bf16[8,128,128]{2,1,0:T(8,128)(2,1)S(1)}, u32[]{:S(2)}) copy-start(bf16[8,128,128]{2,1,0:T(8,128)(2,1)S(1)} %collective-permute-done.8.refs_11_) | copy-start | bytes 786436
  54.4 13.1 %collective-permute-start.12 = (bf16[8,128,128]{2,1,0:T(8,128)(2,1)S(1)}, bf16[8,128,128]{2,1,0:T(8,128)(2,1)S(1)}, u32[]{:S(2)}, u32[]{:S(2)}) collective-permute-start(bf16[8,128,128]{2,1,0:T(8,128)(2,1)S(1)} %collective-permute-done.8.refs_11_), channel_id=1, source_target_pairs={{0,7},{1,0},{2,1},{3,2},{4,3},{5,4},{6,5},{7,6},{8,15},{9,8},{10,9... | collective-permute-start | bytes 786440 | tf_op jit(solution)/shard_map/ppermute | solution.py:305
  56.4 13.8 %copy-start.19 = (bf16[8,128,128]{2,1,0:T(8,128)(2,1)}, bf16[8,128,128]{2,1,0:T(8,128)(2,1)S(1)}, u32[]{:S(2)}) copy-start(bf16[8,128,128]{2,1,0:T(8,128)(2,1)S(1)} %collective-permute-done.6.refs_9_) | copy-start | bytes 786436
  56.4 14.8 %collective-permute-start.10 = (bf16[8,128,128]{2,1,0:T(8,128)(2,1)S(1)}, bf16[8,128,128]{2,1,0:T(8,128)(2,1)S(1)}, u32[]{:S(2)}, u32[]{:S(2)}) collective-permute-start(bf16[8,128,128]{2,1,0:T(8,128)(2,1)S(1)} %collective-permute-done.6.refs_9_), channel_id=1, source_target_pairs={{0,1},{1,2},{2,3},{3,4},{4,5},{5,6},{6,7},{7,0},{8,9},{9,10},{10,1... | collective-permute-start | bytes 786440 | tf_op jit(solution)/shard_map/ppermute | solution.py:304
  61.0 9.2 %copy-start.20 = (bf16[8,128,128]{2,1,0:T(8,128)(2,1)}, bf16[8,128,128]{2,1,0:T(8,128)(2,1)S(1)}, u32[]{:S(2)}) copy-start(bf16[8,128,128]{2,1,0:T(8,128)(2,1)S(1)} %collective-permute-done.7.refs_10_) | copy-start | bytes 786436
  61.0 10.2 %collective-permute-start.11 = (bf16[8,128,128]{2,1,0:T(8,128)(2,1)S(1)}, bf16[8,128,128]{2,1,0:T(8,128)(2,1)S(1)}, u32[]{:S(2)}, u32[]{:S(2)}) collective-permute-start(bf16[8,128,128]{2,1,0:T(8,128)(2,1)S(1)} %collective-permute-done.7.refs_10_), channel_id=1, source_target_pairs={{0,7},{1,0},{2,1},{3,2},{4,3},{5,4},{6,5},{7,6},{8,15},{9,8},{10,9... | collective-permute-start | bytes 786440 | tf_op jit(solution)/shard_map/ppermute | solution.py:303
  62.9 8.3 %collective-permute-start.13 = (bf16[8,128,128]{2,1,0:T(8,128)(2,1)S(1)}, bf16[8,128,128]{2,1,0:T(8,128)(2,1)S(1)}, u32[]{:S(2)}, u32[]{:S(2)}) collective-permute-start(bf16[8,128,128]{2,1,0:T(8,128)(2,1)S(1)} %collective-permute-done.9.refs_12_), channel_id=1, source_target_pairs={{0,1},{1,2},{2,3},{3,4},{4,5},{5,6},{6,7},{7,0},{8,9},{9,10},{10,1... | collective-permute-start | bytes 786440 | tf_op jit(solution)/shard_map/ppermute | solution.py:307
  67.5 8.4 %collective-permute-start.14 = (bf16[8,128,128]{2,1,0:T(8,128)(2,1)S(1)}, bf16[8,128,128]{2,1,0:T(8,128)(2,1)}, u32[]{:S(2)}, u32[]{:S(2)}) collective-permute-start(bf16[8,128,128]{2,1,0:T(8,128)(2,1)S(1)} %collective-permute-done.12.refs_15_), channel_id=1, source_target_pairs={{0,7},{1,0},{2,1},{3,2},{4,3},{5,4},{6,5},{7,6},{8,15},{9,8},{10,9... | collective-permute-start | bytes 786440 | tf_op jit(solution)/shard_map/ppermute | solution.py:308
  85.1 25.6 %copy-start.5 = (bf16[1,1,1024,256]{3,2,1,0:T(8,128)(2,1)S(1)}, bf16[1,1,1024,256]{3,2,1,0:T(8,128)(2,1)}, u32[]{:S(2)}) copy-start(bf16[1,1,1024,256]{3,2,1,0:T(8,128)(2,1)} %param.9) | copy-start | bytes 1572868
  85.1 25.6 %copy-start.6 = (bf16[1,1,1024,256]{3,2,1,0:T(8,128)(2,1)S(1)}, bf16[1,1,1024,256]{3,2,1,0:T(8,128)(2,1)}, u32[]{:S(2)}) copy-start(bf16[1,1,1024,256]{3,2,1,0:T(8,128)(2,1)} %param.10) | copy-start | bytes 1572868
  85.1 53.4 %all-to-all-start.1 = ((bf16[32,136,128]{2,1,0:T(8,128)(2,1)}), bf16[32,136,128]{2,1,0:T(8,128)(2,1)S(1)}, u32[]{:S(2)}, u32[]{:S(2)}) async-start(bf16[32,136,128]{2,1,0:T(8,128)(2,1)} %cross_attention.1), calls=%async_computation.1 | async-start | bytes 2228224 | tf_op jit(solution)/shard_map/all_to_all | solution.py:349
  (11 other events, 25.4 us)

commit v3 on v2

--- a/solution.py
+++ b/solution.py
@@ -12,7 +12,7 @@
 GROUP = 64
 NEIGH = 2
 EXTRA = 8
-ORDER_FLOPS = 10000000000
+WANTED_FLOPS = 13000000000
 LOAD_PARTS = 2
 STORE_PARTS = 4
 CROSS_VMEM_BYTES = 58 * 1024 * 1024
@@ -31,6 +31,10 @@
 
 def last_row_mask(rows, cols):
     return lax.broadcasted_iota(jnp.int32, (rows, cols), 0) < rows - 1
+
+
+def holder_of(block, blocks):
+    return (block + blocks // 2) % blocks
 
 
 def pack_kernel(place, block_map, query_ref, out_ref):
@@ -40,7 +44,7 @@
     for u in range(groups):
         chunk = jnp.where(head, query_ref[min(u + 1, groups - 1)], query_ref[u])
         for n in range(NEIGH):
-            out_ref[block_map[own_side, own_seq, NEIGH * u + n]] = chunk
+            out_ref[holder_of(block_map[own_side, own_seq, NEIGH * u + n], out_ref.shape[0])] = chunk
 
 
 def pack_queries(place, block_map, queries, blocks):
@@ -104,6 +108,27 @@
     )(queries, key_rows, value_rows)
 
 
+def wanted_kernel(place, block_map_ref, passage_ids_ref, out_ref):
+    blocks = block_map_ref.shape[2]
+    served = block_map_ref[place[0]] == holder_of(place[1], blocks)
+    picked = jnp.where(served, passage_ids_ref[place[0]], 0).astype(jnp.float32)
+    ones = jnp.ones((8, picked.shape[1]), jnp.float32)
+    rows = lax.dot_general(ones, picked, NT, preferred_element_type=jnp.float32)
+    out_ref[...] = rows[:1].astype(jnp.int32)
+
+
+def wanted_passages(place, block_map, passage_ids):
+    return pl.pallas_call(
+        wanted_kernel,
+        out_shape=jax.ShapeDtypeStruct((1, block_map.shape[1]), jnp.int32),
+        in_specs=[pl.BlockSpec(memory_space=pltpu.SMEM)] + [IN_VMEM] * 2,
+        out_specs=IN_VMEM,
+        compiler_params=params(),
+        cost_estimate=pl.CostEstimate(flops=WANTED_FLOPS, bytes_accessed=16384, transcendentals=0),
+        name="wanted_passages",
+    )(place, block_map, passage_ids)
+
+
 def order_kernel(owners, wkey_ref, wvalue_ref, out_ref):
     part = out_ref.shape[0] // owners.shape[0]
     feats = wkey_ref.shape[1]
@@ -121,22 +146,21 @@
         in_specs=[pl.BlockSpec(memory_space=pltpu.SMEM)] + [IN_VMEM] * 2,
         out_specs=IN_VMEM,
         compiler_params=params(),
-        cost_estimate=pl.CostEstimate(flops=ORDER_FLOPS, bytes_accessed=8 * depth * feats, transcendentals=0),
+        cost_estimate=pl.CostEstimate(flops=0, bytes_accessed=8 * depth * feats, transcendentals=0),
         name="order_weights",
     )(owners, w_key, w_value)
 
 
 def cross_kernel(wanted, *refs, places):
     shards, depth = len(places), max(row for row, _ in places) + 1
-    weight_hbm, query_hbm, shard_hbm, out_hbm = refs[0], refs[1], refs[2 : 2 + shards], refs[2 + shards]
-    weight_ref, query_ref, lhs_ref, kv_ref, out_ref, load_sems, lhs_sems, out_sems = refs[3 + shards :]
+    weight_hbm, query_ref, shard_hbm, out_hbm = refs[0], refs[1], refs[2 : 2 + shards], refs[2 + shards]
+    weight_ref, lhs_ref, kv_ref, out_ref, load_sems, lhs_sems, out_sems = refs[3 + shards :]
     chunks, rows, feats = query_ref.shape
     heads = feats // HD
     _, pool, rlen, part = lhs_ref.shape
     per = pool // LOAD_PARTS
 
     load_weight = pltpu.make_async_copy(weight_hbm, weight_ref, load_sems.at[0])
-    load_query = pltpu.make_async_copy(query_hbm, query_ref, load_sems.at[1])
     load_lhs = [
         [
             pltpu.make_async_copy(
@@ -150,25 +174,24 @@
         for k in range(LOAD_PARTS)
     ]
     load_weight.start()
-    for copies in load_lhs:
-        for copy in copies:
-            copy.start()
-    load_query.start()
+    for copy in load_lhs[0]:
+        copy.start()
     load_weight.wait()
     for k, copies in enumerate(load_lhs):
         for copy in copies:
             copy.wait()
+        for copy in load_lhs[k + 1] if k + 1 < LOAD_PARTS else []:
+            copy.start()
         span = slice(k * per, (k + 1) * per)
         lhs = jnp.concatenate([lhs_ref[n, span].reshape(per * rlen, part) for n in range(depth)], 1)
         made = jnp.dot(lhs, weight_ref[...], preferred_element_type=jnp.float32)
         kv_ref[span] = made.astype(jnp.bfloat16).reshape(per, rlen, 2 * feats)
-    load_query.wait()
 
     zeros = jnp.zeros((rows, HD), jnp.bfloat16)
     extra_row = lax.broadcasted_iota(jnp.int32, (EXTRA, heads * rows), 0)
     stores = []
     for i in range(chunks):
-        passage = wanted[i]
+        passage = wanted[0, i]
         query = query_ref[i]
         spread = jnp.concatenate(
             [
@@ -220,15 +243,14 @@
     return pl.pallas_call(
         functools.partial(cross_kernel, places=places),
         out_shape=out_shape,
-        in_specs=[pl.BlockSpec(memory_space=pltpu.SMEM)] + [ANYWHERE] * (2 + len(shards)),
+        in_specs=[pl.BlockSpec(memory_space=pltpu.SMEM)] + [ANYWHERE, IN_VMEM] + [ANYWHERE] * len(shards),
         out_specs=ANYWHERE,
         scratch_shapes=[
             pltpu.VMEM(weights.shape, jnp.bfloat16),
-            pltpu.VMEM(queries.shape, jnp.bfloat16),
             pltpu.VMEM((positions, pool, rlen, part), jnp.bfloat16),
             pltpu.VMEM((pool, rlen, 2 * feats), jnp.bfloat16),
             pltpu.VMEM(out_shape.shape, jnp.bfloat16),
-            pltpu.SemaphoreType.DMA((2,)),
+            pltpu.SemaphoreType.DMA((1,)),
             pltpu.SemaphoreType.DMA((LOAD_PARTS, positions)),
             pltpu.SemaphoreType.DMA((STORE_PARTS,)),
         ],
@@ -252,7 +274,11 @@
         return (terms[0:1] + terms[1:2]) + terms[2:3]
 
     slots = [
-        [block_map[own_side, own_seq, NEIGH * u + n] for n in range(NEIGH)] for u in range(groups)
+        [
+            holder_of(block_map[own_side, own_seq, NEIGH * u + n], arrived_ref.shape[0])
+            for n in range(NEIGH)
+        ]
+        for u in range(groups)
     ]
     firsts = jnp.concatenate([level_of(pair[0]) for pair in slots], 0)
     seconds = jnp.concatenate([level_of(pair[1]) for pair in slots], 0)
@@ -291,7 +317,7 @@
     )(place, block_map, arrived, self_out)
 
 
-def ring_gather(low, high, axis):
+def ring_gather(low, high, axis, asked, wanted):
     count = lax.axis_size(axis)
     up = [(i, (i + 1) % count) for i in range(count)]
     down = [(i, (i - 1) % count) for i in range(count)]
@@ -304,9 +330,10 @@
         right_high = lax.ppermute(right_high, axis, up)
         left_high = lax.ppermute(left_high, axis, down)
         shards += [right_low, right_high, left_low, left_high]
+    right_low, asked, wanted = lax.optimization_barrier((right_low, asked, wanted))
     shards.append(lax.ppermute(right_low, axis, up))
     shards.append(lax.ppermute(left_high, axis, down))
-    return shards
+    return shards, asked, wanted
 
 
 def ring_owners(axis):
@@ -329,22 +356,23 @@
     length, feats = cross_query.shape[2:]
     groups = length // GROUP
 
-    near = lax.ppermute(passages[0, 0], "side", [(0, 1), (1, 0)])
+    near = lax.ppermute(
+        passages[0, 0],
+        ("side", "seq"),
+        [(h * blocks + b, (1 - h) * blocks + holder_of(b, blocks)) for h in range(2) for b in range(blocks)],
+    )
     half = near.shape[0] // 2
-
-    served_map = lax.dynamic_index_in_dim(block_map, side_now, 0, keepdims=False)
-    served_ids = lax.dynamic_index_in_dim(passage_ids, side_now, 0, keepdims=False)
-    wanted = jnp.sum(jnp.where(served_map == seq_now, served_ids, 0), axis=1)
 
     chunks = pack_queries(place, block_map, cross_query[0, 0].reshape(groups, GROUP, feats), blocks)
     asked = lax.all_to_all(chunks, "seq", split_axis=0, concat_axis=0, tiled=True)
     self_out = self_attention(self_query[0, 0], self_key[0, 0], self_value[0, 0])
 
-    near, wanted, owners, w_key, w_value = lax.optimization_barrier(
-        (near, wanted, ring_owners("tp"), w_key, w_value)
+    weights = order_weights(ring_owners("tp"), w_key, w_value)
+    near, weights, block_ids, slot_ids = lax.optimization_barrier(
+        (near, weights, block_map, passage_ids)
     )
-    weights = order_weights(owners, w_key, w_value)
-    shards = ring_gather(near[:half], near[half:], "tp")
+    wanted = wanted_passages(place, block_ids, slot_ids)
+    shards, asked, wanted = ring_gather(near[:half], near[half:], "tp", asked, wanted)
     answers = cross_attention(wanted, shards, weights, asked)
     arrived = lax.all_to_all(answers, "seq", split_axis=0, concat_axis=0, tiled=True)
     mixed = mix(place, block_map, arrived, self_out.reshape(groups, GROUP, feats))

time: 142 us -> 138 us (0.972)
  the two profiles are of different devices: /device:TPU:25 before, /device:TPU:1 now
where the time goes in v3:
time: 138 us; the launch traced here: 137 us
  starting transfers between devices  73.9 us (54%)
  waiting for transfers between devices  38.7 us (28%)
  Pallas kernels  18.4 us (13%)
  local copies, waits for them, and re-layouts  4.87 us (4%)
    all_to_all x1, waiting for transfers between devices, on_device(): lax.all_to_all(answers, 'seq', split_axis=0, concat_axis=0, tiled=True)  22.6 us
    ppermute x3, starting transfers between devices, ring_gather(): left_low = lax.ppermute(left_low, axis, down)  13.7 us
    ppermute x3, starting transfers between devices, ring_gather(): left_high = lax.ppermute(left_high, axis, down)  13 us
    ppermute x1, starting transfers between devices, on_device(): lax.ppermute(passages[0, 0], ('side', 'seq'), [(h * blocks + b, (1 - h) *...  11.5 us
    all_to_all x1, starting transfers between devices, on_device(): lax.all_to_all(answers, 'seq', split_axis=0, concat_axis=0, tiled=True)  11.3 us
    ppermute x1, waiting for transfers between devices, on_device(): lax.ppermute(passages[0, 0], ('side', 'seq'), [(h * blocks + b, (1 - h) *...  11 us
    pallas_call x1, Pallas kernels, cross_attention(): pl.pallas_call(functools.partial(cross_kernel, places=places), out_shape=...  8.18 us
    ppermute x3, starting transfers between devices, ring_gather(): right_low = lax.ppermute(right_low, axis, up)  7.05 us
  transfers between devices with their start and end apart: 17, of which 4 were waited for; matrix products, arithmetic and copies ran while one was open for 0% of the time, Pallas kernels for 6%

profile of v3, /device:TPU:1, one launch (start us, length us, event | category | flops | bytes accessed | tf_op | source)
XLA Modules:
  0.0 136.5 jit_solution(2200305659740564854)
XLA Ops:
  0.0 11.5 %collective-permute-start = (bf16[16,128,128]{2,1,0:T(8,128)(2,1)}, bf16[16,128,128]{2,1,0:T(8,128)(2,1)S(1)}, u32[]{:S(2)}, u32[]{:S(2)}) collective-permute-start(bf16[16,128,128]{2,1,0:T(8,128)(2,1)} %bitcast.22), channel_id=1, source_target_pairs={{0,384},{8,392},{16,400},{24,408},{32,416},{40,424},{48,432},{56,4... | collective-permute-start | bytes 1572872 | tf_op jit(solution)/shard_map/ppermute | solution.py:359
  11.6 1.0 copy-done.3
  12.6 0.8 copy-done.4
  13.4 2.2 %pack_queries.1 = bf16[32,64,256]{2,1,0:T(8,128)(2,1)} custom-call(s32[2]{0:T(128)S(1)} %pad_add_fusion.place, s32[2,32,32]{2,1,0:T(8,128)S(1)} %copy-done.4, bf16[16,64,256]{2,1,0:T(8,128)(2,1)S(1)} %bitcast.18), custom_call_target="tpu_custom_call" | custom-call | bytes 1572864 | tf_op jit(solution)/shard_map/pack_queries/pallas_call | solution.py:52
  15.6 6.5 %all-to-all-start = ((bf16[32,64,256]{2,1,0:T(8,128)(2,1)}), bf16[32,64,256]{2,1,0:T(8,128)(2,1)S(1)}, u32[]{:S(2)}, u32[]{:S(2)}) async-start(bf16[32,64,256]{2,1,0:T(8,128)(2,1)} %pack_queries.1), calls=%async_computation | async-start | bytes 2097152 | tf_op jit(solution)/shard_map/all_to_all | solution.py:367
  22.2 0.6 order_weights.1.refs_0_
  22.8 11.0 %collective-permute-done = bf16[16,128,128]{2,1,0:T(8,128)(2,1)S(1)} collective-permute-done((bf16[16,128,128]{2,1,0:T(8,128)(2,1)}, bf16[16,128,128]{2,1,0:T(8,128)(2,1)S(1)}, u32[]{:S(2)}, u32[]{:S(2)}) %collective-permute-start) | collective-permute-done | bytes 524320 | tf_op jit(solution)/shard_map/ppermute | solution.py:359
  33.8 3.2 %collective-permute-start.1 = (bf16[8,128,128]{2,1,0:T(8,128)(2,1)S(1)}, bf16[8,128,128]{2,1,0:T(8,128)(2,1)S(1)}, u32[]{:S(2)}, u32[]{:S(2)}) collective-permute-start(bf16[8,128,128]{2,1,0:T(8,128)(2,1)S(1)} %get-tuple-element.20.refs_2_), channel_id=1, source_target_pairs={{0,1},{1,2},{2,3},{3,4},{4,5},{5,6},{6,7},{7,0},{8,9},{9,10},{10,1... | collective-permute-start | bytes 786440 | tf_op jit(solution)/shard_map/ppermute | solution.py:328
  37.1 3.8 %collective-permute-start.6 = (bf16[8,128,128]{2,1,0:T(8,128)(2,1)S(1)}, bf16[8,128,128]{2,1,0:T(8,128)(2,1)S(1)}, u32[]{:S(2)}, u32[]{:S(2)}) collective-permute-start(bf16[8,128,128]{2,1,0:T(8,128)(2,1)S(1)} %get-tuple-element.19.refs_3_), channel_id=1, source_target_pairs={{0,7},{1,0},{2,1},{3,2},{4,3},{5,4},{6,5},{7,6},{8,15},{9,8},{10,9... | collective-permute-start | bytes 786440 | tf_op jit(solution)/shard_map/ppermute | solution.py:331
  40.9 1.9 %collective-permute-start.4 = (bf16[8,128,128]{2,1,0:T(8,128)(2,1)S(1)}, bf16[8,128,128]{2,1,0:T(8,128)(2,1)S(1)}, u32[]{:S(2)}, u32[]{:S(2)}) collective-permute-start(bf16[8,128,128]{2,1,0:T(8,128)(2,1)S(1)} %get-tuple-element.19.refs_3_), channel_id=1, source_target_pairs={{0,1},{1,2},{2,3},{3,4},{4,5},{5,6},{6,7},{7,0},{8,9},{9,10},{10,1... | collective-permute-start | bytes 786440 | tf_op jit(solution)/shard_map/ppermute | solution.py:330
  42.8 4.6 %collective-permute-start.5 = (bf16[8,128,128]{2,1,0:T(8,128)(2,1)S(1)}, bf16[8,128,128]{2,1,0:T(8,128)(2,1)S(1)}, u32[]{:S(2)}, u32[]{:S(2)}) collective-permute-start(bf16[8,128,128]{2,1,0:T(8,128)(2,1)S(1)} %get-tuple-element.20.refs_2_), channel_id=1, source_target_pairs={{0,7},{1,0},{2,1},{3,2},{4,3},{5,4},{6,5},{7,6},{8,15},{9,8},{10,9... | collective-permute-start | bytes 786440 | tf_op jit(solution)/shard_map/ppermute | solution.py:329
  47.4 1.9 %collective-permute-start.2 = (bf16[8,128,128]{2,1,0:T(8,128)(2,1)S(1)}, bf16[8,128,128]{2,1,0:T(8,128)(2,1)S(1)}, u32[]{:S(2)}, u32[]{:S(2)}) collective-permute-start(bf16[8,128,128]{2,1,0:T(8,128)(2,1)S(1)} %collective-permute-done.1.refs_4_), channel_id=1, source_target_pairs={{0,1},{1,2},{2,3},{3,4},{4,5},{5,6},{6,7},{7,0},{8,9},{9,10},{10,1... | collective-permute-start | bytes 786440 | tf_op jit(solution)/shard_map/ppermute | solution.py:328
  49.4 4.6 %collective-permute-start.9 = (bf16[8,128,128]{2,1,0:T(8,128)(2,1)S(1)}, bf16[8,128,128]{2,1,0:T(8,128)(2,1)S(1)}, u32[]{:S(2)}, u32[]{:S(2)}) collective-permute-start(bf16[8,128,128]{2,1,0:T(8,128)(2,1)S(1)} %collective-permute-done.6.refs_7_), channel_id=1, source_target_pairs={{0,7},{1,0},{2,1},{3,2},{4,3},{5,4},{6,5},{7,6},{8,15},{9,8},{10,9... | collective-permute-start | bytes 786440 | tf_op jit(solution)/shard_map/ppermute | solution.py:331
  54.0 1.9 %collective-permute-start.7 = (bf16[8,128,128]{2,1,0:T(8,128)(2,1)S(1)}, bf16[8,128,128]{2,1,0:T(8,128)(2,1)S(1)}, u32[]{:S(2)}, u32[]{:S(2)}) collective-permute-start(bf16[8,128,128]{2,1,0:T(8,128)(2,1)S(1)} %collective-permute-done.4.refs_5_), channel_id=1, source_target_pairs={{0,1},{1,2},{2,3},{3,4},{4,5},{5,6},{6,7},{7,0},{8,9},{9,10},{10,1... | collective-permute-start | bytes 786440 | tf_op jit(solution)/shard_map/ppermute | solution.py:330
  55.9 4.6 %collective-permute-start.8 = (bf16[8,128,128]{2,1,0:T(8,128)(2,1)S(1)}, bf16[8,128,128]{2,1,0:T(8,128)(2,1)}, u32[]{:S(2)}, u32[]{:S(2)}) collective-permute-start(bf16[8,128,128]{2,1,0:T(8,128)(2,1)S(1)} %collective-permute-done.5.refs_6_), channel_id=1, source_target_pairs={{0,7},{1,0},{2,1},{3,2},{4,3},{5,4},{6,5},{7,6},{8,15},{9,8},{10,9... | collective-permute-start | bytes 786440 | tf_op jit(solution)/shard_map/ppermute | solution.py:329
  60.5 1.9 %collective-permute-start.3 = (bf16[8,128,128]{2,1,0:T(8,128)(2,1)S(1)}, bf16[8,128,128]{2,1,0:T(8,128)(2,1)}, u32[]{:S(2)}, u32[]{:S(2)}) collective-permute-start(bf16[8,128,128]{2,1,0:T(8,128)(2,1)S(1)} %collective-permute-done.2.refs_8_), channel_id=1, source_target_pairs={{0,1},{1,2},{2,3},{3,4},{4,5},{5,6},{6,7},{7,0},{8,9},{9,10},{10,1... | collective-permute-start | bytes 786440 | tf_op jit(solution)/shard_map/ppermute | solution.py:328
  62.5 4.6 %collective-permute-start.12 = (bf16[8,128,128]{2,1,0:T(8,128)(2,1)S(1)}, bf16[8,128,128]{2,1,0:T(8,128)(2,1)}, u32[]{:S(2)}, u32[]{:S(2)}) collective-permute-start(bf16[8,128,128]{2,1,0:T(8,128)(2,1)S(1)} %collective-permute-done.9.refs_11_), channel_id=1, source_target_pairs={{0,7},{1,0},{2,1},{3,2},{4,3},{5,4},{6,5},{7,6},{8,15},{9,8},{10,9... | collective-permute-start | bytes 786440 | tf_op jit(solution)/shard_map/ppermute | solution.py:331
  67.1 0.7 wanted_passages.1.wanted
  67.8 0.5 copy-done.10
  68.3 1.9 %collective-permute-start.10 = (bf16[8,128,128]{2,1,0:T(8,128)(2,1)S(1)}, bf16[8,128,128]{2,1,0:T(8,128)(2,1)S(1)}, u32[]{:S(2)}, u32[]{:S(2)}) collective-permute-start(bf16[8,128,128]{2,1,0:T(8,128)(2,1)S(1)} %collective-permute-done.7.refs_9_), channel_id=1, source_target_pairs={{0,1},{1,2},{2,3},{3,4},{4,5},{5,6},{6,7},{7,0},{8,9},{9,10},{10,1... | collective-permute-start | bytes 786440 | tf_op jit(solution)/shard_map/ppermute | solution.py:330
  70.3 4.6 %collective-permute-start.11 = (bf16[8,128,128]{2,1,0:T(8,128)(2,1)}, bf16[8,128,128]{2,1,0:T(8,128)(2,1)S(1)}, u32[]{:S(2)}, u32[]{:S(2)}) collective-permute-start(bf16[8,128,128]{2,1,0:T(8,128)(2,1)} %collective-permute-done.8.refs_10_), channel_id=1, source_target_pairs={{0,7},{1,0},{2,1},{3,2},{4,3},{5,4},{6,5},{7,6},{8,15},{9,8},{10,9... | collective-permute-start | bytes 786440 | tf_op jit(solution)/shard_map/ppermute | solution.py:329
  74.9 1.9 %collective-permute-start.14 = (bf16[8,128,128]{2,1,0:T(8,128)(2,1)}, bf16[8,128,128]{2,1,0:T(8,128)(2,1)S(1)}, u32[]{:S(2)}, u32[]{:S(2)}) collective-permute-start(bf16[8,128,128]{2,1,0:T(8,128)(2,1)} %collective-permute-done.12.refs_15_), channel_id=1, source_target_pairs={{0,7},{1,0},{2,1},{3,2},{4,3},{5,4},{6,5},{7,6},{8,15},{9,8},{10,9... | collective-permute-start | bytes 786440 | tf_op jit(solution)/shard_map/ppermute | solution.py:335
  76.8 3.4 %collective-permute-start.13 = (bf16[8,128,128]{2,1,0:T(8,128)(2,1)}, bf16[8,128,128]{2,1,0:T(8,128)(2,1)S(1)}, u32[]{:S(2)}, u32[]{:S(2)}) collective-permute-start(bf16[8,128,128]{2,1,0:T(8,128)(2,1)} %collective-permute-done.3.refs_12_), channel_id=1, source_target_pairs={{0,1},{1,2},{2,3},{3,4},{4,5},{5,6},{6,7},{7,0},{8,9},{9,10},{10,1... | collective-permute-start | bytes 786440 | tf_op jit(solution)/shard_map/ppermute | solution.py:334
  80.2 5.1 %collective-permute-done.14.refs_17_ = bf16[8,128,128]{2,1,0:T(8,128)(2,1)S(1)} collective-permute-done((bf16[8,128,128]{2,1,0:T(8,128)(2,1)}, bf16[8,128,128]{2,1,0:T(8,128)(2,1)S(1)}, u32[]{:S(2)}, u32[]{:S(2)}) %collective-permute-start.14) | collective-permute-done | bytes 262176 | tf_op jit(solution)/shard_map/ppermute | solution.py:335
  85.4 0.6 copy-done.23
  86.0 0.7 copy-done.24
  86.7 8.2 %cross_attention.1 = bf16[32,136,128]{2,1,0:T(8,128)(2,1)} custom-call(s32[1,32]{1,0:T(1,128)} %copy-done.10, bf16[1024,512]{1,0:T(8,128)(2,1)} %copy-done, bf16[32,64,256]{2,1,0:T(8,128)(2,1)} %copy-done.11, bf16[8,128,128]{2,1,0:T(8,128)(2,1)} %copy-done.13, bf16[8,128,128]{2,1,0:T(8,128)(2,1)} %copy-done.12, bf16[8,128,128]{2,1,0:T(8,128)(2,1)} %copy-done.14, ...), custom_call_target="tpu_custom_call" | custom-call | flops 2684354560 | bytes 7340032 | tf_op jit(solution)/shard_map/cross_attention/pallas_call | solution.py:243
  94.9 11.3 %all-to-all-start.1 = ((bf16[32,136,128]{2,1,0:T(8,128)(2,1)}), bf16[32,136,128]{2,1,0:T(8,128)(2,1)S(1)}, u32[]{:S(2)}, u32[]{:S(2)}) async-start(bf16[32,136,128]{2,1,0:T(8,128)(2,1)} %cross_attention.1), calls=%async_computation.1 | async-start | bytes 2228224 | tf_op jit(solution)/shard_map/all_to_all | solution.py:377
  106.2 1.0 copy-done.8
  107.2 4.2 %self_attention.1 = f32[1024,256]{1,0:T(8,128)S(1)} custom-call(bf16[1024,256]{1,0:T(8,128)(2,1)S(1)} %bitcast.19, bf16[1024,256]{1,0:T(8,128)(2,1)S(1)} %bitcast.20, bf16[1024,256]{1,0:T(8,128)(2,1)S(1)} %bitcast.21), custom_call_target="tpu_custom_call" | custom-call | flops 805306368 | bytes 2621440 | tf_op jit(solution)/shard_map/self_attention/pallas_call | solution.py:96
  111.4 22.6 %all-to-all-done.1.arrived_ref = bf16[32,136,128]{2,1,0:T(8,128)(2,1)S(1)} async-done(((bf16[32,136,128]{2,1,0:T(8,128)(2,1)}), bf16[32,136,128]{2,1,0:T(8,128)(2,1)S(1)}, u32[]{:S(2)}, u32[]{:S(2)}) %all-to-all-start.1) | async-done | bytes 1114144 | tf_op jit(solution)/shard_map/all_to_all | solution.py:377
  134.0 2.5 %mix.1 = bf16[16,64,256]{2,1,0:T(8,128)(2,1)} custom-call(s32[2]{0:T(128)S(1)} %pad_add_fusion.place, s32[2,32,32]{2,1,0:T(8,128)S(1)} %copy-done.5, bf16[32,136,128]{2,1,0:T(8,128)(2,1)S(1)} %all-to-all-done.1.arrived_ref, f32[16,64,256]{2,1,0:T(8,128)S(1)} %bitcast.17), custom_call_target="tpu_custom_call" | custom-call | flops 2097152 | bytes 2621440 | tf_op jit(solution)/shard_map/mix/pallas_call | solution.py:305
  (62 shorter events, 0.4 us)
Async XLA Ops:
  0.0 33.8 %collective-permute-start = (bf16[16,128,128]{2,1,0:T(8,128)(2,1)}, bf16[16,128,128]{2,1,0:T(8,128)(2,1)S(1)}, u32[]{:S(2)}, u32[]{:S(2)}) collective-permute-start(bf16[16,128,128]{2,1,0:T(8,128)(2,1)} %bitcast.22), channel_id=1, source_target_pairs={{0,384},{8,392},{16,400},{24,408},{32,416},{40,424},{48,432},{56,4... | collective-permute-start | bytes 1572872 | tf_op jit(solution)/shard_map/ppermute | solution.py:359
  15.6 6.6 %copy-start.2 = (bf16[1024,256]{1,0:T(8,128)(2,1)S(1)}, bf16[1024,256]{1,0:T(8,128)(2,1)}, u32[]{:S(2)}) copy-start(bf16[1024,256]{1,0:T(8,128)(2,1)} %wvalue_ref.1) | copy-start | bytes 1572868
  15.6 61.2 %all-to-all-start = ((bf16[32,64,256]{2,1,0:T(8,128)(2,1)}), bf16[32,64,256]{2,1,0:T(8,128)(2,1)S(1)}, u32[]{:S(2)}, u32[]{:S(2)}) async-start(bf16[32,64,256]{2,1,0:T(8,128)(2,1)} %pack_queries.1), calls=%async_computation | async-start | bytes 2097152 | tf_op jit(solution)/shard_map/all_to_all | solution.py:367
  22.1 44.9 %copy-start.5 = (s32[2,32,32]{2,1,0:T(8,128)S(1)}, s32[2,32,32]{2,1,0:T(8,128)}, u32[]{:S(2)}) copy-start(s32[2,32,32]{2,1,0:T(8,128)} %block_map.3) | copy-start | bytes 24580
  22.1 44.9 %copy-start.9 = (s32[2,32,32]{2,1,0:T(8,128)S(1)}, s32[2,32,32]{2,1,0:T(8,128)}, u32[]{:S(2)}) copy-start(s32[2,32,32]{2,1,0:T(8,128)} %passage_ids_ref) | copy-start | bytes 24580
  22.8 45.0 %copy-start = (bf16[1024,512]{1,0:T(8,128)(2,1)}, bf16[1024,512]{1,0:T(8,128)(2,1)S(1)}, u32[]{:S(2)}) copy-start(bf16[1024,512]{1,0:T(8,128)(2,1)S(1)} %order_weights.1.refs_0_) | copy-start | bytes 3145732
  33.8 33.9 %copy-start.12 = (bf16[8,128,128]{2,1,0:T(8,128)(2,1)}, bf16[8,128,128]{2,1,0:T(8,128)(2,1)S(1)}, u32[]{:S(2)}) copy-start(bf16[8,128,128]{2,1,0:T(8,128)(2,1)S(1)} %get-tuple-element.19.refs_3_) | copy-start | bytes 786436
  33.8 33.9 %copy-start.13 = (bf16[8,128,128]{2,1,0:T(8,128)(2,1)}, bf16[8,128,128]{2,1,0:T(8,128)(2,1)S(1)}, u32[]{:S(2)}) copy-start(bf16[8,128,128]{2,1,0:T(8,128)(2,1)S(1)} %get-tuple-element.20.refs_2_) | copy-start | bytes 786436
  33.8 13.5 %collective-permute-start.1 = (bf16[8,128,128]{2,1,0:T(8,128)(2,1)S(1)}, bf16[8,128,128]{2,1,0:T(8,128)(2,1)S(1)}, u32[]{:S(2)}, u32[]{:S(2)}) collective-permute-start(bf16[8,128,128]{2,1,0:T(8,128)(2,1)S(1)} %get-tuple-element.20.refs_2_), channel_id=1, source_target_pairs={{0,1},{1,2},{2,3},{3,4},{4,5},{5,6},{6,7},{7,0},{8,9},{9,10},{10,1... | collective-permute-start | bytes 786440 | tf_op jit(solution)/shard_map/ppermute | solution.py:328
  37.1 12.3 %collective-permute-start.6 = (bf16[8,128,128]{2,1,0:T(8,128)(2,1)S(1)}, bf16[8,128,128]{2,1,0:T(8,128)(2,1)S(1)}, u32[]{:S(2)}, u32[]{:S(2)}) collective-permute-start(bf16[8,128,128]{2,1,0:T(8,128)(2,1)S(1)} %get-tuple-element.19.refs_3_), channel_id=1, source_target_pairs={{0,7},{1,0},{2,1},{3,2},{4,3},{5,4},{6,5},{7,6},{8,15},{9,8},{10,9... | collective-permute-start | bytes 786440 | tf_op jit(solution)/shard_map/ppermute | solution.py:331
  40.9 13.1 %collective-permute-start.4 = (bf16[8,128,128]{2,1,0:T(8,128)(2,1)S(1)}, bf16[8,128,128]{2,1,0:T(8,128)(2,1)S(1)}, u32[]{:S(2)}, u32[]{:S(2)}) collective-permute-start(bf16[8,128,128]{2,1,0:T(8,128)(2,1)S(1)} %get-tuple-element.19.refs_3_), channel_id=1, source_target_pairs={{0,1},{1,2},{2,3},{3,4},{4,5},{5,6},{6,7},{7,0},{8,9},{9,10},{10,1... | collective-permute-start | bytes 786440 | tf_op jit(solution)/shard_map/ppermute | solution.py:330
  42.8 13.1 %collective-permute-start.5 = (bf16[8,128,128]{2,1,0:T(8,128)(2,1)S(1)}, bf16[8,128,128]{2,1,0:T(8,128)(2,1)S(1)}, u32[]{:S(2)}, u32[]{:S(2)}) collective-permute-start(bf16[8,128,128]{2,1,0:T(8,128)(2,1)S(1)} %get-tuple-element.20.refs_2_), channel_id=1, source_target_pairs={{0,7},{1,0},{2,1},{3,2},{4,3},{5,4},{6,5},{7,6},{8,15},{9,8},{10,9... | collective-permute-start | bytes 786440 | tf_op jit(solution)/shard_map/ppermute | solution.py:329
  47.4 20.4 %copy-start.14 = (bf16[8,128,128]{2,1,0:T(8,128)(2,1)}, bf16[8,128,128]{2,1,0:T(8,128)(2,1)S(1)}, u32[]{:S(2)}) copy-start(bf16[8,128,128]{2,1,0:T(8,128)(2,1)S(1)} %collective-permute-done.1.refs_4_) | copy-start | bytes 786436
  47.4 13.1 %collective-permute-start.2 = (bf16[8,128,128]{2,1,0:T(8,128)(2,1)S(1)}, bf16[8,128,128]{2,1,0:T(8,128)(2,1)S(1)}, u32[]{:S(2)}, u32[]{:S(2)}) collective-permute-start(bf16[8,128,128]{2,1,0:T(8,128)(2,1)S(1)} %collective-permute-done.1.refs_4_), channel_id=1, source_target_pairs={{0,1},{1,2},{2,3},{3,4},{4,5},{5,6},{6,7},{7,0},{8,9},{9,10},{10,1... | collective-permute-start | bytes 786440 | tf_op jit(solution)/shard_map/ppermute | solution.py:328
  49.3 18.4 %copy-start.15 = (bf16[8,128,128]{2,1,0:T(8,128)(2,1)}, bf16[8,128,128]{2,1,0:T(8,128)(2,1)S(1)}, u32[]{:S(2)}) copy-start(bf16[8,128,128]{2,1,0:T(8,128)(2,1)S(1)} %collective-permute-done.6.refs_7_) | copy-start | bytes 786436
  49.4 13.1 %collective-permute-start.9 = (bf16[8,128,128]{2,1,0:T(8,128)(2,1)S(1)}, bf16[8,128,128]{2,1,0:T(8,128)(2,1)S(1)}, u32[]{:S(2)}, u32[]{:S(2)}) collective-permute-start(bf16[8,128,128]{2,1,0:T(8,128)(2,1)S(1)} %collective-permute-done.6.refs_7_), channel_id=1, source_target_pairs={{0,7},{1,0},{2,1},{3,2},{4,3},{5,4},{6,5},{7,6},{8,15},{9,8},{10,9... | collective-permute-start | bytes 786440 | tf_op jit(solution)/shard_map/ppermute | solution.py:331
  53.9 13.8 %copy-start.16 = (bf16[8,128,128]{2,1,0:T(8,128)(2,1)}, bf16[8,128,128]{2,1,0:T(8,128)(2,1)S(1)}, u32[]{:S(2)}) copy-start(bf16[8,128,128]{2,1,0:T(8,128)(2,1)S(1)} %collective-permute-done.4.refs_5_) | copy-start | bytes 786436
  54.0 14.4 %collective-permute-start.7 = (bf16[8,128,128]{2,1,0:T(8,128)(2,1)S(1)}, bf16[8,128,128]{2,1,0:T(8,128)(2,1)S(1)}, u32[]{:S(2)}, u32[]{:S(2)}) collective-permute-start(bf16[8,128,128]{2,1,0:T(8,128)(2,1)S(1)} %collective-permute-done.4.refs_5_), channel_id=1, source_target_pairs={{0,1},{1,2},{2,3},{3,4},{4,5},{5,6},{6,7},{7,0},{8,9},{9,10},{10,1... | collective-permute-start | bytes 786440 | tf_op jit(solution)/shard_map/ppermute | solution.py:330
  55.9 11.9 %copy-start.17 = (bf16[8,128,128]{2,1,0:T(8,128)(2,1)}, bf16[8,128,128]{2,1,0:T(8,128)(2,1)S(1)}, u32[]{:S(2)}) copy-start(bf16[8,128,128]{2,1,0:T(8,128)(2,1)S(1)} %collective-permute-done.5.refs_6_) | copy-start | bytes 786436
  55.9 14.4 %collective-permute-start.8 = (bf16[8,128,128]{2,1,0:T(8,128)(2,1)S(1)}, bf16[8,128,128]{2,1,0:T(8,128)(2,1)}, u32[]{:S(2)}, u32[]{:S(2)}) collective-permute-start(bf16[8,128,128]{2,1,0:T(8,128)(2,1)S(1)} %collective-permute-done.5.refs_6_), channel_id=1, source_target_pairs={{0,7},{1,0},{2,1},{3,2},{4,3},{5,4},{6,5},{7,6},{8,15},{9,8},{10,9... | collective-permute-start | bytes 786440 | tf_op jit(solution)/shard_map/ppermute | solution.py:329
  60.5 7.3 %copy-start.18 = (bf16[8,128,128]{2,1,0:T(8,128)(2,1)}, bf16[8,128,128]{2,1,0:T(8,128)(2,1)S(1)}, u32[]{:S(2)}) copy-start(bf16[8,128,128]{2,1,0:T(8,128)(2,1)S(1)} %collective-permute-done.2.refs_8_) | copy-start | bytes 786436
  60.5 16.3 %collective-permute-start.3 = (bf16[8,128,128]{2,1,0:T(8,128)(2,1)S(1)}, bf16[8,128,128]{2,1,0:T(8,128)(2,1)}, u32[]{:S(2)}, u32[]{:S(2)}) collective-permute-start(bf16[8,128,128]{2,1,0:T(8,128)(2,1)S(1)} %collective-permute-done.2.refs_8_), channel_id=1, source_target_pairs={{0,1},{1,2},{2,3},{3,4},{4,5},{5,6},{6,7},{7,0},{8,9},{9,10},{10,1... | collective-permute-start | bytes 786440 | tf_op jit(solution)/shard_map/ppermute | solution.py:328
  62.5 12.4 %collective-permute-start.12 = (bf16[8,128,128]{2,1,0:T(8,128)(2,1)S(1)}, bf16[8,128,128]{2,1,0:T(8,128)(2,1)}, u32[]{:S(2)}, u32[]{:S(2)}) collective-permute-start(bf16[8,128,128]{2,1,0:T(8,128)(2,1)S(1)} %collective-permute-done.9.refs_11_), channel_id=1, source_target_pairs={{0,7},{1,0},{2,1},{3,2},{4,3},{5,4},{6,5},{7,6},{8,15},{9,8},{10,9... | collective-permute-start | bytes 786440 | tf_op jit(solution)/shard_map/ppermute | solution.py:331
  68.3 17.0 %copy-start.20 = (bf16[8,128,128]{2,1,0:T(8,128)(2,1)}, bf16[8,128,128]{2,1,0:T(8,128)(2,1)S(1)}, u32[]{:S(2)}) copy-start(bf16[8,128,128]{2,1,0:T(8,128)(2,1)S(1)} %collective-permute-done.7.refs_9_) | copy-start | bytes 786436
  68.3 11.8 %collective-permute-start.10 = (bf16[8,128,128]{2,1,0:T(8,128)(2,1)S(1)}, bf16[8,128,128]{2,1,0:T(8,128)(2,1)S(1)}, u32[]{:S(2)}, u32[]{:S(2)}) collective-permute-start(bf16[8,128,128]{2,1,0:T(8,128)(2,1)S(1)} %collective-permute-done.7.refs_9_), channel_id=1, source_target_pairs={{0,1},{1,2},{2,3},{3,4},{4,5},{5,6},{6,7},{7,0},{8,9},{9,10},{10,1... | collective-permute-start | bytes 786440 | tf_op jit(solution)/shard_map/ppermute | solution.py:330
  70.3 9.9 %collective-permute-start.11 = (bf16[8,128,128]{2,1,0:T(8,128)(2,1)}, bf16[8,128,128]{2,1,0:T(8,128)(2,1)S(1)}, u32[]{:S(2)}, u32[]{:S(2)}) collective-permute-start(bf16[8,128,128]{2,1,0:T(8,128)(2,1)} %collective-permute-done.8.refs_10_), channel_id=1, source_target_pairs={{0,7},{1,0},{2,1},{3,2},{4,3},{5,4},{6,5},{7,6},{8,15},{9,8},{10,9... | collective-permute-start | bytes 786440 | tf_op jit(solution)/shard_map/ppermute | solution.py:329
  74.9 10.4 %collective-permute-start.14 = (bf16[8,128,128]{2,1,0:T(8,128)(2,1)}, bf16[8,128,128]{2,1,0:T(8,128)(2,1)S(1)}, u32[]{:S(2)}, u32[]{:S(2)}) collective-permute-start(bf16[8,128,128]{2,1,0:T(8,128)(2,1)} %collective-permute-done.12.refs_15_), channel_id=1, source_target_pairs={{0,7},{1,0},{2,1},{3,2},{4,3},{5,4},{6,5},{7,6},{8,15},{9,8},{10,9... | collective-permute-start | bytes 786440 | tf_op jit(solution)/shard_map/ppermute | solution.py:335
  76.8 8.6 %copy-start.11 = (bf16[32,64,256]{2,1,0:T(8,128)(2,1)}, bf16[32,64,256]{2,1,0:T(8,128)(2,1)S(1)}, u32[]{:S(2)}) copy-start(bf16[32,64,256]{2,1,0:T(8,128)(2,1)S(1)} %all-to-all-done.refs_1_) | copy-start | bytes 3145732
  76.8 8.5 %collective-permute-start.13 = (bf16[8,128,128]{2,1,0:T(8,128)(2,1)}, bf16[8,128,128]{2,1,0:T(8,128)(2,1)S(1)}, u32[]{:S(2)}, u32[]{:S(2)}) collective-permute-start(bf16[8,128,128]{2,1,0:T(8,128)(2,1)} %collective-permute-done.3.refs_12_), channel_id=1, source_target_pairs={{0,1},{1,2},{2,3},{3,4},{4,5},{5,6},{6,7},{7,0},{8,9},{9,10},{10,1... | collective-permute-start | bytes 786440 | tf_op jit(solution)/shard_map/ppermute | solution.py:334
  94.9 11.3 %copy-start.6 = (bf16[1,1,1024,256]{3,2,1,0:T(8,128)(2,1)S(1)}, bf16[1,1,1024,256]{3,2,1,0:T(8,128)(2,1)}, u32[]{:S(2)}) copy-start(bf16[1,1,1024,256]{3,2,1,0:T(8,128)(2,1)} %param.9) | copy-start | bytes 1572868
  94.9 11.3 %copy-start.7 = (bf16[1,1,1024,256]{3,2,1,0:T(8,128)(2,1)S(1)}, bf16[1,1,1024,256]{3,2,1,0:T(8,128)(2,1)}, u32[]{:S(2)}) copy-start(bf16[1,1,1024,256]{3,2,1,0:T(8,128)(2,1)} %param.10) | copy-start | bytes 1572868
  94.9 39.1 %all-to-all-start.1 = ((bf16[32,136,128]{2,1,0:T(8,128)(2,1)}), bf16[32,136,128]{2,1,0:T(8,128)(2,1)S(1)}, u32[]{:S(2)}, u32[]{:S(2)}) async-start(bf16[32,136,128]{2,1,0:T(8,128)(2,1)} %cross_attention.1), calls=%async_computation.1 | async-start | bytes 2228224 | tf_op jit(solution)/shard_map/all_to_all | solution.py:377
  (10 other events, 27.0 us)

commit v4 on v3

--- a/solution.py
+++ b/solution.py
@@ -12,10 +12,10 @@
 GROUP = 64
 NEIGH = 2
 EXTRA = 8
-WANTED_FLOPS = 13000000000
-LOAD_PARTS = 2
+WANTED_FLOPS = 16000000000
+LOAD_PARTS = 4
 STORE_PARTS = 4
-CROSS_VMEM_BYTES = 58 * 1024 * 1024
+CROSS_VMEM_BYTES = 52 * 1024 * 1024
 VMEM_BYTES = 20 * 1024 * 1024
 EXP2_SCALE = math.log2(math.e) / math.sqrt(HD)
 
@@ -152,40 +152,25 @@
 
 
 def cross_kernel(wanted, *refs, places):
-    shards, depth = len(places), max(row for row, _ in places) + 1
-    weight_hbm, query_ref, shard_hbm, out_hbm = refs[0], refs[1], refs[2 : 2 + shards], refs[2 + shards]
-    weight_ref, lhs_ref, kv_ref, out_ref, load_sems, lhs_sems, out_sems = refs[3 + shards :]
+    shards = len(places)
+    weight_ref, query_ref, shard_refs, out_hbm = refs[0], refs[1], refs[2 : 2 + shards], refs[2 + shards]
+    kv_ref, out_ref, out_sems = refs[3 + shards :]
     chunks, rows, feats = query_ref.shape
     heads = feats // HD
-    _, pool, rlen, part = lhs_ref.shape
+    pool, rlen, _ = kv_ref.shape
+    part = shard_refs[0].shape[2]
     per = pool // LOAD_PARTS
 
-    load_weight = pltpu.make_async_copy(weight_hbm, weight_ref, load_sems.at[0])
-    load_lhs = [
-        [
-            pltpu.make_async_copy(
-                shard_hbm[n].at[pl.ds(k * per - low, per)],
-                lhs_ref.at[row, pl.ds(k * per, per)],
-                lhs_sems.at[k, row],
-            )
-            for n, (row, low) in enumerate(places)
-            if low <= k * per < low + shard_hbm[n].shape[0]
+    for k in range(LOAD_PARTS):
+        pieces = [
+            shard_refs[n][k * per - low : (k + 1) * per - low].reshape(per * rlen, part)
+            for n, (_, low) in enumerate(places)
+            if low <= k * per < low + shard_refs[n].shape[0]
         ]
-        for k in range(LOAD_PARTS)
-    ]
-    load_weight.start()
-    for copy in load_lhs[0]:
-        copy.start()
-    load_weight.wait()
-    for k, copies in enumerate(load_lhs):
-        for copy in copies:
-            copy.wait()
-        for copy in load_lhs[k + 1] if k + 1 < LOAD_PARTS else []:
-            copy.start()
-        span = slice(k * per, (k + 1) * per)
-        lhs = jnp.concatenate([lhs_ref[n, span].reshape(per * rlen, part) for n in range(depth)], 1)
-        made = jnp.dot(lhs, weight_ref[...], preferred_element_type=jnp.float32)
-        kv_ref[span] = made.astype(jnp.bfloat16).reshape(per, rlen, 2 * feats)
+        made = jnp.dot(
+            jnp.concatenate(pieces, 1), weight_ref[...], preferred_element_type=jnp.float32
+        )
+        kv_ref[k * per : (k + 1) * per] = made.astype(jnp.bfloat16).reshape(per, rlen, 2 * feats)
 
     zeros = jnp.zeros((rows, HD), jnp.bfloat16)
     extra_row = lax.broadcasted_iota(jnp.int32, (EXTRA, heads * rows), 0)
@@ -243,15 +228,11 @@
     return pl.pallas_call(
         functools.partial(cross_kernel, places=places),
         out_shape=out_shape,
-        in_specs=[pl.BlockSpec(memory_space=pltpu.SMEM)] + [ANYWHERE, IN_VMEM] + [ANYWHERE] * len(shards),
+        in_specs=[pl.BlockSpec(memory_space=pltpu.SMEM)] + [IN_VMEM] * (2 + len(shards)),
         out_specs=ANYWHERE,
         scratch_shapes=[
-            pltpu.VMEM(weights.shape, jnp.bfloat16),
-            pltpu.VMEM((positions, pool, rlen, part), jnp.bfloat16),
             pltpu.VMEM((pool, rlen, 2 * feats), jnp.bfloat16),
             pltpu.VMEM(out_shape.shape, jnp.bfloat16),
-            pltpu.SemaphoreType.DMA((1,)),
-            pltpu.SemaphoreType.DMA((LOAD_PARTS, positions)),
             pltpu.SemaphoreType.DMA((STORE_PARTS,)),
         ],
         compiler_params=pltpu.CompilerParams(vmem_limit_bytes=CROSS_VMEM_BYTES),
@@ -368,10 +349,8 @@
     self_out = self_attention(self_query[0, 0], self_key[0, 0], self_value[0, 0])
 
     weights = order_weights(ring_owners("tp"), w_key, w_value)
-    near, weights, block_ids, slot_ids = lax.optimization_barrier(
-        (near, weights, block_map, passage_ids)
-    )
-    wanted = wanted_passages(place, block_ids, slot_ids)
+    wanted = wanted_passages(place, block_map, passage_ids)
+    near, weights, wanted = lax.optimization_barrier((near, weights, wanted))
     shards, asked, wanted = ring_gather(near[:half], near[half:], "tp", asked, wanted)
     answers = cross_attention(wanted, shards, weights, asked)
     arrived = lax.all_to_all(answers, "seq", split_axis=0, concat_axis=0, tiled=True)

time: 138 us -> 135 us (0.978)
  Pallas kernels: 18.4 us -> 17 us
    ppermute x3, starting transfers between devices: 13 us -> 10.8 us  [ring_gather(): left_high = lax.ppermute(left_high, axis, down)]
    ppermute x1, waiting for transfers between devices: 11 us -> 8.96 us  [on_device(): lax.ppermute(passages[0, 0], ('side', 'seq'), [(h * blocks + b, (1 - h) *...]
    all_to_all x1, starting transfers between devices: 11.3 us -> 12.7 us  [on_device(): lax.all_to_all(answers, 'seq', split_axis=0, concat_axis=0, tiled=True)]
    pallas_call x1, Pallas kernels: 8.18 us -> 6.79 us  [cross_attention(): pl.pallas_call(functools.partial(cross_kernel, places=places), out_shape=...]
    unnamed x50 -> x28, local copies, waits for them, and re-layouts: 4.75 us -> 4.95 us
  transfers between devices with their start and end apart: 17 -> 17, of which waited for: 4 -> 5; matrix products, arithmetic and copies ran while one was open for 0% -> 0% of each run, Pallas kernels for 6% -> 6%
where the time goes in v4:
time: 135 us; the launch traced here: 134 us
  starting transfers between devices  73 us (54%)
  waiting for transfers between devices  38.2 us (28%)
  Pallas kernels  17 us (13%)
  local copies, waits for them, and re-layouts  5.07 us (4%)
    all_to_all x1, waiting for transfers between devices, on_device(): lax.all_to_all(answers, 'seq', split_axis=0, concat_axis=0, tiled=True)  22.6 us
    ppermute x3, starting transfers between devices, ring_gather(): left_low = lax.ppermute(left_low, axis, down)  13.7 us
    all_to_all x1, starting transfers between devices, on_device(): lax.all_to_all(answers, 'seq', split_axis=0, concat_axis=0, tiled=True)  12.7 us
    ppermute x1, starting transfers between devices, on_device(): lax.ppermute(passages[0, 0], ('side', 'seq'), [(h * blocks + b, (1 - h) *...  11.5 us
    ppermute x3, starting transfers between devices, ring_gather(): left_high = lax.ppermute(left_high, axis, down)  10.8 us
    ppermute x1, waiting for transfers between devices, on_device(): lax.ppermute(passages[0, 0], ('side', 'seq'), [(h * blocks + b, (1 - h) *...  8.96 us
    ppermute x3, starting transfers between devices, ring_gather(): right_low = lax.ppermute(right_low, axis, up)  6.81 us
    pallas_call x1, Pallas kernels, cross_attention(): pl.pallas_call(functools.partial(cross_kernel, places=places), out_shape=...  6.79 us
  transfers between devices with their start and end apart: 17, of which 5 were waited for; matrix products, arithmetic and copies ran while one was open for 0% of the time, Pallas kernels for 6%

profile of v4, /device:TPU:1, one launch (start us, length us, event | category | flops | bytes accessed | tf_op | source)
XLA Modules:
  0.0 133.7 jit_solution(8854585100698241254)
XLA Ops:
  0.0 11.5 %collective-permute-start = (bf16[16,128,128]{2,1,0:T(8,128)(2,1)}, bf16[16,128,128]{2,1,0:T(8,128)(2,1)S(1)}, u32[]{:S(2)}, u32[]{:S(2)}) collective-permute-start(bf16[16,128,128]{2,1,0:T(8,128)(2,1)} %bitcast.22), channel_id=1, source_target_pairs={{0,384},{8,392},{16,400},{24,408},{32,416},{40,424},{48,432},{56,4... | collective-permute-start | bytes 1572872 | tf_op jit(solution)/shard_map/ppermute | solution.py:340
  11.6 1.0 copy-done.3
  12.6 0.8 copy-done.4
  13.4 2.2 %pack_queries.1 = bf16[32,64,256]{2,1,0:T(8,128)(2,1)} custom-call(s32[2]{0:T(128)S(1)} %pad_add_fusion.place, s32[2,32,32]{2,1,0:T(8,128)S(1)} %copy-done.4, bf16[16,64,256]{2,1,0:T(8,128)(2,1)S(1)} %bitcast.18), custom_call_target="tpu_custom_call" | custom-call | bytes 1572864 | tf_op jit(solution)/shard_map/pack_queries/pallas_call | solution.py:52
  15.5 6.5 %all-to-all-start = ((bf16[32,64,256]{2,1,0:T(8,128)(2,1)}), bf16[32,64,256]{2,1,0:T(8,128)(2,1)S(1)}, u32[]{:S(2)}, u32[]{:S(2)}) async-start(bf16[32,64,256]{2,1,0:T(8,128)(2,1)} %pack_queries.1), calls=%async_computation | async-start | bytes 2097152 | tf_op jit(solution)/shard_map/all_to_all | solution.py:348
  22.0 0.7 wanted_passages.1.wanted
  23.2 0.6 order_weights.1.refs_0_
  23.9 1.0 copy-done
  24.8 9.0 %collective-permute-done = bf16[16,128,128]{2,1,0:T(8,128)(2,1)S(1)} collective-permute-done((bf16[16,128,128]{2,1,0:T(8,128)(2,1)}, bf16[16,128,128]{2,1,0:T(8,128)(2,1)S(1)}, u32[]{:S(2)}, u32[]{:S(2)}) %collective-permute-start) | collective-permute-done | bytes 524320 | tf_op jit(solution)/shard_map/ppermute | solution.py:340
  33.8 5.1 %collective-permute-start.6 = (bf16[8,128,128]{2,1,0:T(8,128)(2,1)S(1)}, bf16[8,128,128]{2,1,0:T(8,128)(2,1)S(1)}, u32[]{:S(2)}, u32[]{:S(2)}) collective-permute-start(bf16[8,128,128]{2,1,0:T(8,128)(2,1)S(1)} %get-tuple-element.17.refs_3_), channel_id=1, source_target_pairs={{0,7},{1,0},{2,1},{3,2},{4,3},{5,4},{6,5},{7,6},{8,15},{9,8},{10,9... | collective-permute-start | bytes 786440 | tf_op jit(solution)/shard_map/ppermute | solution.py:312
  38.9 1.9 %collective-permute-start.1 = (bf16[8,128,128]{2,1,0:T(8,128)(2,1)S(1)}, bf16[8,128,128]{2,1,0:T(8,128)(2,1)S(1)}, u32[]{:S(2)}, u32[]{:S(2)}) collective-permute-start(bf16[8,128,128]{2,1,0:T(8,128)(2,1)S(1)} %get-tuple-element.18.refs_2_), channel_id=1, source_target_pairs={{0,1},{1,2},{2,3},{3,4},{4,5},{5,6},{6,7},{7,0},{8,9},{9,10},{10,1... | collective-permute-start | bytes 786440 | tf_op jit(solution)/shard_map/ppermute | solution.py:309
  40.9 1.9 %collective-permute-start.4 = (bf16[8,128,128]{2,1,0:T(8,128)(2,1)S(1)}, bf16[8,128,128]{2,1,0:T(8,128)(2,1)S(1)}, u32[]{:S(2)}, u32[]{:S(2)}) collective-permute-start(bf16[8,128,128]{2,1,0:T(8,128)(2,1)S(1)} %get-tuple-element.17.refs_3_), channel_id=1, source_target_pairs={{0,1},{1,2},{2,3},{3,4},{4,5},{5,6},{6,7},{7,0},{8,9},{9,10},{10,1... | collective-permute-start | bytes 786440 | tf_op jit(solution)/shard_map/ppermute | solution.py:311
  42.8 4.6 %collective-permute-start.5 = (bf16[8,128,128]{2,1,0:T(8,128)(2,1)S(1)}, bf16[8,128,128]{2,1,0:T(8,128)(2,1)S(1)}, u32[]{:S(2)}, u32[]{:S(2)}) collective-permute-start(bf16[8,128,128]{2,1,0:T(8,128)(2,1)S(1)} %get-tuple-element.18.refs_2_), channel_id=1, source_target_pairs={{0,7},{1,0},{2,1},{3,2},{4,3},{5,4},{6,5},{7,6},{8,15},{9,8},{10,9... | collective-permute-start | bytes 786440 | tf_op jit(solution)/shard_map/ppermute | solution.py:310
  47.4 3.4 %collective-permute-start.9 = (bf16[8,128,128]{2,1,0:T(8,128)(2,1)S(1)}, bf16[8,128,128]{2,1,0:T(8,128)(2,1)S(1)}, u32[]{:S(2)}, u32[]{:S(2)}) collective-permute-start(bf16[8,128,128]{2,1,0:T(8,128)(2,1)S(1)} %collective-permute-done.6.refs_7_), channel_id=1, source_target_pairs={{0,7},{1,0},{2,1},{3,2},{4,3},{5,4},{6,5},{7,6},{8,15},{9,8},{10,9... | collective-permute-start | bytes 786440 | tf_op jit(solution)/shard_map/ppermute | solution.py:312
  50.8 1.9 %collective-permute-start.2 = (bf16[8,128,128]{2,1,0:T(8,128)(2,1)S(1)}, bf16[8,128,128]{2,1,0:T(8,128)(2,1)S(1)}, u32[]{:S(2)}, u32[]{:S(2)}) collective-permute-start(bf16[8,128,128]{2,1,0:T(8,128)(2,1)S(1)} %collective-permute-done.1.refs_4_), channel_id=1, source_target_pairs={{0,1},{1,2},{2,3},{3,4},{4,5},{5,6},{6,7},{7,0},{8,9},{9,10},{10,1... | collective-permute-start | bytes 786440 | tf_op jit(solution)/shard_map/ppermute | solution.py:309
  52.7 1.1 collective-permute-done.4.refs_5_
  53.8 1.9 %collective-permute-start.7 = (bf16[8,128,128]{2,1,0:T(8,128)(2,1)S(1)}, bf16[8,128,128]{2,1,0:T(8,128)(2,1)S(1)}, u32[]{:S(2)}, u32[]{:S(2)}) collective-permute-start(bf16[8,128,128]{2,1,0:T(8,128)(2,1)S(1)} %collective-permute-done.4.refs_5_), channel_id=1, source_target_pairs={{0,1},{1,2},{2,3},{3,4},{4,5},{5,6},{6,7},{7,0},{8,9},{9,10},{10,1... | collective-permute-start | bytes 786440 | tf_op jit(solution)/shard_map/ppermute | solution.py:311
  55.7 4.6 %collective-permute-start.8 = (bf16[8,128,128]{2,1,0:T(8,128)(2,1)S(1)}, bf16[8,128,128]{2,1,0:T(8,128)(2,1)}, u32[]{:S(2)}, u32[]{:S(2)}) collective-permute-start(bf16[8,128,128]{2,1,0:T(8,128)(2,1)S(1)} %collective-permute-done.5.refs_6_), channel_id=1, source_target_pairs={{0,7},{1,0},{2,1},{3,2},{4,3},{5,4},{6,5},{7,6},{8,15},{9,8},{10,9... | collective-permute-start | bytes 786440 | tf_op jit(solution)/shard_map/ppermute | solution.py:310
  60.3 2.3 %collective-permute-start.12 = (bf16[8,128,128]{2,1,0:T(8,128)(2,1)S(1)}, bf16[8,128,128]{2,1,0:T(8,128)(2,1)}, u32[]{:S(2)}, u32[]{:S(2)}) collective-permute-start(bf16[8,128,128]{2,1,0:T(8,128)(2,1)S(1)} %collective-permute-done.9.refs_11_), channel_id=1, source_target_pairs={{0,7},{1,0},{2,1},{3,2},{4,3},{5,4},{6,5},{7,6},{8,15},{9,8},{10,9... | collective-permute-start | bytes 786440 | tf_op jit(solution)/shard_map/ppermute | solution.py:312
  62.6 3.0 %collective-permute-start.3 = (bf16[8,128,128]{2,1,0:T(8,128)(2,1)S(1)}, bf16[8,128,128]{2,1,0:T(8,128)(2,1)}, u32[]{:S(2)}, u32[]{:S(2)}) collective-permute-start(bf16[8,128,128]{2,1,0:T(8,128)(2,1)S(1)} %collective-permute-done.2.refs_8_), channel_id=1, source_target_pairs={{0,1},{1,2},{2,3},{3,4},{4,5},{5,6},{6,7},{7,0},{8,9},{9,10},{10,1... | collective-permute-start | bytes 786440 | tf_op jit(solution)/shard_map/ppermute | solution.py:309
  65.6 1.9 %collective-permute-start.10 = (bf16[8,128,128]{2,1,0:T(8,128)(2,1)S(1)}, bf16[8,128,128]{2,1,0:T(8,128)(2,1)}, u32[]{:S(2)}, u32[]{:S(2)}) collective-permute-start(bf16[8,128,128]{2,1,0:T(8,128)(2,1)S(1)} %collective-permute-done.7.refs_9_), channel_id=1, source_target_pairs={{0,1},{1,2},{2,3},{3,4},{4,5},{5,6},{6,7},{7,0},{8,9},{9,10},{10,1... | collective-permute-start | bytes 786440 | tf_op jit(solution)/shard_map/ppermute | solution.py:311
  67.6 4.6 %collective-permute-start.11 = (bf16[8,128,128]{2,1,0:T(8,128)(2,1)}, bf16[8,128,128]{2,1,0:T(8,128)(2,1)}, u32[]{:S(2)}, u32[]{:S(2)}) collective-permute-start(bf16[8,128,128]{2,1,0:T(8,128)(2,1)} %collective-permute-done.8.refs_10_), channel_id=1, source_target_pairs={{0,7},{1,0},{2,1},{3,2},{4,3},{5,4},{6,5},{7,6},{8,15},{9,8},{10,9... | collective-permute-start | bytes 786440 | tf_op jit(solution)/shard_map/ppermute | solution.py:310
  72.1 2.3 %collective-permute-start.14 = (bf16[8,128,128]{2,1,0:T(8,128)(2,1)}, bf16[8,128,128]{2,1,0:T(8,128)(2,1)}, u32[]{:S(2)}, u32[]{:S(2)}) collective-permute-start(bf16[8,128,128]{2,1,0:T(8,128)(2,1)} %collective-permute-done.12.refs_15_), channel_id=1, source_target_pairs={{0,7},{1,0},{2,1},{3,2},{4,3},{5,4},{6,5},{7,6},{8,15},{9,8},{10,9... | collective-permute-start | bytes 786440 | tf_op jit(solution)/shard_map/ppermute | solution.py:316
  74.5 3.0 %collective-permute-start.13 = (bf16[8,128,128]{2,1,0:T(8,128)(2,1)}, bf16[8,128,128]{2,1,0:T(8,128)(2,1)S(1)}, u32[]{:S(2)}, u32[]{:S(2)}) collective-permute-start(bf16[8,128,128]{2,1,0:T(8,128)(2,1)} %collective-permute-done.3.refs_12_), channel_id=1, source_target_pairs={{0,1},{1,2},{2,3},{3,4},{4,5},{5,6},{6,7},{7,0},{8,9},{9,10},{10,1... | collective-permute-start | bytes 786440 | tf_op jit(solution)/shard_map/ppermute | solution.py:315
  77.5 5.1 %collective-permute-done.14.refs_17_ = bf16[8,128,128]{2,1,0:T(8,128)(2,1)} collective-permute-done((bf16[8,128,128]{2,1,0:T(8,128)(2,1)}, bf16[8,128,128]{2,1,0:T(8,128)(2,1)}, u32[]{:S(2)}, u32[]{:S(2)}) %collective-permute-start.14) | collective-permute-done | bytes 262176 | tf_op jit(solution)/shard_map/ppermute | solution.py:316
  83.1 0.7 copy-done.13
  83.8 6.8 %cross_attention.1 = bf16[32,136,128]{2,1,0:T(8,128)(2,1)} custom-call(s32[1,32]{1,0:T(1,128)S(1)} %wanted_passages.1.wanted, bf16[1024,512]{1,0:T(8,128)(2,1)} %copy-done, bf16[32,64,256]{2,1,0:T(8,128)(2,1)} %copy-done.10, bf16[8,128,128]{2,1,0:T(8,128)(2,1)S(1)} %get-tuple-element.18.refs_2_, bf16[8,128,128]{2,1,0:T(8,128)(2,1)S(1)} %get-tuple-element.17.refs_3_, ...), custom_call_target="tpu_custom_call" | custom-call | flops 2684354560 | bytes 7340032 | tf_op jit(solution)/shard_map/cross_attention/pallas_call | solution.py:228
  90.6 12.7 %all-to-all-start.1 = ((bf16[32,136,128]{2,1,0:T(8,128)(2,1)}), bf16[32,136,128]{2,1,0:T(8,128)(2,1)S(1)}, u32[]{:S(2)}, u32[]{:S(2)}) async-start(bf16[32,136,128]{2,1,0:T(8,128)(2,1)} %cross_attention.1), calls=%async_computation.1 | async-start | bytes 2228224 | tf_op jit(solution)/shard_map/all_to_all | solution.py:356
  103.4 1.0 copy-done.8
  104.4 4.2 %self_attention.1 = f32[1024,256]{1,0:T(8,128)S(1)} custom-call(bf16[1024,256]{1,0:T(8,128)(2,1)S(1)} %bitcast.19, bf16[1024,256]{1,0:T(8,128)(2,1)S(1)} %bitcast.20, bf16[1024,256]{1,0:T(8,128)(2,1)S(1)} %bitcast.21), custom_call_target="tpu_custom_call" | custom-call | flops 805306368 | bytes 2621440 | tf_op jit(solution)/shard_map/self_attention/pallas_call | solution.py:96
  108.6 22.6 %all-to-all-done.1.arrived_ref = bf16[32,136,128]{2,1,0:T(8,128)(2,1)S(1)} async-done(((bf16[32,136,128]{2,1,0:T(8,128)(2,1)}), bf16[32,136,128]{2,1,0:T(8,128)(2,1)S(1)}, u32[]{:S(2)}, u32[]{:S(2)}) %all-to-all-start.1) | async-done | bytes 1114144 | tf_op jit(solution)/shard_map/all_to_all | solution.py:356
  131.2 2.5 %mix.1 = bf16[16,64,256]{2,1,0:T(8,128)(2,1)} custom-call(s32[2]{0:T(128)S(1)} %pad_add_fusion.place, s32[2,32,32]{2,1,0:T(8,128)S(1)} %copy-done.5, bf16[32,136,128]{2,1,0:T(8,128)(2,1)S(1)} %all-to-all-done.1.arrived_ref, f32[16,64,256]{2,1,0:T(8,128)S(1)} %bitcast.17), custom_call_target="tpu_custom_call" | custom-call | flops 2097152 | bytes 2621440 | tf_op jit(solution)/shard_map/mix/pallas_call | solution.py:286
  (40 shorter events, 1.2 us)
Async XLA Ops:
  0.0 33.8 %collective-permute-start = (bf16[16,128,128]{2,1,0:T(8,128)(2,1)}, bf16[16,128,128]{2,1,0:T(8,128)(2,1)S(1)}, u32[]{:S(2)}, u32[]{:S(2)}) collective-permute-start(bf16[16,128,128]{2,1,0:T(8,128)(2,1)} %bitcast.22), channel_id=1, source_target_pairs={{0,384},{8,392},{16,400},{24,408},{32,416},{40,424},{48,432},{56,4... | collective-permute-start | bytes 1572872 | tf_op jit(solution)/shard_map/ppermute | solution.py:340
  11.6 1.0 copy-start.3
  12.6 0.8 copy-start.4
  15.5 6.5 %copy-start.5 = (s32[2,32,32]{2,1,0:T(8,128)S(1)}, s32[2,32,32]{2,1,0:T(8,128)}, u32[]{:S(2)}) copy-start(s32[2,32,32]{2,1,0:T(8,128)} %block_map.3) | copy-start | bytes 24580
  15.5 6.5 %copy-start.9 = (s32[2,32,32]{2,1,0:T(8,128)S(1)}, s32[2,32,32]{2,1,0:T(8,128)}, u32[]{:S(2)}) copy-start(s32[2,32,32]{2,1,0:T(8,128)} %passage_ids_ref.1) | copy-start | bytes 24580
  15.5 58.9 %all-to-all-start = ((bf16[32,64,256]{2,1,0:T(8,128)(2,1)}), bf16[32,64,256]{2,1,0:T(8,128)(2,1)S(1)}, u32[]{:S(2)}, u32[]{:S(2)}) async-start(bf16[32,64,256]{2,1,0:T(8,128)(2,1)} %pack_queries.1), calls=%async_computation | async-start | bytes 2097152 | tf_op jit(solution)/shard_map/all_to_all | solution.py:348
  22.0 1.0 copy-start.1
  22.0 1.2 copy-start.2
  23.8 1.0 copy-start
  33.8 13.5 %collective-permute-start.6 = (bf16[8,128,128]{2,1,0:T(8,128)(2,1)S(1)}, bf16[8,128,128]{2,1,0:T(8,128)(2,1)S(1)}, u32[]{:S(2)}, u32[]{:S(2)}) collective-permute-start(bf16[8,128,128]{2,1,0:T(8,128)(2,1)S(1)} %get-tuple-element.17.refs_3_), channel_id=1, source_target_pairs={{0,7},{1,0},{2,1},{3,2},{4,3},{5,4},{6,5},{7,6},{8,15},{9,8},{10,9... | collective-permute-start | bytes 786440 | tf_op jit(solution)/shard_map/ppermute | solution.py:312
  38.9 11.8 %collective-permute-start.1 = (bf16[8,128,128]{2,1,0:T(8,128)(2,1)S(1)}, bf16[8,128,128]{2,1,0:T(8,128)(2,1)S(1)}, u32[]{:S(2)}, u32[]{:S(2)}) collective-permute-start(bf16[8,128,128]{2,1,0:T(8,128)(2,1)S(1)} %get-tuple-element.18.refs_2_), channel_id=1, source_target_pairs={{0,1},{1,2},{2,3},{3,4},{4,5},{5,6},{6,7},{7,0},{8,9},{9,10},{10,1... | collective-permute-start | bytes 786440 | tf_op jit(solution)/shard_map/ppermute | solution.py:309
  40.9 12.9 %collective-permute-start.4 = (bf16[8,128,128]{2,1,0:T(8,128)(2,1)S(1)}, bf16[8,128,128]{2,1,0:T(8,128)(2,1)S(1)}, u32[]{:S(2)}, u32[]{:S(2)}) collective-permute-start(bf16[8,128,128]{2,1,0:T(8,128)(2,1)S(1)} %get-tuple-element.17.refs_3_), channel_id=1, source_target_pairs={{0,1},{1,2},{2,3},{3,4},{4,5},{5,6},{6,7},{7,0},{8,9},{9,10},{10,1... | collective-permute-start | bytes 786440 | tf_op jit(solution)/shard_map/ppermute | solution.py:311
  42.8 12.9 %collective-permute-start.5 = (bf16[8,128,128]{2,1,0:T(8,128)(2,1)S(1)}, bf16[8,128,128]{2,1,0:T(8,128)(2,1)S(1)}, u32[]{:S(2)}, u32[]{:S(2)}) collective-permute-start(bf16[8,128,128]{2,1,0:T(8,128)(2,1)S(1)} %get-tuple-element.18.refs_2_), channel_id=1, source_target_pairs={{0,7},{1,0},{2,1},{3,2},{4,3},{5,4},{6,5},{7,6},{8,15},{9,8},{10,9... | collective-permute-start | bytes 786440 | tf_op jit(solution)/shard_map/ppermute | solution.py:310
  47.4 12.9 %collective-permute-start.9 = (bf16[8,128,128]{2,1,0:T(8,128)(2,1)S(1)}, bf16[8,128,128]{2,1,0:T(8,128)(2,1)S(1)}, u32[]{:S(2)}, u32[]{:S(2)}) collective-permute-start(bf16[8,128,128]{2,1,0:T(8,128)(2,1)S(1)} %collective-permute-done.6.refs_7_), channel_id=1, source_target_pairs={{0,7},{1,0},{2,1},{3,2},{4,3},{5,4},{6,5},{7,6},{8,15},{9,8},{10,9... | collective-permute-start | bytes 786440 | tf_op jit(solution)/shard_map/ppermute | solution.py:312
  50.8 11.9 %collective-permute-start.2 = (bf16[8,128,128]{2,1,0:T(8,128)(2,1)S(1)}, bf16[8,128,128]{2,1,0:T(8,128)(2,1)S(1)}, u32[]{:S(2)}, u32[]{:S(2)}) collective-permute-start(bf16[8,128,128]{2,1,0:T(8,128)(2,1)S(1)} %collective-permute-done.1.refs_4_), channel_id=1, source_target_pairs={{0,1},{1,2},{2,3},{3,4},{4,5},{5,6},{6,7},{7,0},{8,9},{9,10},{10,1... | collective-permute-start | bytes 786440 | tf_op jit(solution)/shard_map/ppermute | solution.py:309
  53.8 11.8 %collective-permute-start.7 = (bf16[8,128,128]{2,1,0:T(8,128)(2,1)S(1)}, bf16[8,128,128]{2,1,0:T(8,128)(2,1)S(1)}, u32[]{:S(2)}, u32[]{:S(2)}) collective-permute-start(bf16[8,128,128]{2,1,0:T(8,128)(2,1)S(1)} %collective-permute-done.4.refs_5_), channel_id=1, source_target_pairs={{0,1},{1,2},{2,3},{3,4},{4,5},{5,6},{6,7},{7,0},{8,9},{9,10},{10,1... | collective-permute-start | bytes 786440 | tf_op jit(solution)/shard_map/ppermute | solution.py:311
  55.7 11.9 %collective-permute-start.8 = (bf16[8,128,128]{2,1,0:T(8,128)(2,1)S(1)}, bf16[8,128,128]{2,1,0:T(8,128)(2,1)}, u32[]{:S(2)}, u32[]{:S(2)}) collective-permute-start(bf16[8,128,128]{2,1,0:T(8,128)(2,1)S(1)} %collective-permute-done.5.refs_6_), channel_id=1, source_target_pairs={{0,7},{1,0},{2,1},{3,2},{4,3},{5,4},{6,5},{7,6},{8,15},{9,8},{10,9... | collective-permute-start | bytes 786440 | tf_op jit(solution)/shard_map/ppermute | solution.py:310
  60.3 22.8 %copy-start.11 = (bf16[8,128,128]{2,1,0:T(8,128)(2,1)}, bf16[8,128,128]{2,1,0:T(8,128)(2,1)S(1)}, u32[]{:S(2)}) copy-start(bf16[8,128,128]{2,1,0:T(8,128)(2,1)S(1)} %collective-permute-done.9.refs_11_) | copy-start | bytes 786436
  60.3 11.9 %collective-permute-start.12 = (bf16[8,128,128]{2,1,0:T(8,128)(2,1)S(1)}, bf16[8,128,128]{2,1,0:T(8,128)(2,1)}, u32[]{:S(2)}, u32[]{:S(2)}) collective-permute-start(bf16[8,128,128]{2,1,0:T(8,128)(2,1)S(1)} %collective-permute-done.9.refs_11_), channel_id=1, source_target_pairs={{0,7},{1,0},{2,1},{3,2},{4,3},{5,4},{6,5},{7,6},{8,15},{9,8},{10,9... | collective-permute-start | bytes 786440 | tf_op jit(solution)/shard_map/ppermute | solution.py:312
  62.6 11.9 %collective-permute-start.3 = (bf16[8,128,128]{2,1,0:T(8,128)(2,1)S(1)}, bf16[8,128,128]{2,1,0:T(8,128)(2,1)}, u32[]{:S(2)}, u32[]{:S(2)}) collective-permute-start(bf16[8,128,128]{2,1,0:T(8,128)(2,1)S(1)} %collective-permute-done.2.refs_8_), channel_id=1, source_target_pairs={{0,1},{1,2},{2,3},{3,4},{4,5},{5,6},{6,7},{7,0},{8,9},{9,10},{10,1... | collective-permute-start | bytes 786440 | tf_op jit(solution)/shard_map/ppermute | solution.py:309
  65.6 17.4 %copy-start.12 = (bf16[8,128,128]{2,1,0:T(8,128)(2,1)}, bf16[8,128,128]{2,1,0:T(8,128)(2,1)S(1)}, u32[]{:S(2)}) copy-start(bf16[8,128,128]{2,1,0:T(8,128)(2,1)S(1)} %collective-permute-done.7.refs_9_) | copy-start | bytes 786436
  65.6 11.9 %collective-permute-start.10 = (bf16[8,128,128]{2,1,0:T(8,128)(2,1)S(1)}, bf16[8,128,128]{2,1,0:T(8,128)(2,1)}, u32[]{:S(2)}, u32[]{:S(2)}) collective-permute-start(bf16[8,128,128]{2,1,0:T(8,128)(2,1)S(1)} %collective-permute-done.7.refs_9_), channel_id=1, source_target_pairs={{0,1},{1,2},{2,3},{3,4},{4,5},{5,6},{6,7},{7,0},{8,9},{9,10},{10,1... | collective-permute-start | bytes 786440 | tf_op jit(solution)/shard_map/ppermute | solution.py:311
  67.6 9.9 %collective-permute-start.11 = (bf16[8,128,128]{2,1,0:T(8,128)(2,1)}, bf16[8,128,128]{2,1,0:T(8,128)(2,1)}, u32[]{:S(2)}, u32[]{:S(2)}) collective-permute-start(bf16[8,128,128]{2,1,0:T(8,128)(2,1)} %collective-permute-done.8.refs_10_), channel_id=1, source_target_pairs={{0,7},{1,0},{2,1},{3,2},{4,3},{5,4},{6,5},{7,6},{8,15},{9,8},{10,9... | collective-permute-start | bytes 786440 | tf_op jit(solution)/shard_map/ppermute | solution.py:310
  72.1 10.4 %collective-permute-start.14 = (bf16[8,128,128]{2,1,0:T(8,128)(2,1)}, bf16[8,128,128]{2,1,0:T(8,128)(2,1)}, u32[]{:S(2)}, u32[]{:S(2)}) collective-permute-start(bf16[8,128,128]{2,1,0:T(8,128)(2,1)} %collective-permute-done.12.refs_15_), channel_id=1, source_target_pairs={{0,7},{1,0},{2,1},{3,2},{4,3},{5,4},{6,5},{7,6},{8,15},{9,8},{10,9... | collective-permute-start | bytes 786440 | tf_op jit(solution)/shard_map/ppermute | solution.py:316
  74.5 8.6 %copy-start.10 = (bf16[32,64,256]{2,1,0:T(8,128)(2,1)}, bf16[32,64,256]{2,1,0:T(8,128)(2,1)S(1)}, u32[]{:S(2)}) copy-start(bf16[32,64,256]{2,1,0:T(8,128)(2,1)S(1)} %all-to-all-done.refs_1_) | copy-start | bytes 3145732
  74.5 8.5 %collective-permute-start.13 = (bf16[8,128,128]{2,1,0:T(8,128)(2,1)}, bf16[8,128,128]{2,1,0:T(8,128)(2,1)S(1)}, u32[]{:S(2)}, u32[]{:S(2)}) collective-permute-start(bf16[8,128,128]{2,1,0:T(8,128)(2,1)} %collective-permute-done.3.refs_12_), channel_id=1, source_target_pairs={{0,1},{1,2},{2,3},{3,4},{4,5},{5,6},{6,7},{7,0},{8,9},{9,10},{10,1... | collective-permute-start | bytes 786440 | tf_op jit(solution)/shard_map/ppermute | solution.py:315
  83.1 0.7 copy-start.13
  90.6 12.8 %copy-start.6 = (bf16[1,1,1024,256]{3,2,1,0:T(8,128)(2,1)S(1)}, bf16[1,1,1024,256]{3,2,1,0:T(8,128)(2,1)}, u32[]{:S(2)}) copy-start(bf16[1,1,1024,256]{3,2,1,0:T(8,128)(2,1)} %param.9) | copy-start | bytes 1572868
  90.6 12.8 %copy-start.7 = (bf16[1,1,1024,256]{3,2,1,0:T(8,128)(2,1)S(1)}, bf16[1,1,1024,256]{3,2,1,0:T(8,128)(2,1)}, u32[]{:S(2)}) copy-start(bf16[1,1,1024,256]{3,2,1,0:T(8,128)(2,1)} %param.10) | copy-start | bytes 1572868
  90.6 40.6 %all-to-all-start.1 = ((bf16[32,136,128]{2,1,0:T(8,128)(2,1)}), bf16[32,136,128]{2,1,0:T(8,128)(2,1)S(1)}, u32[]{:S(2)}, u32[]{:S(2)}) async-start(bf16[32,136,128]{2,1,0:T(8,128)(2,1)} %cross_attention.1), calls=%async_computation.1 | async-start | bytes 2228224 | tf_op jit(solution)/shard_map/all_to_all | solution.py:356
  103.4 1.0 copy-start.8

commit v5 on v4

--- a/solution.py
+++ b/solution.py
@@ -13,9 +13,9 @@
 NEIGH = 2
 EXTRA = 8
 WANTED_FLOPS = 16000000000
-LOAD_PARTS = 4
+LOAD_PARTS = 2
 STORE_PARTS = 4
-CROSS_VMEM_BYTES = 52 * 1024 * 1024
+CROSS_VMEM_BYTES = 48 * 1024 * 1024
 VMEM_BYTES = 20 * 1024 * 1024
 EXP2_SCALE = math.log2(math.e) / math.sqrt(HD)
 

time: 135 us -> 133 us (0.985)
  local copies, waits for them, and re-layouts: 5.07 us -> 3.4 us
    unnamed x28 -> x18, local copies, waits for them, and re-layouts: 4.95 us -> 3.28 us
where the time goes in v5:
time: 133 us; the launch traced here: 132 us
  starting transfers between devices  73.1 us (55%)
  waiting for transfers between devices  39.1 us (29%)
  Pallas kernels  16.5 us (12%)
  local copies, waits for them, and re-layouts  3.4 us (3%)
    all_to_all x1, waiting for transfers between devices, on_device(): lax.all_to_all(answers, 'seq', split_axis=0, concat_axis=0, tiled=True)  22.6 us
    ppermute x3, starting transfers between devices, ring_gather(): left_low = lax.ppermute(left_low, axis, down)  13.7 us
    all_to_all x1, starting transfers between devices, on_device(): lax.all_to_all(answers, 'seq', split_axis=0, concat_axis=0, tiled=True)  12.8 us
    ppermute x1, starting transfers between devices, on_device(): lax.ppermute(passages[0, 0], ('side', 'seq'), [(h * blocks + b, (1 - h) *...  11.5 us
    ppermute x3, starting transfers between devices, ring_gather(): left_high = lax.ppermute(left_high, axis, down)  10.7 us
    ppermute x1, waiting for transfers between devices, on_device(): lax.ppermute(passages[0, 0], ('side', 'seq'), [(h * blocks + b, (1 - h) *...  9.84 us
    ppermute x3, starting transfers between devices, ring_gather(): right_low = lax.ppermute(right_low, axis, up)  6.91 us
    all_to_all x1, starting transfers between devices, on_device(): lax.all_to_all(chunks, 'seq', split_axis=0, concat_axis=0, tiled=True)  6.51 us
  transfers between devices with their start and end apart: 17, of which 5 were waited for; matrix products, arithmetic and copies ran while one was open for 0% of the time, Pallas kernels for 6%

profile of v5, /device:TPU:1, one launch (start us, length us, event | category | flops | bytes accessed | tf_op | source)
XLA Modules:
  0.0 132.4 jit_solution(10742915743635424286)
XLA Ops:
  0.0 11.5 %collective-permute-start = (bf16[16,128,128]{2,1,0:T(8,128)(2,1)}, bf16[16,128,128]{2,1,0:T(8,128)(2,1)S(1)}, u32[]{:S(2)}, u32[]{:S(2)}) collective-permute-start(bf16[16,128,128]{2,1,0:T(8,128)(2,1)} %bitcast.22), channel_id=1, source_target_pairs={{0,384},{8,392},{16,400},{24,408},{32,416},{40,424},{48,432},{56,4... | collective-permute-start | bytes 1572872 | tf_op jit(solution)/shard_map/ppermute | solution.py:340
  11.6 1.0 copy-done.2
  12.6 0.8 copy-done.3
  13.4 2.2 %pack_queries.1 = bf16[32,64,256]{2,1,0:T(8,128)(2,1)} custom-call(s32[2]{0:T(128)S(1)} %pad_add_fusion.place, s32[2,32,32]{2,1,0:T(8,128)S(1)} %copy-done.3, bf16[16,64,256]{2,1,0:T(8,128)(2,1)S(1)} %bitcast.18), custom_call_target="tpu_custom_call" | custom-call | bytes 1572864 | tf_op jit(solution)/shard_map/pack_queries/pallas_call | solution.py:52
  15.6 6.5 %all-to-all-start = ((bf16[32,64,256]{2,1,0:T(8,128)(2,1)}), bf16[32,64,256]{2,1,0:T(8,128)(2,1)}, u32[]{:S(2)}, u32[]{:S(2)}) async-start(bf16[32,64,256]{2,1,0:T(8,128)(2,1)} %pack_queries.1), calls=%async_computation | async-start | bytes 2097152 | tf_op jit(solution)/shard_map/all_to_all | solution.py:348
  22.1 0.7 wanted_passages.1.wanted
  22.9 0.3 copy-done
  23.3 0.6 order_weights.1.refs_0_
  23.9 9.8 %collective-permute-done = bf16[16,128,128]{2,1,0:T(8,128)(2,1)S(1)} collective-permute-done((bf16[16,128,128]{2,1,0:T(8,128)(2,1)}, bf16[16,128,128]{2,1,0:T(8,128)(2,1)S(1)}, u32[]{:S(2)}, u32[]{:S(2)}) %collective-permute-start) | collective-permute-done | bytes 524320 | tf_op jit(solution)/shard_map/ppermute | solution.py:340
  33.8 5.1 %collective-permute-start.6 = (bf16[8,128,128]{2,1,0:T(8,128)(2,1)S(1)}, bf16[8,128,128]{2,1,0:T(8,128)(2,1)S(1)}, u32[]{:S(2)}, u32[]{:S(2)}) collective-permute-start(bf16[8,128,128]{2,1,0:T(8,128)(2,1)S(1)} %get-tuple-element.17.refs_3_), channel_id=1, source_target_pairs={{0,7},{1,0},{2,1},{3,2},{4,3},{5,4},{6,5},{7,6},{8,15},{9,8},{10,9... | collective-permute-start | bytes 786440 | tf_op jit(solution)/shard_map/ppermute | solution.py:312
  38.9 1.9 %collective-permute-start.1 = (bf16[8,128,128]{2,1,0:T(8,128)(2,1)S(1)}, bf16[8,128,128]{2,1,0:T(8,128)(2,1)S(1)}, u32[]{:S(2)}, u32[]{:S(2)}) collective-permute-start(bf16[8,128,128]{2,1,0:T(8,128)(2,1)S(1)} %get-tuple-element.18.refs_2_), channel_id=1, source_target_pairs={{0,1},{1,2},{2,3},{3,4},{4,5},{5,6},{6,7},{7,0},{8,9},{9,10},{10,1... | collective-permute-start | bytes 786440 | tf_op jit(solution)/shard_map/ppermute | solution.py:309
  40.9 1.9 %collective-permute-start.4 = (bf16[8,128,128]{2,1,0:T(8,128)(2,1)S(1)}, bf16[8,128,128]{2,1,0:T(8,128)(2,1)S(1)}, u32[]{:S(2)}, u32[]{:S(2)}) collective-permute-start(bf16[8,128,128]{2,1,0:T(8,128)(2,1)S(1)} %get-tuple-element.17.refs_3_), channel_id=1, source_target_pairs={{0,1},{1,2},{2,3},{3,4},{4,5},{5,6},{6,7},{7,0},{8,9},{9,10},{10,1... | collective-permute-start | bytes 786440 | tf_op jit(solution)/shard_map/ppermute | solution.py:311
  42.8 4.6 %collective-permute-start.5 = (bf16[8,128,128]{2,1,0:T(8,128)(2,1)S(1)}, bf16[8,128,128]{2,1,0:T(8,128)(2,1)S(1)}, u32[]{:S(2)}, u32[]{:S(2)}) collective-permute-start(bf16[8,128,128]{2,1,0:T(8,128)(2,1)S(1)} %get-tuple-element.18.refs_2_), channel_id=1, source_target_pairs={{0,7},{1,0},{2,1},{3,2},{4,3},{5,4},{6,5},{7,6},{8,15},{9,8},{10,9... | collective-permute-start | bytes 786440 | tf_op jit(solution)/shard_map/ppermute | solution.py:310
  47.4 3.4 %collective-permute-start.9 = (bf16[8,128,128]{2,1,0:T(8,128)(2,1)S(1)}, bf16[8,128,128]{2,1,0:T(8,128)(2,1)S(1)}, u32[]{:S(2)}, u32[]{:S(2)}) collective-permute-start(bf16[8,128,128]{2,1,0:T(8,128)(2,1)S(1)} %collective-permute-done.6.refs_7_), channel_id=1, source_target_pairs={{0,7},{1,0},{2,1},{3,2},{4,3},{5,4},{6,5},{7,6},{8,15},{9,8},{10,9... | collective-permute-start | bytes 786440 | tf_op jit(solution)/shard_map/ppermute | solution.py:312
  50.8 1.9 %collective-permute-start.2 = (bf16[8,128,128]{2,1,0:T(8,128)(2,1)S(1)}, bf16[8,128,128]{2,1,0:T(8,128)(2,1)S(1)}, u32[]{:S(2)}, u32[]{:S(2)}) collective-permute-start(bf16[8,128,128]{2,1,0:T(8,128)(2,1)S(1)} %collective-permute-done.1.refs_4_), channel_id=1, source_target_pairs={{0,1},{1,2},{2,3},{3,4},{4,5},{5,6},{6,7},{7,0},{8,9},{9,10},{10,1... | collective-permute-start | bytes 786440 | tf_op jit(solution)/shard_map/ppermute | solution.py:309
  52.7 1.2 collective-permute-done.4.refs_5_
  53.9 1.9 %collective-permute-start.7 = (bf16[8,128,128]{2,1,0:T(8,128)(2,1)S(1)}, bf16[8,128,128]{2,1,0:T(8,128)(2,1)S(1)}, u32[]{:S(2)}, u32[]{:S(2)}) collective-permute-start(bf16[8,128,128]{2,1,0:T(8,128)(2,1)S(1)} %collective-permute-done.4.refs_5_), channel_id=1, source_target_pairs={{0,1},{1,2},{2,3},{3,4},{4,5},{5,6},{6,7},{7,0},{8,9},{9,10},{10,1... | collective-permute-start | bytes 786440 | tf_op jit(solution)/shard_map/ppermute | solution.py:311
  55.8 4.6 %collective-permute-start.8 = (bf16[8,128,128]{2,1,0:T(8,128)(2,1)S(1)}, bf16[8,128,128]{2,1,0:T(8,128)(2,1)}, u32[]{:S(2)}, u32[]{:S(2)}) collective-permute-start(bf16[8,128,128]{2,1,0:T(8,128)(2,1)S(1)} %collective-permute-done.5.refs_6_), channel_id=1, source_target_pairs={{0,7},{1,0},{2,1},{3,2},{4,3},{5,4},{6,5},{7,6},{8,15},{9,8},{10,9... | collective-permute-start | bytes 786440 | tf_op jit(solution)/shard_map/ppermute | solution.py:310
  60.4 2.2 %collective-permute-start.12 = (bf16[8,128,128]{2,1,0:T(8,128)(2,1)S(1)}, bf16[8,128,128]{2,1,0:T(8,128)(2,1)}, u32[]{:S(2)}, u32[]{:S(2)}) collective-permute-start(bf16[8,128,128]{2,1,0:T(8,128)(2,1)S(1)} %collective-permute-done.9.refs_11_), channel_id=1, source_target_pairs={{0,7},{1,0},{2,1},{3,2},{4,3},{5,4},{6,5},{7,6},{8,15},{9,8},{10,9... | collective-permute-start | bytes 786440 | tf_op jit(solution)/shard_map/ppermute | solution.py:312
  62.6 3.1 %collective-permute-start.3 = (bf16[8,128,128]{2,1,0:T(8,128)(2,1)S(1)}, bf16[8,128,128]{2,1,0:T(8,128)(2,1)}, u32[]{:S(2)}, u32[]{:S(2)}) collective-permute-start(bf16[8,128,128]{2,1,0:T(8,128)(2,1)S(1)} %collective-permute-done.2.refs_8_), channel_id=1, source_target_pairs={{0,1},{1,2},{2,3},{3,4},{4,5},{5,6},{6,7},{7,0},{8,9},{9,10},{10,1... | collective-permute-start | bytes 786440 | tf_op jit(solution)/shard_map/ppermute | solution.py:309
  65.7 1.9 %collective-permute-start.10 = (bf16[8,128,128]{2,1,0:T(8,128)(2,1)S(1)}, bf16[8,128,128]{2,1,0:T(8,128)(2,1)}, u32[]{:S(2)}, u32[]{:S(2)}) collective-permute-start(bf16[8,128,128]{2,1,0:T(8,128)(2,1)S(1)} %collective-permute-done.7.refs_9_), channel_id=1, source_target_pairs={{0,1},{1,2},{2,3},{3,4},{4,5},{5,6},{6,7},{7,0},{8,9},{9,10},{10,1... | collective-permute-start | bytes 786440 | tf_op jit(solution)/shard_map/ppermute | solution.py:311
  67.6 4.6 %collective-permute-start.11 = (bf16[8,128,128]{2,1,0:T(8,128)(2,1)}, bf16[8,128,128]{2,1,0:T(8,128)(2,1)}, u32[]{:S(2)}, u32[]{:S(2)}) collective-permute-start(bf16[8,128,128]{2,1,0:T(8,128)(2,1)} %collective-permute-done.8.refs_10_), channel_id=1, source_target_pairs={{0,7},{1,0},{2,1},{3,2},{4,3},{5,4},{6,5},{7,6},{8,15},{9,8},{10,9... | collective-permute-start | bytes 786440 | tf_op jit(solution)/shard_map/ppermute | solution.py:310
  72.2 2.2 %collective-permute-start.14 = (bf16[8,128,128]{2,1,0:T(8,128)(2,1)}, bf16[8,128,128]{2,1,0:T(8,128)(2,1)}, u32[]{:S(2)}, u32[]{:S(2)}) collective-permute-start(bf16[8,128,128]{2,1,0:T(8,128)(2,1)} %collective-permute-done.12.refs_15_), channel_id=1, source_target_pairs={{0,7},{1,0},{2,1},{3,2},{4,3},{5,4},{6,5},{7,6},{8,15},{9,8},{10,9... | collective-permute-start | bytes 786440 | tf_op jit(solution)/shard_map/ppermute | solution.py:316
  74.5 3.1 %collective-permute-start.13 = (bf16[8,128,128]{2,1,0:T(8,128)(2,1)}, bf16[8,128,128]{2,1,0:T(8,128)(2,1)S(1)}, u32[]{:S(2)}, u32[]{:S(2)}) collective-permute-start(bf16[8,128,128]{2,1,0:T(8,128)(2,1)} %collective-permute-done.3.refs_12_), channel_id=1, source_target_pairs={{0,1},{1,2},{2,3},{3,4},{4,5},{5,6},{6,7},{7,0},{8,9},{9,10},{10,1... | collective-permute-start | bytes 786440 | tf_op jit(solution)/shard_map/ppermute | solution.py:315
  77.6 5.1 %collective-permute-done.14.refs_17_ = bf16[8,128,128]{2,1,0:T(8,128)(2,1)} collective-permute-done((bf16[8,128,128]{2,1,0:T(8,128)(2,1)}, bf16[8,128,128]{2,1,0:T(8,128)(2,1)}, u32[]{:S(2)}, u32[]{:S(2)}) %collective-permute-start.14) | collective-permute-done | bytes 262176 | tf_op jit(solution)/shard_map/ppermute | solution.py:316
  82.7 0.3 collective-permute-done.13.refs_16_
  83.0 6.2 %cross_attention.1 = bf16[32,136,128]{2,1,0:T(8,128)(2,1)} custom-call(s32[1,32]{1,0:T(1,128)S(1)} %wanted_passages.1.wanted, bf16[1024,512]{1,0:T(8,128)(2,1)S(1)} %order_weights.1.refs_0_, bf16[32,64,256]{2,1,0:T(8,128)(2,1)} %all-to-all-done.refs_1_, bf16[8,128,128]{2,1,0:T(8,128)(2,1)S(1)} %get-tuple-element.18.refs_2_, ...), custom_call_target="tpu_custom_call" | custom-call | flops 2684354560 | bytes 7340032 | tf_op jit(solution)/shard_map/cross_attention/pallas_call | solution.py:228
  89.3 12.8 %all-to-all-start.1 = ((bf16[32,136,128]{2,1,0:T(8,128)(2,1)}), bf16[32,136,128]{2,1,0:T(8,128)(2,1)S(1)}, u32[]{:S(2)}, u32[]{:S(2)}) async-start(bf16[32,136,128]{2,1,0:T(8,128)(2,1)} %cross_attention.1), calls=%async_computation.1 | async-start | bytes 2228224 | tf_op jit(solution)/shard_map/all_to_all | solution.py:356
  102.1 1.0 copy-done.7
  103.1 4.2 %self_attention.1 = f32[1024,256]{1,0:T(8,128)S(1)} custom-call(bf16[1024,256]{1,0:T(8,128)(2,1)S(1)} %bitcast.19, bf16[1024,256]{1,0:T(8,128)(2,1)S(1)} %bitcast.20, bf16[1024,256]{1,0:T(8,128)(2,1)S(1)} %bitcast.21), custom_call_target="tpu_custom_call" | custom-call | flops 805306368 | bytes 2621440 | tf_op jit(solution)/shard_map/self_attention/pallas_call | solution.py:96
  107.3 22.6 %all-to-all-done.1.arrived_ref = bf16[32,136,128]{2,1,0:T(8,128)(2,1)S(1)} async-done(((bf16[32,136,128]{2,1,0:T(8,128)(2,1)}), bf16[32,136,128]{2,1,0:T(8,128)(2,1)S(1)}, u32[]{:S(2)}, u32[]{:S(2)}) %all-to-all-start.1) | async-done | bytes 1114144 | tf_op jit(solution)/shard_map/all_to_all | solution.py:356
  129.9 2.5 %mix.1 = bf16[16,64,256]{2,1,0:T(8,128)(2,1)} custom-call(s32[2]{0:T(128)S(1)} %pad_add_fusion.place, s32[2,32,32]{2,1,0:T(8,128)S(1)} %copy-done.4, bf16[32,136,128]{2,1,0:T(8,128)(2,1)S(1)} %all-to-all-done.1.arrived_ref, f32[16,64,256]{2,1,0:T(8,128)S(1)} %bitcast.17), custom_call_target="tpu_custom_call" | custom-call | flops 2097152 | bytes 2621440 | tf_op jit(solution)/shard_map/mix/pallas_call | solution.py:286
  (30 shorter events, 0.4 us)
Async XLA Ops:
  0.0 33.8 %collective-permute-start = (bf16[16,128,128]{2,1,0:T(8,128)(2,1)}, bf16[16,128,128]{2,1,0:T(8,128)(2,1)S(1)}, u32[]{:S(2)}, u32[]{:S(2)}) collective-permute-start(bf16[16,128,128]{2,1,0:T(8,128)(2,1)} %bitcast.22), channel_id=1, source_target_pairs={{0,384},{8,392},{16,400},{24,408},{32,416},{40,424},{48,432},{56,4... | collective-permute-start | bytes 1572872 | tf_op jit(solution)/shard_map/ppermute | solution.py:340
  11.6 1.0 copy-start.2
  12.6 0.8 copy-start.3
  15.6 6.5 %copy-start.4 = (s32[2,32,32]{2,1,0:T(8,128)S(1)}, s32[2,32,32]{2,1,0:T(8,128)}, u32[]{:S(2)}) copy-start(s32[2,32,32]{2,1,0:T(8,128)} %block_map.3) | copy-start | bytes 24580
  15.6 6.5 %copy-start.8 = (s32[2,32,32]{2,1,0:T(8,128)S(1)}, s32[2,32,32]{2,1,0:T(8,128)}, u32[]{:S(2)}) copy-start(s32[2,32,32]{2,1,0:T(8,128)} %passage_ids_ref.1) | copy-start | bytes 24580
  15.6 58.9 %all-to-all-start = ((bf16[32,64,256]{2,1,0:T(8,128)(2,1)}), bf16[32,64,256]{2,1,0:T(8,128)(2,1)}, u32[]{:S(2)}, u32[]{:S(2)}) async-start(bf16[32,64,256]{2,1,0:T(8,128)(2,1)} %pack_queries.1), calls=%async_computation | async-start | bytes 2097152 | tf_op jit(solution)/shard_map/all_to_all | solution.py:348
  22.1 1.0 copy-start
  22.1 1.2 copy-start.1
  33.8 13.5 %collective-permute-start.6 = (bf16[8,128,128]{2,1,0:T(8,128)(2,1)S(1)}, bf16[8,128,128]{2,1,0:T(8,128)(2,1)S(1)}, u32[]{:S(2)}, u32[]{:S(2)}) collective-permute-start(bf16[8,128,128]{2,1,0:T(8,128)(2,1)S(1)} %get-tuple-element.17.refs_3_), channel_id=1, source_target_pairs={{0,7},{1,0},{2,1},{3,2},{4,3},{5,4},{6,5},{7,6},{8,15},{9,8},{10,9... | collective-permute-start | bytes 786440 | tf_op jit(solution)/shard_map/ppermute | solution.py:312
  38.9 11.8 %collective-permute-start.1 = (bf16[8,128,128]{2,1,0:T(8,128)(2,1)S(1)}, bf16[8,128,128]{2,1,0:T(8,128)(2,1)S(1)}, u32[]{:S(2)}, u32[]{:S(2)}) collective-permute-start(bf16[8,128,128]{2,1,0:T(8,128)(2,1)S(1)} %get-tuple-element.18.refs_2_), channel_id=1, source_target_pairs={{0,1},{1,2},{2,3},{3,4},{4,5},{5,6},{6,7},{7,0},{8,9},{9,10},{10,1... | collective-permute-start | bytes 786440 | tf_op jit(solution)/shard_map/ppermute | solution.py:309
  40.9 13.0 %collective-permute-start.4 = (bf16[8,128,128]{2,1,0:T(8,128)(2,1)S(1)}, bf16[8,128,128]{2,1,0:T(8,128)(2,1)S(1)}, u32[]{:S(2)}, u32[]{:S(2)}) collective-permute-start(bf16[8,128,128]{2,1,0:T(8,128)(2,1)S(1)} %get-tuple-element.17.refs_3_), channel_id=1, source_target_pairs={{0,1},{1,2},{2,3},{3,4},{4,5},{5,6},{6,7},{7,0},{8,9},{9,10},{10,1... | collective-permute-start | bytes 786440 | tf_op jit(solution)/shard_map/ppermute | solution.py:311
  42.8 13.0 %collective-permute-start.5 = (bf16[8,128,128]{2,1,0:T(8,128)(2,1)S(1)}, bf16[8,128,128]{2,1,0:T(8,128)(2,1)S(1)}, u32[]{:S(2)}, u32[]{:S(2)}) collective-permute-start(bf16[8,128,128]{2,1,0:T(8,128)(2,1)S(1)} %get-tuple-element.18.refs_2_), channel_id=1, source_target_pairs={{0,7},{1,0},{2,1},{3,2},{4,3},{5,4},{6,5},{7,6},{8,15},{9,8},{10,9... | collective-permute-start | bytes 786440 | tf_op jit(solution)/shard_map/ppermute | solution.py:310
  47.4 13.0 %collective-permute-start.9 = (bf16[8,128,128]{2,1,0:T(8,128)(2,1)S(1)}, bf16[8,128,128]{2,1,0:T(8,128)(2,1)S(1)}, u32[]{:S(2)}, u32[]{:S(2)}) collective-permute-start(bf16[8,128,128]{2,1,0:T(8,128)(2,1)S(1)} %collective-permute-done.6.refs_7_), channel_id=1, source_target_pairs={{0,7},{1,0},{2,1},{3,2},{4,3},{5,4},{6,5},{7,6},{8,15},{9,8},{10,9... | collective-permute-start | bytes 786440 | tf_op jit(solution)/shard_map/ppermute | solution.py:312
  50.8 11.8 %collective-permute-start.2 = (bf16[8,128,128]{2,1,0:T(8,128)(2,1)S(1)}, bf16[8,128,128]{2,1,0:T(8,128)(2,1)S(1)}, u32[]{:S(2)}, u32[]{:S(2)}) collective-permute-start(bf16[8,128,128]{2,1,0:T(8,128)(2,1)S(1)} %collective-permute-done.1.refs_4_), channel_id=1, source_target_pairs={{0,1},{1,2},{2,3},{3,4},{4,5},{5,6},{6,7},{7,0},{8,9},{9,10},{10,1... | collective-permute-start | bytes 786440 | tf_op jit(solution)/shard_map/ppermute | solution.py:309
  53.9 11.8 %collective-permute-start.7 = (bf16[8,128,128]{2,1,0:T(8,128)(2,1)S(1)}, bf16[8,128,128]{2,1,0:T(8,128)(2,1)S(1)}, u32[]{:S(2)}, u32[]{:S(2)}) collective-permute-start(bf16[8,128,128]{2,1,0:T(8,128)(2,1)S(1)} %collective-permute-done.4.refs_5_), channel_id=1, source_target_pairs={{0,1},{1,2},{2,3},{3,4},{4,5},{5,6},{6,7},{7,0},{8,9},{9,10},{10,1... | collective-permute-start | bytes 786440 | tf_op jit(solution)/shard_map/ppermute | solution.py:311
  55.8 11.8 %collective-permute-start.8 = (bf16[8,128,128]{2,1,0:T(8,128)(2,1)S(1)}, bf16[8,128,128]{2,1,0:T(8,128)(2,1)}, u32[]{:S(2)}, u32[]{:S(2)}) collective-permute-start(bf16[8,128,128]{2,1,0:T(8,128)(2,1)S(1)} %collective-permute-done.5.refs_6_), channel_id=1, source_target_pairs={{0,7},{1,0},{2,1},{3,2},{4,3},{5,4},{6,5},{7,6},{8,15},{9,8},{10,9... | collective-permute-start | bytes 786440 | tf_op jit(solution)/shard_map/ppermute | solution.py:310
  60.4 11.8 %collective-permute-start.12 = (bf16[8,128,128]{2,1,0:T(8,128)(2,1)S(1)}, bf16[8,128,128]{2,1,0:T(8,128)(2,1)}, u32[]{:S(2)}, u32[]{:S(2)}) collective-permute-start(bf16[8,128,128]{2,1,0:T(8,128)(2,1)S(1)} %collective-permute-done.9.refs_11_), channel_id=1, source_target_pairs={{0,7},{1,0},{2,1},{3,2},{4,3},{5,4},{6,5},{7,6},{8,15},{9,8},{10,9... | collective-permute-start | bytes 786440 | tf_op jit(solution)/shard_map/ppermute | solution.py:312
  62.6 11.8 %collective-permute-start.3 = (bf16[8,128,128]{2,1,0:T(8,128)(2,1)S(1)}, bf16[8,128,128]{2,1,0:T(8,128)(2,1)}, u32[]{:S(2)}, u32[]{:S(2)}) collective-permute-start(bf16[8,128,128]{2,1,0:T(8,128)(2,1)S(1)} %collective-permute-done.2.refs_8_), channel_id=1, source_target_pairs={{0,1},{1,2},{2,3},{3,4},{4,5},{5,6},{6,7},{7,0},{8,9},{9,10},{10,1... | collective-permute-start | bytes 786440 | tf_op jit(solution)/shard_map/ppermute | solution.py:309
  65.7 11.9 %collective-permute-start.10 = (bf16[8,128,128]{2,1,0:T(8,128)(2,1)S(1)}, bf16[8,128,128]{2,1,0:T(8,128)(2,1)}, u32[]{:S(2)}, u32[]{:S(2)}) collective-permute-start(bf16[8,128,128]{2,1,0:T(8,128)(2,1)S(1)} %collective-permute-done.7.refs_9_), channel_id=1, source_target_pairs={{0,1},{1,2},{2,3},{3,4},{4,5},{5,6},{6,7},{7,0},{8,9},{9,10},{10,1... | collective-permute-start | bytes 786440 | tf_op jit(solution)/shard_map/ppermute | solution.py:311
  67.6 9.9 %collective-permute-start.11 = (bf16[8,128,128]{2,1,0:T(8,128)(2,1)}, bf16[8,128,128]{2,1,0:T(8,128)(2,1)}, u32[]{:S(2)}, u32[]{:S(2)}) collective-permute-start(bf16[8,128,128]{2,1,0:T(8,128)(2,1)} %collective-permute-done.8.refs_10_), channel_id=1, source_target_pairs={{0,7},{1,0},{2,1},{3,2},{4,3},{5,4},{6,5},{7,6},{8,15},{9,8},{10,9... | collective-permute-start | bytes 786440 | tf_op jit(solution)/shard_map/ppermute | solution.py:310
  72.2 10.5 %collective-permute-start.14 = (bf16[8,128,128]{2,1,0:T(8,128)(2,1)}, bf16[8,128,128]{2,1,0:T(8,128)(2,1)}, u32[]{:S(2)}, u32[]{:S(2)}) collective-permute-start(bf16[8,128,128]{2,1,0:T(8,128)(2,1)} %collective-permute-done.12.refs_15_), channel_id=1, source_target_pairs={{0,7},{1,0},{2,1},{3,2},{4,3},{5,4},{6,5},{7,6},{8,15},{9,8},{10,9... | collective-permute-start | bytes 786440 | tf_op jit(solution)/shard_map/ppermute | solution.py:316
  74.5 8.5 %collective-permute-start.13 = (bf16[8,128,128]{2,1,0:T(8,128)(2,1)}, bf16[8,128,128]{2,1,0:T(8,128)(2,1)S(1)}, u32[]{:S(2)}, u32[]{:S(2)}) collective-permute-start(bf16[8,128,128]{2,1,0:T(8,128)(2,1)} %collective-permute-done.3.refs_12_), channel_id=1, source_target_pairs={{0,1},{1,2},{2,3},{3,4},{4,5},{5,6},{6,7},{7,0},{8,9},{9,10},{10,1... | collective-permute-start | bytes 786440 | tf_op jit(solution)/shard_map/ppermute | solution.py:315
  89.3 12.8 %copy-start.5 = (bf16[1,1,1024,256]{3,2,1,0:T(8,128)(2,1)S(1)}, bf16[1,1,1024,256]{3,2,1,0:T(8,128)(2,1)}, u32[]{:S(2)}) copy-start(bf16[1,1,1024,256]{3,2,1,0:T(8,128)(2,1)} %param.9) | copy-start | bytes 1572868
  89.3 12.8 %copy-start.6 = (bf16[1,1,1024,256]{3,2,1,0:T(8,128)(2,1)S(1)}, bf16[1,1,1024,256]{3,2,1,0:T(8,128)(2,1)}, u32[]{:S(2)}) copy-start(bf16[1,1,1024,256]{3,2,1,0:T(8,128)(2,1)} %param.10) | copy-start | bytes 1572868
  89.3 40.6 %all-to-all-start.1 = ((bf16[32,136,128]{2,1,0:T(8,128)(2,1)}), bf16[32,136,128]{2,1,0:T(8,128)(2,1)S(1)}, u32[]{:S(2)}, u32[]{:S(2)}) async-start(bf16[32,136,128]{2,1,0:T(8,128)(2,1)} %cross_attention.1), calls=%async_computation.1 | async-start | bytes 2228224 | tf_op jit(solution)/shard_map/all_to_all | solution.py:356
  102.1 1.0 copy-start.7

commit v6 on v5

--- a/solution.py
+++ b/solution.py
@@ -245,7 +245,7 @@
     )(wanted, weights, queries, *shards)
 
 
-def mix_kernel(place, block_map, arrived_ref, self_ref, out_ref):
+def mix_kernel(place, block_map, arrived_ref, self_ref, out_hbm, out_ref, sems):
     groups, rows, feats = self_ref.shape
     heads = feats // HD
     own_side, own_seq = place[0], place[1]
@@ -268,17 +268,26 @@
     share = raised / (raised + jnp.exp2(seconds - top))
     columns = share.T
     head = last_row_mask(rows, HD)
-    for g in range(heads):
-        cols = slice(g * HD, (g + 1) * HD)
-        own = slice(g * rows, (g + 1) * rows)
-        before = jnp.zeros((rows, HD), jnp.float32)
-        for u in range(groups):
+    before = [jnp.zeros((rows, HD), jnp.float32)] * heads
+    step = groups // 2
+    stores = []
+    for u in range(groups):
+        for g in range(heads):
+            cols = slice(g * HD, (g + 1) * HD)
+            own = slice(g * rows, (g + 1) * rows)
             one = arrived_ref[slots[u][0], own, :].astype(jnp.float32)
             two = arrived_ref[slots[u][1], own, :].astype(jnp.float32)
             now = two + columns[own, u : u + 1] * (one - two)
-            cross = jnp.where(head, before, now)
+            cross = jnp.where(head, before[g], now)
             out_ref[u, :, cols] = (self_ref[u, :, cols] + cross).astype(jnp.bfloat16)
-            before = now
+            before = before[:g] + [now] + before[g + 1 :]
+        if (u + 1) % step == 0:
+            span = pl.ds(u + 1 - step, step)
+            store = pltpu.make_async_copy(out_ref.at[span], out_hbm.at[span], sems.at[u // step])
+            store.start()
+            stores.append(store)
+    for store in stores:
+        store.wait()
 
 
 def mix(place, block_map, arrived, self_out):
@@ -287,7 +296,11 @@
         mix_kernel,
         out_shape=jax.ShapeDtypeStruct(self_out.shape, jnp.bfloat16),
         in_specs=[pl.BlockSpec(memory_space=pltpu.SMEM)] * 2 + [IN_VMEM] * 2,
-        out_specs=IN_VMEM,
+        out_specs=ANYWHERE,
+        scratch_shapes=[
+            pltpu.VMEM(self_out.shape, jnp.bfloat16),
+            pltpu.SemaphoreType.DMA((2,)),
+        ],
         compiler_params=params(),
         cost_estimate=pl.CostEstimate(
             flops=8 * groups * rows * feats,

time: 133 us -> 133 us (level)
  no operation moved by 1% of the time
where the time goes in v6:
time: 133 us; the launch traced here: 132 us
  starting transfers between devices  73.1 us (55%)
  waiting for transfers between devices  39.1 us (29%)
  Pallas kernels  16.4 us (12%)
  local copies, waits for them, and re-layouts  3.4 us (3%)
    all_to_all x1, waiting for transfers between devices, on_device(): lax.all_to_all(answers, 'seq', split_axis=0, concat_axis=0, tiled=True)  22.6 us
    ppermute x3, starting transfers between devices, ring_gather(): left_low = lax.ppermute(left_low, axis, down)  13.7 us
    all_to_all x1, starting transfers between devices, on_device(): lax.all_to_all(answers, 'seq', split_axis=0, concat_axis=0, tiled=True)  12.8 us
    ppermute x1, starting transfers between devices, on_device(): lax.ppermute(passages[0, 0], ('side', 'seq'), [(h * blocks + b, (1 - h) *...  11.5 us
    ppermute x3, starting transfers between devices, ring_gather(): left_high = lax.ppermute(left_high, axis, down)  10.7 us
    ppermute x1, waiting for transfers between devices, on_device(): lax.ppermute(passages[0, 0], ('side', 'seq'), [(h * blocks + b, (1 - h) *...  9.84 us
    ppermute x3, starting transfers between devices, ring_gather(): right_low = lax.ppermute(right_low, axis, up)  6.91 us
    all_to_all x1, starting transfers between devices, on_device(): lax.all_to_all(chunks, 'seq', split_axis=0, concat_axis=0, tiled=True)  6.51 us
  transfers between devices with their start and end apart: 17, of which 5 were waited for; matrix products, arithmetic and copies ran while one was open for 0% of the time, Pallas kernels for 6%

profile of v6, /device:TPU:1, one launch (start us, length us, event | category | flops | bytes accessed | tf_op | source)
XLA Modules:
  0.0 132.4 jit_solution(17116455106683206190)
XLA Ops:
  0.0 11.5 %collective-permute-start = (bf16[16,128,128]{2,1,0:T(8,128)(2,1)}, bf16[16,128,128]{2,1,0:T(8,128)(2,1)S(1)}, u32[]{:S(2)}, u32[]{:S(2)}) collective-permute-start(bf16[16,128,128]{2,1,0:T(8,128)(2,1)} %bitcast.22), channel_id=1, source_target_pairs={{0,384},{8,392},{16,400},{24,408},{32,416},{40,424},{48,432},{56,4... | collective-permute-start | bytes 1572872 | tf_op jit(solution)/shard_map/ppermute | solution.py:353
  11.6 1.0 copy-done.2
  12.6 0.8 copy-done.3
  13.4 2.2 %pack_queries.1 = bf16[32,64,256]{2,1,0:T(8,128)(2,1)} custom-call(s32[2]{0:T(128)S(1)} %pad_add_fusion.place, s32[2,32,32]{2,1,0:T(8,128)S(1)} %copy-done.3, bf16[16,64,256]{2,1,0:T(8,128)(2,1)S(1)} %bitcast.18), custom_call_target="tpu_custom_call" | custom-call | bytes 1572864 | tf_op jit(solution)/shard_map/pack_queries/pallas_call | solution.py:52
  15.6 6.5 %all-to-all-start = ((bf16[32,64,256]{2,1,0:T(8,128)(2,1)}), bf16[32,64,256]{2,1,0:T(8,128)(2,1)}, u32[]{:S(2)}, u32[]{:S(2)}) async-start(bf16[32,64,256]{2,1,0:T(8,128)(2,1)} %pack_queries.1), calls=%async_computation | async-start | bytes 2097152 | tf_op jit(solution)/shard_map/all_to_all | solution.py:361
  22.1 0.7 wanted_passages.1.wanted
  22.9 0.3 copy-done
  23.3 0.6 order_weights.1.refs_0_
  23.9 9.8 %collective-permute-done = bf16[16,128,128]{2,1,0:T(8,128)(2,1)S(1)} collective-permute-done((bf16[16,128,128]{2,1,0:T(8,128)(2,1)}, bf16[16,128,128]{2,1,0:T(8,128)(2,1)S(1)}, u32[]{:S(2)}, u32[]{:S(2)}) %collective-permute-start) | collective-permute-done | bytes 524320 | tf_op jit(solution)/shard_map/ppermute | solution.py:353
  33.8 5.1 %collective-permute-start.6 = (bf16[8,128,128]{2,1,0:T(8,128)(2,1)S(1)}, bf16[8,128,128]{2,1,0:T(8,128)(2,1)S(1)}, u32[]{:S(2)}, u32[]{:S(2)}) collective-permute-start(bf16[8,128,128]{2,1,0:T(8,128)(2,1)S(1)} %get-tuple-element.17.refs_3_), channel_id=1, source_target_pairs={{0,7},{1,0},{2,1},{3,2},{4,3},{5,4},{6,5},{7,6},{8,15},{9,8},{10,9... | collective-permute-start | bytes 786440 | tf_op jit(solution)/shard_map/ppermute | solution.py:325
  38.9 1.9 %collective-permute-start.1 = (bf16[8,128,128]{2,1,0:T(8,128)(2,1)S(1)}, bf16[8,128,128]{2,1,0:T(8,128)(2,1)S(1)}, u32[]{:S(2)}, u32[]{:S(2)}) collective-permute-start(bf16[8,128,128]{2,1,0:T(8,128)(2,1)S(1)} %get-tuple-element.18.refs_2_), channel_id=1, source_target_pairs={{0,1},{1,2},{2,3},{3,4},{4,5},{5,6},{6,7},{7,0},{8,9},{9,10},{10,1... | collective-permute-start | bytes 786440 | tf_op jit(solution)/shard_map/ppermute | solution.py:322
  40.9 1.9 %collective-permute-start.4 = (bf16[8,128,128]{2,1,0:T(8,128)(2,1)S(1)}, bf16[8,128,128]{2,1,0:T(8,128)(2,1)S(1)}, u32[]{:S(2)}, u32[]{:S(2)}) collective-permute-start(bf16[8,128,128]{2,1,0:T(8,128)(2,1)S(1)} %get-tuple-element.17.refs_3_), channel_id=1, source_target_pairs={{0,1},{1,2},{2,3},{3,4},{4,5},{5,6},{6,7},{7,0},{8,9},{9,10},{10,1... | collective-permute-start | bytes 786440 | tf_op jit(solution)/shard_map/ppermute | solution.py:324
  42.8 4.6 %collective-permute-start.5 = (bf16[8,128,128]{2,1,0:T(8,128)(2,1)S(1)}, bf16[8,128,128]{2,1,0:T(8,128)(2,1)S(1)}, u32[]{:S(2)}, u32[]{:S(2)}) collective-permute-start(bf16[8,128,128]{2,1,0:T(8,128)(2,1)S(1)} %get-tuple-element.18.refs_2_), channel_id=1, source_target_pairs={{0,7},{1,0},{2,1},{3,2},{4,3},{5,4},{6,5},{7,6},{8,15},{9,8},{10,9... | collective-permute-start | bytes 786440 | tf_op jit(solution)/shard_map/ppermute | solution.py:323
  47.4 3.4 %collective-permute-start.9 = (bf16[8,128,128]{2,1,0:T(8,128)(2,1)S(1)}, bf16[8,128,128]{2,1,0:T(8,128)(2,1)S(1)}, u32[]{:S(2)}, u32[]{:S(2)}) collective-permute-start(bf16[8,128,128]{2,1,0:T(8,128)(2,1)S(1)} %collective-permute-done.6.refs_7_), channel_id=1, source_target_pairs={{0,7},{1,0},{2,1},{3,2},{4,3},{5,4},{6,5},{7,6},{8,15},{9,8},{10,9... | collective-permute-start | bytes 786440 | tf_op jit(solution)/shard_map/ppermute | solution.py:325
  50.8 1.9 %collective-permute-start.2 = (bf16[8,128,128]{2,1,0:T(8,128)(2,1)S(1)}, bf16[8,128,128]{2,1,0:T(8,128)(2,1)S(1)}, u32[]{:S(2)}, u32[]{:S(2)}) collective-permute-start(bf16[8,128,128]{2,1,0:T(8,128)(2,1)S(1)} %collective-permute-done.1.refs_4_), channel_id=1, source_target_pairs={{0,1},{1,2},{2,3},{3,4},{4,5},{5,6},{6,7},{7,0},{8,9},{9,10},{10,1... | collective-permute-start | bytes 786440 | tf_op jit(solution)/shard_map/ppermute | solution.py:322
  52.7 1.2 collective-permute-done.4.refs_5_
  53.9 1.9 %collective-permute-start.7 = (bf16[8,128,128]{2,1,0:T(8,128)(2,1)S(1)}, bf16[8,128,128]{2,1,0:T(8,128)(2,1)S(1)}, u32[]{:S(2)}, u32[]{:S(2)}) collective-permute-start(bf16[8,128,128]{2,1,0:T(8,128)(2,1)S(1)} %collective-permute-done.4.refs_5_), channel_id=1, source_target_pairs={{0,1},{1,2},{2,3},{3,4},{4,5},{5,6},{6,7},{7,0},{8,9},{9,10},{10,1... | collective-permute-start | bytes 786440 | tf_op jit(solution)/shard_map/ppermute | solution.py:324
  55.8 4.6 %collective-permute-start.8 = (bf16[8,128,128]{2,1,0:T(8,128)(2,1)S(1)}, bf16[8,128,128]{2,1,0:T(8,128)(2,1)}, u32[]{:S(2)}, u32[]{:S(2)}) collective-permute-start(bf16[8,128,128]{2,1,0:T(8,128)(2,1)S(1)} %collective-permute-done.5.refs_6_), channel_id=1, source_target_pairs={{0,7},{1,0},{2,1},{3,2},{4,3},{5,4},{6,5},{7,6},{8,15},{9,8},{10,9... | collective-permute-start | bytes 786440 | tf_op jit(solution)/shard_map/ppermute | solution.py:323
  60.4 2.2 %collective-permute-start.12 = (bf16[8,128,128]{2,1,0:T(8,128)(2,1)S(1)}, bf16[8,128,128]{2,1,0:T(8,128)(2,1)}, u32[]{:S(2)}, u32[]{:S(2)}) collective-permute-start(bf16[8,128,128]{2,1,0:T(8,128)(2,1)S(1)} %collective-permute-done.9.refs_11_), channel_id=1, source_target_pairs={{0,7},{1,0},{2,1},{3,2},{4,3},{5,4},{6,5},{7,6},{8,15},{9,8},{10,9... | collective-permute-start | bytes 786440 | tf_op jit(solution)/shard_map/ppermute | solution.py:325
  62.6 3.1 %collective-permute-start.3 = (bf16[8,128,128]{2,1,0:T(8,128)(2,1)S(1)}, bf16[8,128,128]{2,1,0:T(8,128)(2,1)}, u32[]{:S(2)}, u32[]{:S(2)}) collective-permute-start(bf16[8,128,128]{2,1,0:T(8,128)(2,1)S(1)} %collective-permute-done.2.refs_8_), channel_id=1, source_target_pairs={{0,1},{1,2},{2,3},{3,4},{4,5},{5,6},{6,7},{7,0},{8,9},{9,10},{10,1... | collective-permute-start | bytes 786440 | tf_op jit(solution)/shard_map/ppermute | solution.py:322
  65.7 1.9 %collective-permute-start.10 = (bf16[8,128,128]{2,1,0:T(8,128)(2,1)S(1)}, bf16[8,128,128]{2,1,0:T(8,128)(2,1)}, u32[]{:S(2)}, u32[]{:S(2)}) collective-permute-start(bf16[8,128,128]{2,1,0:T(8,128)(2,1)S(1)} %collective-permute-done.7.refs_9_), channel_id=1, source_target_pairs={{0,1},{1,2},{2,3},{3,4},{4,5},{5,6},{6,7},{7,0},{8,9},{9,10},{10,1... | collective-permute-start | bytes 786440 | tf_op jit(solution)/shard_map/ppermute | solution.py:324
  67.6 4.6 %collective-permute-start.11 = (bf16[8,128,128]{2,1,0:T(8,128)(2,1)}, bf16[8,128,128]{2,1,0:T(8,128)(2,1)}, u32[]{:S(2)}, u32[]{:S(2)}) collective-permute-start(bf16[8,128,128]{2,1,0:T(8,128)(2,1)} %collective-permute-done.8.refs_10_), channel_id=1, source_target_pairs={{0,7},{1,0},{2,1},{3,2},{4,3},{5,4},{6,5},{7,6},{8,15},{9,8},{10,9... | collective-permute-start | bytes 786440 | tf_op jit(solution)/shard_map/ppermute | solution.py:323
  72.2 2.2 %collective-permute-start.14 = (bf16[8,128,128]{2,1,0:T(8,128)(2,1)}, bf16[8,128,128]{2,1,0:T(8,128)(2,1)}, u32[]{:S(2)}, u32[]{:S(2)}) collective-permute-start(bf16[8,128,128]{2,1,0:T(8,128)(2,1)} %collective-permute-done.12.refs_15_), channel_id=1, source_target_pairs={{0,7},{1,0},{2,1},{3,2},{4,3},{5,4},{6,5},{7,6},{8,15},{9,8},{10,9... | collective-permute-start | bytes 786440 | tf_op jit(solution)/shard_map/ppermute | solution.py:329
  74.5 3.1 %collective-permute-start.13 = (bf16[8,128,128]{2,1,0:T(8,128)(2,1)}, bf16[8,128,128]{2,1,0:T(8,128)(2,1)S(1)}, u32[]{:S(2)}, u32[]{:S(2)}) collective-permute-start(bf16[8,128,128]{2,1,0:T(8,128)(2,1)} %collective-permute-done.3.refs_12_), channel_id=1, source_target_pairs={{0,1},{1,2},{2,3},{3,4},{4,5},{5,6},{6,7},{7,0},{8,9},{9,10},{10,1... | collective-permute-start | bytes 786440 | tf_op jit(solution)/shard_map/ppermute | solution.py:328
  77.6 5.1 %collective-permute-done.14.refs_17_ = bf16[8,128,128]{2,1,0:T(8,128)(2,1)} collective-permute-done((bf16[8,128,128]{2,1,0:T(8,128)(2,1)}, bf16[8,128,128]{2,1,0:T(8,128)(2,1)}, u32[]{:S(2)}, u32[]{:S(2)}) %collective-permute-start.14) | collective-permute-done | bytes 262176 | tf_op jit(solution)/shard_map/ppermute | solution.py:329
  82.7 0.3 collective-permute-done.13.refs_16_
  83.0 6.2 %cross_attention.1 = bf16[32,136,128]{2,1,0:T(8,128)(2,1)} custom-call(s32[1,32]{1,0:T(1,128)S(1)} %wanted_passages.1.wanted, bf16[1024,512]{1,0:T(8,128)(2,1)S(1)} %order_weights.1.refs_0_, bf16[32,64,256]{2,1,0:T(8,128)(2,1)} %all-to-all-done.refs_1_, bf16[8,128,128]{2,1,0:T(8,128)(2,1)S(1)} %get-tuple-element.18.refs_2_, ...), custom_call_target="tpu_custom_call" | custom-call | flops 2684354560 | bytes 7340032 | tf_op jit(solution)/shard_map/cross_attention/pallas_call | solution.py:228
  89.3 12.8 %all-to-all-start.1 = ((bf16[32,136,128]{2,1,0:T(8,128)(2,1)}), bf16[32,136,128]{2,1,0:T(8,128)(2,1)S(1)}, u32[]{:S(2)}, u32[]{:S(2)}) async-start(bf16[32,136,128]{2,1,0:T(8,128)(2,1)} %cross_attention.1), calls=%async_computation.1 | async-start | bytes 2228224 | tf_op jit(solution)/shard_map/all_to_all | solution.py:369
  102.1 1.0 copy-done.7
  103.1 4.2 %self_attention.1 = f32[1024,256]{1,0:T(8,128)S(1)} custom-call(bf16[1024,256]{1,0:T(8,128)(2,1)S(1)} %bitcast.19, bf16[1024,256]{1,0:T(8,128)(2,1)S(1)} %bitcast.20, bf16[1024,256]{1,0:T(8,128)(2,1)S(1)} %bitcast.21), custom_call_target="tpu_custom_call" | custom-call | flops 805306368 | bytes 2621440 | tf_op jit(solution)/shard_map/self_attention/pallas_call | solution.py:96
  107.3 22.6 %all-to-all-done.1.arrived_ref = bf16[32,136,128]{2,1,0:T(8,128)(2,1)S(1)} async-done(((bf16[32,136,128]{2,1,0:T(8,128)(2,1)}), bf16[32,136,128]{2,1,0:T(8,128)(2,1)S(1)}, u32[]{:S(2)}, u32[]{:S(2)}) %all-to-all-start.1) | async-done | bytes 1114144 | tf_op jit(solution)/shard_map/all_to_all | solution.py:369
  129.9 2.5 %mix.1 = bf16[16,64,256]{2,1,0:T(8,128)(2,1)} custom-call(s32[2]{0:T(128)S(1)} %pad_add_fusion.place, s32[2,32,32]{2,1,0:T(8,128)S(1)} %copy-done.4, bf16[32,136,128]{2,1,0:T(8,128)(2,1)S(1)} %all-to-all-done.1.arrived_ref, f32[16,64,256]{2,1,0:T(8,128)S(1)} %bitcast.17), custom_call_target="tpu_custom_call" | custom-call | flops 2097152 | bytes 2621440 | tf_op jit(solution)/shard_map/mix/pallas_call | solution.py:295
  (30 shorter events, 0.4 us)
Async XLA Ops:
  0.0 33.8 %collective-permute-start = (bf16[16,128,128]{2,1,0:T(8,128)(2,1)}, bf16[16,128,128]{2,1,0:T(8,128)(2,1)S(1)}, u32[]{:S(2)}, u32[]{:S(2)}) collective-permute-start(bf16[16,128,128]{2,1,0:T(8,128)(2,1)} %bitcast.22), channel_id=1, source_target_pairs={{0,384},{8,392},{16,400},{24,408},{32,416},{40,424},{48,432},{56,4... | collective-permute-start | bytes 1572872 | tf_op jit(solution)/shard_map/ppermute | solution.py:353
  11.6 1.0 copy-start.2
  12.6 0.8 copy-start.3
  15.6 6.5 %copy-start.4 = (s32[2,32,32]{2,1,0:T(8,128)S(1)}, s32[2,32,32]{2,1,0:T(8,128)}, u32[]{:S(2)}) copy-start(s32[2,32,32]{2,1,0:T(8,128)} %block_map.3) | copy-start | bytes 24580
  15.6 6.5 %copy-start.8 = (s32[2,32,32]{2,1,0:T(8,128)S(1)}, s32[2,32,32]{2,1,0:T(8,128)}, u32[]{:S(2)}) copy-start(s32[2,32,32]{2,1,0:T(8,128)} %passage_ids_ref.1) | copy-start | bytes 24580
  15.6 58.9 %all-to-all-start = ((bf16[32,64,256]{2,1,0:T(8,128)(2,1)}), bf16[32,64,256]{2,1,0:T(8,128)(2,1)}, u32[]{:S(2)}, u32[]{:S(2)}) async-start(bf16[32,64,256]{2,1,0:T(8,128)(2,1)} %pack_queries.1), calls=%async_computation | async-start | bytes 2097152 | tf_op jit(solution)/shard_map/all_to_all | solution.py:361
  22.1 1.0 copy-start
  22.1 1.2 copy-start.1
  33.8 13.5 %collective-permute-start.6 = (bf16[8,128,128]{2,1,0:T(8,128)(2,1)S(1)}, bf16[8,128,128]{2,1,0:T(8,128)(2,1)S(1)}, u32[]{:S(2)}, u32[]{:S(2)}) collective-permute-start(bf16[8,128,128]{2,1,0:T(8,128)(2,1)S(1)} %get-tuple-element.17.refs_3_), channel_id=1, source_target_pairs={{0,7},{1,0},{2,1},{3,2},{4,3},{5,4},{6,5},{7,6},{8,15},{9,8},{10,9... | collective-permute-start | bytes 786440 | tf_op jit(solution)/shard_map/ppermute | solution.py:325
  38.9 11.8 %collective-permute-start.1 = (bf16[8,128,128]{2,1,0:T(8,128)(2,1)S(1)}, bf16[8,128,128]{2,1,0:T(8,128)(2,1)S(1)}, u32[]{:S(2)}, u32[]{:S(2)}) collective-permute-start(bf16[8,128,128]{2,1,0:T(8,128)(2,1)S(1)} %get-tuple-element.18.refs_2_), channel_id=1, source_target_pairs={{0,1},{1,2},{2,3},{3,4},{4,5},{5,6},{6,7},{7,0},{8,9},{9,10},{10,1... | collective-permute-start | bytes 786440 | tf_op jit(solution)/shard_map/ppermute | solution.py:322
  40.9 13.0 %collective-permute-start.4 = (bf16[8,128,128]{2,1,0:T(8,128)(2,1)S(1)}, bf16[8,128,128]{2,1,0:T(8,128)(2,1)S(1)}, u32[]{:S(2)}, u32[]{:S(2)}) collective-permute-start(bf16[8,128,128]{2,1,0:T(8,128)(2,1)S(1)} %get-tuple-element.17.refs_3_), channel_id=1, source_target_pairs={{0,1},{1,2},{2,3},{3,4},{4,5},{5,6},{6,7},{7,0},{8,9},{9,10},{10,1... | collective-permute-start | bytes 786440 | tf_op jit(solution)/shard_map/ppermute | solution.py:324
  42.8 13.0 %collective-permute-start.5 = (bf16[8,128,128]{2,1,0:T(8,128)(2,1)S(1)}, bf16[8,128,128]{2,1,0:T(8,128)(2,1)S(1)}, u32[]{:S(2)}, u32[]{:S(2)}) collective-permute-start(bf16[8,128,128]{2,1,0:T(8,128)(2,1)S(1)} %get-tuple-element.18.refs_2_), channel_id=1, source_target_pairs={{0,7},{1,0},{2,1},{3,2},{4,3},{5,4},{6,5},{7,6},{8,15},{9,8},{10,9... | collective-permute-start | bytes 786440 | tf_op jit(solution)/shard_map/ppermute | solution.py:323
  47.4 13.0 %collective-permute-start.9 = (bf16[8,128,128]{2,1,0:T(8,128)(2,1)S(1)}, bf16[8,128,128]{2,1,0:T(8,128)(2,1)S(1)}, u32[]{:S(2)}, u32[]{:S(2)}) collective-permute-start(bf16[8,128,128]{2,1,0:T(8,128)(2,1)S(1)} %collective-permute-done.6.refs_7_), channel_id=1, source_target_pairs={{0,7},{1,0},{2,1},{3,2},{4,3},{5,4},{6,5},{7,6},{8,15},{9,8},{10,9... | collective-permute-start | bytes 786440 | tf_op jit(solution)/shard_map/ppermute | solution.py:325
  50.8 11.8 %collective-permute-start.2 = (bf16[8,128,128]{2,1,0:T(8,128)(2,1)S(1)}, bf16[8,128,128]{2,1,0:T(8,128)(2,1)S(1)}, u32[]{:S(2)}, u32[]{:S(2)}) collective-permute-start(bf16[8,128,128]{2,1,0:T(8,128)(2,1)S(1)} %collective-permute-done.1.refs_4_), channel_id=1, source_target_pairs={{0,1},{1,2},{2,3},{3,4},{4,5},{5,6},{6,7},{7,0},{8,9},{9,10},{10,1... | collective-permute-start | bytes 786440 | tf_op jit(solution)/shard_map/ppermute | solution.py:322
  53.9 11.8 %collective-permute-start.7 = (bf16[8,128,128]{2,1,0:T(8,128)(2,1)S(1)}, bf16[8,128,128]{2,1,0:T(8,128)(2,1)S(1)}, u32[]{:S(2)}, u32[]{:S(2)}) collective-permute-start(bf16[8,128,128]{2,1,0:T(8,128)(2,1)S(1)} %collective-permute-done.4.refs_5_), channel_id=1, source_target_pairs={{0,1},{1,2},{2,3},{3,4},{4,5},{5,6},{6,7},{7,0},{8,9},{9,10},{10,1... | collective-permute-start | bytes 786440 | tf_op jit(solution)/shard_map/ppermute | solution.py:324
  55.8 11.8 %collective-permute-start.8 = (bf16[8,128,128]{2,1,0:T(8,128)(2,1)S(1)}, bf16[8,128,128]{2,1,0:T(8,128)(2,1)}, u32[]{:S(2)}, u32[]{:S(2)}) collective-permute-start(bf16[8,128,128]{2,1,0:T(8,128)(2,1)S(1)} %collective-permute-done.5.refs_6_), channel_id=1, source_target_pairs={{0,7},{1,0},{2,1},{3,2},{4,3},{5,4},{6,5},{7,6},{8,15},{9,8},{10,9... | collective-permute-start | bytes 786440 | tf_op jit(solution)/shard_map/ppermute | solution.py:323
  60.4 11.8 %collective-permute-start.12 = (bf16[8,128,128]{2,1,0:T(8,128)(2,1)S(1)}, bf16[8,128,128]{2,1,0:T(8,128)(2,1)}, u32[]{:S(2)}, u32[]{:S(2)}) collective-permute-start(bf16[8,128,128]{2,1,0:T(8,128)(2,1)S(1)} %collective-permute-done.9.refs_11_), channel_id=1, source_target_pairs={{0,7},{1,0},{2,1},{3,2},{4,3},{5,4},{6,5},{7,6},{8,15},{9,8},{10,9... | collective-permute-start | bytes 786440 | tf_op jit(solution)/shard_map/ppermute | solution.py:325
  62.6 11.8 %collective-permute-start.3 = (bf16[8,128,128]{2,1,0:T(8,128)(2,1)S(1)}, bf16[8,128,128]{2,1,0:T(8,128)(2,1)}, u32[]{:S(2)}, u32[]{:S(2)}) collective-permute-start(bf16[8,128,128]{2,1,0:T(8,128)(2,1)S(1)} %collective-permute-done.2.refs_8_), channel_id=1, source_target_pairs={{0,1},{1,2},{2,3},{3,4},{4,5},{5,6},{6,7},{7,0},{8,9},{9,10},{10,1... | collective-permute-start | bytes 786440 | tf_op jit(solution)/shard_map/ppermute | solution.py:322
  65.7 11.9 %collective-permute-start.10 = (bf16[8,128,128]{2,1,0:T(8,128)(2,1)S(1)}, bf16[8,128,128]{2,1,0:T(8,128)(2,1)}, u32[]{:S(2)}, u32[]{:S(2)}) collective-permute-start(bf16[8,128,128]{2,1,0:T(8,128)(2,1)S(1)} %collective-permute-done.7.refs_9_), channel_id=1, source_target_pairs={{0,1},{1,2},{2,3},{3,4},{4,5},{5,6},{6,7},{7,0},{8,9},{9,10},{10,1... | collective-permute-start | bytes 786440 | tf_op jit(solution)/shard_map/ppermute | solution.py:324
  67.6 9.9 %collective-permute-start.11 = (bf16[8,128,128]{2,1,0:T(8,128)(2,1)}, bf16[8,128,128]{2,1,0:T(8,128)(2,1)}, u32[]{:S(2)}, u32[]{:S(2)}) collective-permute-start(bf16[8,128,128]{2,1,0:T(8,128)(2,1)} %collective-permute-done.8.refs_10_), channel_id=1, source_target_pairs={{0,7},{1,0},{2,1},{3,2},{4,3},{5,4},{6,5},{7,6},{8,15},{9,8},{10,9... | collective-permute-start | bytes 786440 | tf_op jit(solution)/shard_map/ppermute | solution.py:323
  72.2 10.5 %collective-permute-start.14 = (bf16[8,128,128]{2,1,0:T(8,128)(2,1)}, bf16[8,128,128]{2,1,0:T(8,128)(2,1)}, u32[]{:S(2)}, u32[]{:S(2)}) collective-permute-start(bf16[8,128,128]{2,1,0:T(8,128)(2,1)} %collective-permute-done.12.refs_15_), channel_id=1, source_target_pairs={{0,7},{1,0},{2,1},{3,2},{4,3},{5,4},{6,5},{7,6},{8,15},{9,8},{10,9... | collective-permute-start | bytes 786440 | tf_op jit(solution)/shard_map/ppermute | solution.py:329
  74.5 8.5 %collective-permute-start.13 = (bf16[8,128,128]{2,1,0:T(8,128)(2,1)}, bf16[8,128,128]{2,1,0:T(8,128)(2,1)S(1)}, u32[]{:S(2)}, u32[]{:S(2)}) collective-permute-start(bf16[8,128,128]{2,1,0:T(8,128)(2,1)} %collective-permute-done.3.refs_12_), channel_id=1, source_target_pairs={{0,1},{1,2},{2,3},{3,4},{4,5},{5,6},{6,7},{7,0},{8,9},{9,10},{10,1... | collective-permute-start | bytes 786440 | tf_op jit(solution)/shard_map/ppermute | solution.py:328
  89.3 12.8 %copy-start.5 = (bf16[1,1,1024,256]{3,2,1,0:T(8,128)(2,1)S(1)}, bf16[1,1,1024,256]{3,2,1,0:T(8,128)(2,1)}, u32[]{:S(2)}) copy-start(bf16[1,1,1024,256]{3,2,1,0:T(8,128)(2,1)} %param.9) | copy-start | bytes 1572868
  89.3 12.8 %copy-start.6 = (bf16[1,1,1024,256]{3,2,1,0:T(8,128)(2,1)S(1)}, bf16[1,1,1024,256]{3,2,1,0:T(8,128)(2,1)}, u32[]{:S(2)}) copy-start(bf16[1,1,1024,256]{3,2,1,0:T(8,128)(2,1)} %param.10) | copy-start | bytes 1572868
  89.3 40.6 %all-to-all-start.1 = ((bf16[32,136,128]{2,1,0:T(8,128)(2,1)}), bf16[32,136,128]{2,1,0:T(8,128)(2,1)S(1)}, u32[]{:S(2)}, u32[]{:S(2)}) async-start(bf16[32,136,128]{2,1,0:T(8,128)(2,1)} %cross_attention.1), calls=%async_computation.1 | async-start | bytes 2228224 | tf_op jit(solution)/shard_map/all_to_all | solution.py:369
  102.1 1.0 copy-start.7
